TPU v7x, 256 devices: a whole 4x4x8 slice. The times are simulated.
256 devices in a mesh: gz: 64 (over y, z, core), gy: 4 (over x).
Axes of the slice: x: 4, y: 4, z: 8, core: 2. Of those that a mesh axis runs over, the one named last changes fastest.
Arguments:
- state: bfloat16 [32, 256, 64, 256], P(None, 'gz', 'gy'), may hold values from -6 to 6
- residual: bfloat16 [4096, 4, 768], P('gz'), may hold values from -6 to 6
- projector: bfloat16 [4, 768, 512], replicated, may hold values from -0.21875 to 0.21875
- pair_counts: int32 [4, 64, 7], P('gy'), may hold values from 0 to 32, as said below
- pair_block: int32 [4, 64, 224], P('gy'), may hold values from 0 to 63
- pair_tile: int32 [4, 64, 224], P('gy'), may hold values from 0 to 7
- pair_view: int32 [4, 64, 224], P('gy'), may hold values from 0 to 3
- enc_weight: bfloat16 [2, 2, 2, 64, 33], replicated, may hold values from -0.375 to 0.375
- dec_weight: bfloat16 [4, 4, 4, 32, 64], replicated, may hold values from -0.25 to 0.25
Outputs:
- new_state: bfloat16 [32, 256, 64, 256], P(None, 'gz', 'gy')
Inputs may be any that keep to these rules, and one draw needn't show every extreme that they name: pair_counts[j, i, o] is 0 where slab i - 3 + o lies outside 0 .. 63, exactly 32 for o = 3, and 1 to 32 otherwise. The slots of pair_block, pair_tile and pair_view past the last group of a source slab are unused.
All inputs are finite; a program needn't handle non-finite values.
Results may differ from a plain program's by a relative error of at most 0.0054.
Values may be sent and summed in bfloat16 or wider, within the bound.
No kernel may reach another device: no remote copies, remote signals or barrier semaphores. Data moves between devices by JAX's collectives and lax.ppermute only.
A program may use at most 128 MiB of HBM per device.

v0:
```python
import jax
import jax.numpy as jnp
from jax import lax
from jax.sharding import PartitionSpec as P

TY = 2
CAP = 32
REACH = 3
SPAN = 7
NPD = 224


def shifted(block, axis, distance):
    devices = range(lax.axis_size(axis))
    route = [(i - distance, i) for i in devices if i - distance in devices]
    return lax.ppermute(block, axis, route)


def gelu_tanh(values):
    return jax.nn.gelu(values, approximate=True)


def transposed(coarse, weight):
    kernel = weight[::-1, ::-1, ::-1]
    result = lax.conv_general_dilated(
        coarse[None],
        kernel,
        (1, 1, 1),
        ((3, 3), (3, 3), (3, 3)),
        lhs_dilation=(2, 2, 2),
        dimension_numbers=("NCDHW", "DHWOI", "NCDHW"),
        preferred_element_type=jnp.float32,
    )
    return result[0]


def per_device(
    state,
    residual,
    projector,
    pair_counts,
    pair_block,
    pair_tile,
    pair_view,
    enc_weight,
    dec_weight,
):
    chans, zd, yd, xd = state.shape
    dcols = residual.shape[2]
    nviews = projector.shape[0]
    tile_cells = projector.shape[2]
    my_slab = lax.axis_index("gz")
    zc, yc, xc = (zd // 2, yd // 2, xd // 2)
    grid = state.reshape(chans, zc, 2, yc, 2, xc, 2)
    from_state = jnp.einsum(
        "czaybxe,abeoc->ozyx", grid, enc_weight[..., :chans], preferred_element_type=jnp.float32
    )
    counts = pair_counts[0]
    starts = jnp.cumsum(counts, axis=1) - counts
    slot = jnp.arange(CAP, dtype=jnp.int32)
    my_counts = lax.dynamic_index_in_dim(counts, my_slab, 0, keepdims=False)
    my_starts = lax.dynamic_index_in_dim(starts, my_slab, 0, keepdims=False)
    my_blocks = lax.dynamic_index_in_dim(pair_block[0], my_slab, 0, keepdims=False)
    position = jnp.clip(my_starts[:, None] + slot[None, :], 0, NPD - 1)
    sending = slot[None, :] < my_counts[:, None]
    block_ids = jnp.take(my_blocks, position.reshape(-1), axis=0)
    rays = jnp.take(residual, block_ids, axis=0).reshape(SPAN, CAP, zd, dcols)
    rays = jnp.where(sending[:, :, None, None], rays, jnp.zeros_like(rays))
    pieces = []
    for source_pos in range(SPAN):
        shift_by = REACH - source_pos
        if shift_by == 0:
            pieces.append(rays[REACH])
        else:
            pieces.append(shifted(rays[REACH + shift_by], "gz", shift_by))
    arrived = jnp.stack(pieces)
    edge = ((REACH, REACH), (0, 0))
    near_counts = lax.dynamic_slice_in_dim(jnp.pad(counts, edge), my_slab, SPAN, 0)
    near_starts = lax.dynamic_slice_in_dim(jnp.pad(starts, edge), my_slab, SPAN, 0)
    near_tiles = lax.dynamic_slice_in_dim(jnp.pad(pair_tile[0], edge), my_slab, SPAN, 0)
    near_views = lax.dynamic_slice_in_dim(jnp.pad(pair_view[0], edge), my_slab, SPAN, 0)
    order = jnp.arange(SPAN)
    recv_count = near_counts[order, SPAN - 1 - order]
    recv_start = near_starts[order, SPAN - 1 - order]
    recv_pos = jnp.clip(recv_start[:, None] + slot[None, :], 0, NPD - 1)
    receiving = (slot[None, :] < recv_count[:, None]).reshape(-1)
    tiles = jnp.take_along_axis(near_tiles, recv_pos, axis=1).reshape(-1)
    views = jnp.take_along_axis(near_views, recv_pos, axis=1).reshape(-1)
    pairs = SPAN * CAP
    onehot = (views[:, None] == jnp.arange(nviews)[None, :]).astype(jnp.bfloat16)
    spread = arrived.reshape(pairs, zd, 1, dcols) * onehot[:, None, :, None]
    contrib = jnp.dot(
        spread.reshape(pairs * zd, nviews * dcols),
        projector.reshape(nviews * dcols, tile_cells),
        preferred_element_type=jnp.float32,
    ).reshape(pairs, zd, tile_cells)
    ntile = yd // TY
    placing = ((tiles[:, None] == jnp.arange(ntile)[None, :]) & receiving[:, None]).astype(
        jnp.float32
    )
    tiled = jnp.einsum("sn,szt->nzt", placing, contrib, precision=lax.Precision.HIGHEST)
    bproj = (
        tiled.reshape(ntile, zd, TY, xd)
        .transpose(1, 0, 2, 3)
        .reshape(zd, yd, xd)
        .astype(jnp.bfloat16)
    )
    extra = bproj.reshape(zc, 2, yc, 2, xc, 2)
    from_bproj = jnp.einsum(
        "zaybxe,abeo->ozyx", extra, enc_weight[..., chans], preferred_element_type=jnp.float32
    )
    coarse = gelu_tanh(from_state + from_bproj).astype(jnp.bfloat16)
    fine = transposed(coarse, dec_weight)[:, :, :, 1 : xd + 1]
    lower_rim = shifted(fine[:, zd + 1].astype(jnp.bfloat16), "gz", 1).astype(jnp.float32)
    upper_rim = shifted(fine[:, 0].astype(jnp.bfloat16), "gz", -1).astype(jnp.float32)
    core = fine[:, 1 : zd + 1]
    core = core + jnp.pad(lower_rim[:, None], ((0, 0), (0, zd - 1), (0, 0), (0, 0)))
    core = core + jnp.pad(upper_rim[:, None], ((0, 0), (zd - 1, 0), (0, 0), (0, 0)))
    from_left = shifted(core[:, :, yd + 1].astype(jnp.bfloat16), "gy", 1).astype(jnp.float32)
    from_right = shifted(core[:, :, 0].astype(jnp.bfloat16), "gy", -1).astype(jnp.float32)
    core = core[:, :, 1 : yd + 1]
    core = core + jnp.pad(from_left[:, :, None], ((0, 0), (0, 0), (0, yd - 1), (0, 0)))
    decoded = core + jnp.pad(from_right[:, :, None], ((0, 0), (0, 0), (yd - 1, 0), (0, 0)))
    return (state.astype(jnp.float32) + decoded).astype(jnp.bfloat16)


def solution(mesh):
    in_specs = (
        P(None, "gz", "gy", None),
        P("gz", None, None),
        P(),
        P("gy", None, None),
        P("gy", None, None),
        P("gy", None, None),
        P("gy", None, None),
        P(),
        P(),
    )
    out_specs = P(None, "gz", "gy", None)
    return jax.shard_map(
        per_device, mesh=mesh, in_specs=in_specs, out_specs=out_specs, check_vma=False
    )
```

profile of v0, /device:TPU:31, one launch (start us, length us, event | category | flops | bytes accessed | tf_op | source)
XLA Modules:
  0.0 267.6 jit_solution(3910173407140207195)
XLA Ops:
  0.0 0.8 copy.61
  0.8 1.7 dynamic-slice_reduce_fusion.1
  2.5 0.7 constant_dynamic-slice_fusion
  3.3 0.7 fusion.39
  4.0 0.2 dynamic-slice_reduce_fusion
  4.1 0.5 copy-done.8
  4.7 0.6 min.19
  5.4 0.6 compare_select_fusion.4
  6.0 0.6 pad_clamp_fusion.1
  6.6 2.1 gather_fusion.2
  8.8 0.6 compare_select_fusion.3
  9.4 1.3 iota_compare_fusion.2
  10.7 2.9 %gather_fusion.3 = bf16[224,4,768]{2,1,0:T(4,128)(2,1)} fusion(bf16[64,4,768]{2,1,0:T(4,128)(2,1)S(1)} %copy-done.3, s32[1024]{0:T(1024)S(1)} %pad_clamp_fusion), kind=kCustom, calls=%fused_computation.5 | custom fusion | bytes 2753408 | tf_op jit(solution)/shard_map/jit(_take)/gather | solution.py:67
  13.7 2.4 select_select_fusion
  16.0 1.1 copy-done.1
  17.2 0.9 slice_bitcast_fusion.5
  18.1 4.1 %collective-permute-start.2 = (bf16[32,4,768]{2,1,0:T(4,128)(2,1)S(1)}, bf16[32,4,768]{2,1,0:T(4,128)(2,1)}, u32[]{:S(2)}, u32[]{:S(2)}) collective-permute-start(bf16[32,4,768]{2,1,0:T(4,128)(2,1)S(1)} %get-tuple-element.14), channel_id=1, source_target_pairs={{0,4},{4,8},{8,12},{12,16},{16,20},{20,24},{24,28},{28,32},{32,36}... | collective-permute-start | bytes 589832 | tf_op jit(solution)/shard_map/ppermute | solution.py:16
  22.2 3.5 %collective-permute-start.1 = (bf16[32,4,768]{2,1,0:T(4,128)(2,1)}, bf16[32,4,768]{2,1,0:T(4,128)(2,1)}, u32[]{:S(2)}, u32[]{:S(2)}) collective-permute-start(bf16[32,4,768]{2,1,0:T(4,128)(2,1)} %get-tuple-element.15), channel_id=1, source_target_pairs={{0,8},{4,12},{8,16},{12,20},{16,24},{20,28},{24,32},{28,36},{32,40... | collective-permute-start | bytes 589832 | tf_op jit(solution)/shard_map/ppermute | solution.py:16
  25.8 3.6 %collective-permute-start = (bf16[32,4,768]{2,1,0:T(4,128)(2,1)}, bf16[32,4,768]{2,1,0:T(4,128)(2,1)}, u32[]{:S(2)}, u32[]{:S(2)}) collective-permute-start(bf16[32,4,768]{2,1,0:T(4,128)(2,1)} %get-tuple-element.16), channel_id=1, source_target_pairs={{0,12},{4,16},{8,20},{12,24},{16,28},{20,32},{24,36},{28,40},{32,4... | collective-permute-start | bytes 589832 | tf_op jit(solution)/shard_map/ppermute | solution.py:16
  29.3 0.1 pad_dynamic-slice_fusion.2
  29.4 0.6 gather_fusion.1
  30.1 0.7 gather_fusion
  30.8 0.1 lt.111
  30.9 0.1 bitcast_or_fusion
  31.0 0.1 reshape.267
  31.1 1.9 gather_fusion.5
  33.0 1.9 gather_fusion.4
  35.1 0.1 eq.34
  35.2 0.1 eq.38
  35.3 4.7 %copy.20 = bf16[32,4,16,256]{0,3,2,1:T(8,128)(2,1)} copy(bf16[32,4,16,256]{3,2,1,0:T(8,128)(2,1)} %param.11) | data formatting | bytes 2097152 | tf_op args[0]
  40.0 4.5 %fusion.2 = f32[64,2,8,128,1,1,1]{3,0,6,5,1,2,4:T(8,128)} fusion(bf16[32,2,2,8,2,128,2]{0,6,5,4,3,2,1:T(2,128)(2,1)} %bitcast.115, bf16[2,2,2,64,32]{3,2,4,1,0:T(2,128)(2,1)S(1)} %slice-done), kind=kOutput, calls=%fused_computation.8 | convolution fusion | flops 67108864 | bytes 1605632 | tf_op jit(solution)/shard_map/czaybxe,abeoc->ozyx/dot_general | solution.py:55
  44.5 1.7 bitcast_dynamic-update-slice_fusion.5
  46.2 1.7 bitcast_dynamic-update-slice_fusion.4
  47.9 1.7 bitcast_dynamic-update-slice_fusion.3
  49.6 0.9 slice_bitcast_fusion.2
  50.5 2.3 collective-permute-start.3
  52.8 0.1 fusion.24
  52.9 4.1 %collective-permute-start.5 = (bf16[32,4,768]{2,1,0:T(4,128)(2,1)S(1)}, bf16[32,4,768]{2,1,0:T(4,128)(2,1)S(1)}, u32[]{:S(2)}, u32[]{:S(2)}) collective-permute-start(bf16[32,4,768]{2,1,0:T(4,128)(2,1)S(1)} %get-tuple-element.10), channel_id=1, source_target_pairs={{12,0},{16,4},{20,8},{24,12},{28,16},{32,20},{36,24},{40,28},{44,3... | collective-permute-start | bytes 589832 | tf_op jit(solution)/shard_map/ppermute | solution.py:16
  57.0 3.5 %collective-permute-start.4 = (bf16[32,4,768]{2,1,0:T(4,128)(2,1)S(1)}, bf16[32,4,768]{2,1,0:T(4,128)(2,1)S(1)}, u32[]{:S(2)}, u32[]{:S(2)}) collective-permute-start(bf16[32,4,768]{2,1,0:T(4,128)(2,1)S(1)} %get-tuple-element.11), channel_id=1, source_target_pairs={{8,0},{12,4},{16,8},{20,12},{24,16},{28,20},{32,24},{36,28},{40,32... | collective-permute-start | bytes 589832 | tf_op jit(solution)/shard_map/ppermute | solution.py:16
  60.6 0.8 bitcast_dynamic-update-slice_fusion.2
  61.4 8.2 %collective-permute-done.4 = bf16[32,4,768]{2,1,0:T(4,128)(2,1)S(1)} collective-permute-done((bf16[32,4,768]{2,1,0:T(4,128)(2,1)S(1)}, bf16[32,4,768]{2,1,0:T(4,128)(2,1)S(1)}, u32[]{:S(2)}, u32[]{:S(2)}) %collective-permute-start.4) | collective-permute-done | bytes 196640 | tf_op jit(solution)/shard_map/ppermute | solution.py:16
  69.6 0.7 bitcast_dynamic-update-slice_fusion.1
  70.3 0.8 bitcast_dynamic-update-slice_fusion
  71.1 6.7 %broadcast_multiply_fusion = bf16[224,4,4,768]{3,2,1,0:T(4,128)(2,1)} fusion(bf16[224,4]{1,0:T(8,128)(2,1)S(1)} %fusion.24, bf16[224,4,768]{2,1,0:T(4,128)(2,1)} %bitcast.25), kind=kLoop, calls=%fused_computation.11 | loop fusion | flops 2752512 | bytes 6883072 | tf_op jit(solution)/shard_map/mul | solution.py:91
  77.8 7.2 %fusion = f32[224,4,512,1]{2,0,3,1:T(8,128)S(1)} fusion(bf16[224,4,4,768]{3,2,1,0:T(4,128)(2,1)} %broadcast_multiply_fusion, bf16[4,768,512]{2,1,0:T(8,128)(2,1)S(1)} %copy-done), kind=kOutput, calls=%fused_computation.6 | convolution fusion | flops 2818572288 | bytes 10485760 | tf_op jit(solution)/shard_map/dot_general | solution.py:92
  85.0 0.7 fusion.12
  85.7 1.0 copy.22
  86.7 1.3 copy.24
  88.0 1.5 fusion.23
  89.5 2.0 copy.25
  91.4 116.5 %fusion.42 = f32[1,32,6,18,258]{1,0,4,3,2:T(1,128)} fusion(bf16[1,64,2,8,128]{1,0,4,3,2:T(2,128)(2,1)} %copy.25, bf16[4,4,4,32,64]{4,3,2,1,0:T(8,128)(2,1)} %param.19), kind=kOutput, calls=%fused_computation.97 | convolution fusion | flops 536870912 | bytes 4090880 | tf_op jit(solution)/shard_map/conv_general_dilated | solution.py:25
  208.0 32.7 %copy.26 = f32[1,32,6,18,258]{4,1,3,2,0:T(8,128)} copy(f32[1,32,6,18,258]{1,0,4,3,2:T(1,128)} %fusion.42) | data formatting | bytes 7133184 | tf_op jit(solution)/shard_map/conv_general_dilated | solution.py:25
  240.6 2.9 %bitcast_convert_fusion = bf16[32,6,18,258]{3,0,2,1:T(8,128)(2,1)S(1)} fusion(f32[1,32,6,18,258]{4,1,3,2,0:T(8,128)} %copy.26), kind=kLoop, calls=%fused_computation.95 | loop fusion | flops 891648 | bytes 5349888 | tf_op jit(solution)/shard_map/convert.15
  243.6 0.3 slice_bitcast_fusion.1
  243.9 3.8 %collective-permute-start.6 = (bf16[32,18,256]{2,0,1:T(8,128)(2,1)S(1)}, bf16[32,18,256]{2,0,1:T(8,128)(2,1)S(1)}, u32[]{:S(2)}, u32[]{:S(2)}) collective-permute-start(bf16[32,18,256]{2,0,1:T(8,128)(2,1)S(1)} %get-tuple-element.8), channel_id=1, source_target_pairs={{0,4},{4,8},{8,12},{12,16},{16,20},{20,24},{24,28},{28,32},{32,36}... | collective-permute-start | bytes 884744 | tf_op jit(solution)/shard_map/ppermute | solution.py:16
  247.7 1.9 collective-permute-start.7
  249.6 1.7 collective-permute-done.6
  251.3 4.4 %collective-permute-done.7 = bf16[32,18,256]{2,0,1:T(8,128)(2,1)S(1)} collective-permute-done((bf16[32,18,256]{2,0,1:T(8,128)(2,1)S(1)}, bf16[32,18,256]{2,0,1:T(8,128)(2,1)S(1)}, u32[]{:S(2)}, u32[]{:S(2)}) %collective-permute-start.7) | collective-permute-done | bytes 294944 | tf_op jit(solution)/shard_map/ppermute | solution.py:16
  255.7 2.8 %fusion.40 = (bf16[32,4,18,256]{3,0,2,1:T(8,128)(2,1)S(1)}, f32[32,4,18,256]{3,0,2,1:T(8,128)S(1)}) fusion(bf16[32,1,18,256]{3,0,2,1:T(8,128)(2,1)S(1)} %bitcast.118, bf16[32,1,18,256]{3,0,2,1:T(8,128)(2,1)S(1)} %bitcast.117, f32[32,6,18,258]{3,0,2,1:T(8,128)} %bitcast.113), kind=kLoop, calls=%fused_computation.96 | loop fusion | flops 2949120 | bytes 6488064 | tf_op jit(solution)/shard_map/convert.13
  258.6 1.3 collective-permute-start.8
  259.9 4.0 %collective-permute-start.9 = (bf16[32,4,256]{2,0,1:T(8,128)(2,1)S(1)}, bf16[32,4,256]{2,0,1:T(8,128)(2,1)S(1)}, u32[]{:S(2)}, u32[]{:S(2)}) collective-permute-start(bf16[32,4,256]{2,0,1:T(8,128)(2,1)S(1)} %get-tuple-element.18), channel_id=1, source_target_pairs={{1,0},{2,1},{3,2},{5,4},{6,5},{7,6},{9,8},{10,9},{11,10},{13,12},{... | collective-permute-start | bytes 196616 | tf_op jit(solution)/shard_map/ppermute | solution.py:16
  263.9 1.3 collective-permute-done.9
  265.2 0.8 fusion.8
  266.0 1.6 copy.29
  (37 shorter events, 0.6 us)
Async XLA Ops:
  0.0 77.8 %copy-start = (bf16[4,768,512]{2,1,0:T(8,128)(2,1)S(1)}, bf16[4,768,512]{2,1,0:T(8,128)(2,1)}, u32[]{:S(2)}) copy-start(bf16[4,768,512]{2,1,0:T(8,128)(2,1)} %param.13) | copy-start | bytes 9437188
  0.0 10.7 %copy-start.3 = (bf16[64,4,768]{2,1,0:T(4,128)(2,1)S(1)}, bf16[64,4,768]{2,1,0:T(4,128)(2,1)}, u32[]{:S(2)}) copy-start(bf16[64,4,768]{2,1,0:T(4,128)(2,1)} %param.12) | copy-start | bytes 1179652
  4.1 0.5 copy-start.8
  10.7 2.9 %copy-start.9 = (pred[7,32]{1,0:T(8,128)(4,1)S(1)}, pred[7,32]{1,0:T(8,128)(4,1)}, u32[]{:S(2)}) copy-start(pred[7,32]{1,0:T(8,128)(4,1)} %get-tuple-element.25) | copy-start | bytes 676
  13.7 17.4 %copy-start.5 = (s32[1,64,224]{2,1,0:T(8,128)S(1)}, s32[1,64,224]{2,1,0:T(8,128)}, u32[]{:S(2)}) copy-start(s32[1,64,224]{2,1,0:T(8,128)} %param.17) | copy-start | bytes 172036
  13.7 17.4 %copy-start.6 = (s32[1,64,224]{2,1,0:T(8,128)S(1)}, s32[1,64,224]{2,1,0:T(8,128)}, u32[]{:S(2)}) copy-start(s32[1,64,224]{2,1,0:T(8,128)} %param.16) | copy-start | bytes 172036
  16.0 1.1 copy-start.1
  18.1 29.8 %collective-permute-start.2 = (bf16[32,4,768]{2,1,0:T(4,128)(2,1)S(1)}, bf16[32,4,768]{2,1,0:T(4,128)(2,1)}, u32[]{:S(2)}, u32[]{:S(2)}) collective-permute-start(bf16[32,4,768]{2,1,0:T(4,128)(2,1)S(1)} %get-tuple-element.14), channel_id=1, source_target_pairs={{0,4},{4,8},{8,12},{12,16},{16,20},{20,24},{24,28},{28,32},{32,36}... | collective-permute-start | bytes 589832 | tf_op jit(solution)/shard_map/ppermute | solution.py:16
  22.2 24.0 %collective-permute-start.1 = (bf16[32,4,768]{2,1,0:T(4,128)(2,1)}, bf16[32,4,768]{2,1,0:T(4,128)(2,1)}, u32[]{:S(2)}, u32[]{:S(2)}) collective-permute-start(bf16[32,4,768]{2,1,0:T(4,128)(2,1)} %get-tuple-element.15), channel_id=1, source_target_pairs={{0,8},{4,12},{8,16},{12,20},{16,24},{20,28},{24,32},{28,36},{32,40... | collective-permute-start | bytes 589832 | tf_op jit(solution)/shard_map/ppermute | solution.py:16
  25.8 18.8 %collective-permute-start = (bf16[32,4,768]{2,1,0:T(4,128)(2,1)}, bf16[32,4,768]{2,1,0:T(4,128)(2,1)}, u32[]{:S(2)}, u32[]{:S(2)}) collective-permute-start(bf16[32,4,768]{2,1,0:T(4,128)(2,1)} %get-tuple-element.16), channel_id=1, source_target_pairs={{0,12},{4,16},{8,20},{12,24},{16,28},{20,32},{24,36},{28,40},{32,4... | collective-permute-start | bytes 589832 | tf_op jit(solution)/shard_map/ppermute | solution.py:16
  35.3 4.7 %slice-start = ((bf16[2,2,2,64,33]{3,2,4,1,0:T(2,128)(2,1)}), bf16[2,2,2,64,32]{3,2,4,1,0:T(2,128)(2,1)S(1)}, s32[]{:S(2)}) async-start(bf16[2,2,2,64,33]{3,2,4,1,0:T(2,128)(2,1)} %param.18), calls=%async_computation | async-start | bytes 131072 | tf_op jit(solution)/shard_map/slice | solution.py:56
  40.0 9.6 %copy-start.2 = (bf16[7,32,4,768]{3,2,1,0:T(4,128)(2,1)S(1)}, bf16[7,32,4,768]{3,2,1,0:T(4,128)(2,1)}, u32[]{:S(2)}) copy-start(bf16[7,32,4,768]{3,2,1,0:T(4,128)(2,1)} %copy-done.1) | copy-start | bytes 4128772
  50.5 10.1 %collective-permute-start.3 = (bf16[32,4,768]{2,1,0:T(4,128)(2,1)S(1)}, bf16[32,4,768]{2,1,0:T(4,128)(2,1)S(1)}, u32[]{:S(2)}, u32[]{:S(2)}) collective-permute-start(bf16[32,4,768]{2,1,0:T(4,128)(2,1)S(1)} %get-tuple-element.12), channel_id=1, source_target_pairs={{4,0},{8,4},{12,8},{16,12},{20,16},{24,20},{28,24},{32,28},{36,32}... | collective-permute-start | bytes 589832 | tf_op jit(solution)/shard_map/ppermute | solution.py:16
  52.9 17.4 %collective-permute-start.5 = (bf16[32,4,768]{2,1,0:T(4,128)(2,1)S(1)}, bf16[32,4,768]{2,1,0:T(4,128)(2,1)S(1)}, u32[]{:S(2)}, u32[]{:S(2)}) collective-permute-start(bf16[32,4,768]{2,1,0:T(4,128)(2,1)S(1)} %get-tuple-element.10), channel_id=1, source_target_pairs={{12,0},{16,4},{20,8},{24,12},{28,16},{32,20},{36,24},{40,28},{44,3... | collective-permute-start | bytes 589832 | tf_op jit(solution)/shard_map/ppermute | solution.py:16
  57.0 12.5 %collective-permute-start.4 = (bf16[32,4,768]{2,1,0:T(4,128)(2,1)S(1)}, bf16[32,4,768]{2,1,0:T(4,128)(2,1)S(1)}, u32[]{:S(2)}, u32[]{:S(2)}) collective-permute-start(bf16[32,4,768]{2,1,0:T(4,128)(2,1)S(1)} %get-tuple-element.11), channel_id=1, source_target_pairs={{8,0},{12,4},{16,8},{20,12},{24,16},{28,20},{32,24},{36,28},{40,32... | collective-permute-start | bytes 589832 | tf_op jit(solution)/shard_map/ppermute | solution.py:16
  85.0 3.0 %copy-start.7 = (bf16[2,2,2,64,33]{3,2,4,1,0:T(2,128)(2,1)S(1)}, bf16[2,2,2,64,33]{3,2,4,1,0:T(2,128)(2,1)}, u32[]{:S(2)}) copy-start(bf16[2,2,2,64,33]{3,2,4,1,0:T(2,128)(2,1)} %param.18) | copy-start | bytes 101380
  243.9 7.4 %collective-permute-start.6 = (bf16[32,18,256]{2,0,1:T(8,128)(2,1)S(1)}, bf16[32,18,256]{2,0,1:T(8,128)(2,1)S(1)}, u32[]{:S(2)}, u32[]{:S(2)}) collective-permute-start(bf16[32,18,256]{2,0,1:T(8,128)(2,1)S(1)} %get-tuple-element.8), channel_id=1, source_target_pairs={{0,4},{4,8},{8,12},{12,16},{16,20},{20,24},{24,28},{28,32},{32,36}... | collective-permute-start | bytes 884744 | tf_op jit(solution)/shard_map/ppermute | solution.py:16
  247.7 8.0 %collective-permute-start.7 = (bf16[32,18,256]{2,0,1:T(8,128)(2,1)S(1)}, bf16[32,18,256]{2,0,1:T(8,128)(2,1)S(1)}, u32[]{:S(2)}, u32[]{:S(2)}) collective-permute-start(bf16[32,18,256]{2,0,1:T(8,128)(2,1)S(1)} %get-tuple-element.9), channel_id=1, source_target_pairs={{4,0},{8,4},{12,8},{16,12},{20,16},{24,20},{28,24},{32,28},{36,32}... | collective-permute-start | bytes 884744 | tf_op jit(solution)/shard_map/ppermute | solution.py:16
  255.7 9.5 %copy-start.4 = (bf16[32,4,16,256]{3,2,1,0:T(8,128)(2,1)S(1)}, bf16[32,4,16,256]{3,2,1,0:T(8,128)(2,1)}, u32[]{:S(2)}) copy-start(bf16[32,4,16,256]{3,2,1,0:T(8,128)(2,1)} %param.11) | copy-start | bytes 3145732
  258.6 5.3 %collective-permute-start.8 = (bf16[32,4,256]{2,0,1:T(8,128)(2,1)S(1)}, bf16[32,4,256]{2,0,1:T(8,128)(2,1)S(1)}, u32[]{:S(2)}, u32[]{:S(2)}) collective-permute-start(bf16[32,4,256]{2,0,1:T(8,128)(2,1)S(1)} %get-tuple-element.17), channel_id=1, source_target_pairs={{0,1},{1,2},{2,3},{4,5},{5,6},{6,7},{8,9},{9,10},{10,11},{12,13},{... | collective-permute-start | bytes 196616 | tf_op jit(solution)/shard_map/ppermute | solution.py:16
  259.9 5.3 %collective-permute-start.9 = (bf16[32,4,256]{2,0,1:T(8,128)(2,1)S(1)}, bf16[32,4,256]{2,0,1:T(8,128)(2,1)S(1)}, u32[]{:S(2)}, u32[]{:S(2)}) collective-permute-start(bf16[32,4,256]{2,0,1:T(8,128)(2,1)S(1)} %get-tuple-element.18), channel_id=1, source_target_pairs={{1,0},{2,1},{3,2},{5,4},{6,5},{7,6},{9,8},{10,9},{11,10},{13,12},{... | collective-permute-start | bytes 196616 | tf_op jit(solution)/shard_map/ppermute | solution.py:16
where the time goes:
time: 272 us; the launch traced here: 268 us
  matrix products  130 us (48%)
  local copies, waits for them, and re-layouts  69.2 us (25%)
  starting transfers between devices  32.1 us (12%)
  other arithmetic  20 us (7%)
  waiting for transfers between devices  15.6 us (6%)
    conv_general_dilated x1, matrix products, transposed(): lax.conv_general_dilated(coarse[None], kernel, (1, 1, 1), ((3, 3), (3, 3)...  117 us
    conv_general_dilated x1, local copies, waits for them, and re-layouts, transposed(): lax.conv_general_dilated(coarse[None], kernel, (1, 1, 1), ((3, 3), (3, 3)...  32.7 us
    ppermute x10, starting transfers between devices, shifted(): return lax.ppermute(block, axis, route)  32.1 us
    ppermute x10, waiting for transfers between devices, shifted(): return lax.ppermute(block, axis, route)  15.6 us
    unnamed x27, local copies, waits for them, and re-layouts  13.8 us
    dot_general x1, matrix products, per_device(): jnp.dot(spread.reshape(pairs * zd, nviews * dcols), projector.reshape(nvi...  7.19 us
    mul x1, other arithmetic, per_device(): spread = arrived.reshape(pairs, zd, 1, dcols) * onehot[:, None, :, None]  6.68 us
    another operation x2, other arithmetic  5.77 us
  transfers between devices with their start and end apart: 10, of which 4 were waited for; matrix products, arithmetic and copies ran while one was open for 8% of the time, Pallas kernels for 0%

commit v1 on v0

v1 whole, which is shorter than its diff:
```python
import jax
import jax.numpy as jnp
from jax import lax
from jax.experimental import pallas as pl
from jax.experimental.pallas import tpu as pltpu
from jax.sharding import PartitionSpec as P

C1, C2 = 32, 64
ZD, YD, XD = 4, 16, 256
XC = XD // 2
SPAN = 7
NPD = 224
VIEWS = 4
NB = 64
DC = 768
TILE = 512
KL = 256
ROWS = 10
NL = ROWS * XC
WIN = 8 * ROWS
MSG = 112
LIST = 256
PAYR = 2 * WIN + 5 * C2
BF, F32, I32 = jnp.bfloat16, jnp.float32, jnp.int32
VLIM = 40 * 1024 * 1024


def dot(a, b):
    return jnp.dot(a, b, preferred_element_type=F32)


def iota(shape, dim):
    return lax.broadcasted_iota(I32, shape, dim)


def split_columns():
    row, col = iota((XD, XD), 0), iota((XD, XD), 1)
    return (row == 2 * (col % XC) + col // XC).astype(BF)


def merge_columns():
    row, col = iota((XD, XD), 0), iota((XD, XD), 1)
    return (col == 2 * (row % XC) + row // XC).astype(BF)


def edge_kernel(counts, block, tile, view, state, idx, up, down, own, lists):
    slab = idx[0]
    split = split_columns()
    row, col = iota((4 * C1, C1 * YD), 0), iota((4 * C1, C1 * YD), 1)
    y = row // C1
    y = jnp.where(y < 2, y, y + YD - 4)
    pick = (col == (row % C1) * YD + y).astype(BF)
    for z in range(ZD):
        plane = state[:, z].reshape(C1 * YD, XD)
        rows = dot(dot(pick, plane).astype(BF), split).astype(BF)
        down[z * 64 : z * 64 + 64, :] = rows[:64]
        up[z * 64 : z * 64 + 64, :] = rows[64:]
    slot = iota((1, NPD), 1)
    group = jnp.zeros((1, NPD), I32)
    end = 0
    for o in range(SPAN):
        end = end + counts[0, slab, o]
        group = group + (slot >= end).astype(I32)
    valid = group < SPAN
    b = block[0, pl.ds(slab, 1), :]
    t = tile[0, pl.ds(slab, 1), :]
    v = view[0, pl.ds(slab, 1), :]
    key = v * NB + b
    own[...] = jnp.full((8, KL), -1, I32)
    own[0:1, :NPD] = key
    own[1:2, :NPD] = jnp.where(valid, group * 16 + t + 1, -1)
    lists[...] = jnp.full((16, KL), -1.0, F32)
    lists[0:1, :NPD] = key.astype(F32)
    lists[1:2, :NPD] = jnp.where(valid & (t == 7), group, -1).astype(F32)
    up[LIST:, :] = lists[...].astype(BF)
    lists[1:2, :NPD] = jnp.where(valid & (t == 0), group, -1).astype(F32)
    down[LIST:, :] = lists[...].astype(BF)


def project_kernel(res, proj, high, low):
    rays = res[...].reshape(4 * NB, DC)
    y = dot(rays, proj[0])
    hi = y.astype(BF)
    lo = (y - hi.astype(F32)).astype(BF)
    for r in range(4):
        high[r] = hi[r * NB : (r + 1) * NB]
        low[r] = lo[r * NB : (r + 1) * NB]


def place_kernel(own, left, right, high, low, idx, mine, up, down, keys):
    part = idx[1]
    keys[0:1, 0:KL] = own[0:1, :].astype(F32)
    keys[1:2, 0:KL] = own[1:2, :].astype(F32)
    lk = left[LIST:, :].astype(F32)
    rk = right[LIST:, :].astype(F32)
    keys[0:1, KL : 2 * KL] = lk[0:1]
    keys[0:1, 2 * KL :] = rk[0:1]
    lg, rg = lk[1:2], rk[1:2]
    keys[1:2, KL : 2 * KL] = jnp.where((lg >= 0) & (part > 0), lg * 16, -1.0)
    keys[1:2, 2 * KL :] = jnp.where((rg >= 0) & (part < 3), rg * 16 + 9, -1.0)
    key = keys[0:1, :].astype(I32)
    skey = keys[1:2, :].astype(I32)
    total = 3 * WIN + 2 * MSG
    row = iota((total, 1), 0)
    inwin = row < 3 * WIN
    w = row // WIN
    k = row % WIN
    n = k // 8
    s = w * 4 - 6 + k % 8
    m = row - 3 * WIN
    isdown = m >= MSG
    mm = jnp.where(isdown, m - MSG, m)
    first = mm < WIN
    mn = jnp.where(first, mm // 8, (mm - WIN) // 2)
    ms_up = jnp.where(first, 6 + mm % 8, 14 + mm % 2)
    ms_dn = jnp.where(first, -10 + mm % 8, -12 + mm % 2)
    n = jnp.where(inwin, n, mn)
    s = jnp.where(inwin, s, jnp.where(isdown, ms_dn, ms_up))
    s = s + 12
    rkey = jnp.where(n < ROWS, (s // 4) * 16 + n, -2)
    r = s % 4
    a = (rkey == skey).astype(BF)
    bk = (iota((VIEWS * NB, 1), 0) == key).astype(BF)
    count = lax.dot_general(a, bk, (((1,), (1,)), ((), ())), preferred_element_type=F32)
    acc = jnp.zeros((total, TILE), F32)
    for q in range(4):
        c = jnp.where(r == q, count, 0.0).astype(BF)
        acc = acc + dot(c, high[q]) + dot(c, low[q])
    mine[...] = acc[: 3 * WIN]
    up[...] = acc[3 * WIN : 3 * WIN + MSG].astype(BF)
    down[...] = acc[3 * WIN + MSG :].astype(BF)


def window_matrix(w, down):
    row, col = iota((WIN, MSG), 0), iota((WIN, MSG), 1)
    n, s = row // 8, 4 * w - 6 + row % 8
    first = col < WIN
    mn = jnp.where(first, col // 8, (col - WIN) // 2)
    if down:
        ms = jnp.where(first, 2 + col % 8, col % 2)
    else:
        ms = jnp.where(first, col % 8 - 6, 2 + col % 2)
    return ((mn == n) & (ms == s)).astype(BF)


def encode_kernel(state, left, right, enc, dec, fs, pre, planes, wdec, x, we):
    split = split_columns()
    row, col = iota((C1 * YD, C1 * YD), 0), iota((C1 * YD, C1 * YD), 1)
    perm = (col == (row % C1) * YD + row // C1).astype(BF)
    for p in range(2):
        for q in range(2):
            for s in range(2):
                k = p * 4 + q * 2 + s
                we[:, k * C1 : (k + 1) * C1] = enc[p, q, s][:, :C1]
    for a in range(2):
        for p in range(2):
            z = 2 * a + p
            plane = state[:, z].reshape(C1 * YD, XD)
            d = dot(dot(perm, plane).astype(BF), split).astype(BF)
            planes[z] = d
            for q in range(2):
                for s in range(2):
                    k = (p * 4 + q * 2 + s) * C1
                    lanes = slice(s * XC, (s + 1) * XC)
                    h = z * 64 + q * C1
                    x[k : k + C1, 0:XC] = left[h : h + C1, lanes]
                    x[k : k + C1, 9 * XC : 10 * XC] = right[h : h + C1, lanes]
                    for b in range(8):
                        y = (2 * b + q) * C1
                        x[k : k + C1, (b + 1) * XC : (b + 2) * XC] = d[y : y + C1, lanes]
        f = dot(we[...], x[...])
        fs[a] = f
        for t in range(5):
            pre[a, t * C2 : (t + 1) * C2, :] = f[:, t * XD : (t + 1) * XD].astype(BF)
    wdec[...] = jnp.zeros_like(wdec)
    taps = (((0, 3), (1, 1)), ((1, 2), (2, 0)))
    for pz in range(2):
        for sel in range(2):
            kz = taps[pz][sel][1]
            for py in range(2):
                for dy, ky in taps[py]:
                    for px in range(2):
                        for dx, kx in taps[px]:
                            r0 = (py * 2 + px) * C1
                            c0 = (sel * 9 + dy * 3 + dx) * C2
                            wdec[pz, r0 : r0 + C1, c0 : c0 + C2] = dec[kz, ky, kx]


def relay_kernel(mine, up, down, pre, pay_up, pay_down):
    for w, pay, plane in ((2, pay_up, 1), (0, pay_down, 0)):
        total = mine[w * WIN : (w + 1) * WIN] + dot(window_matrix(w, False), up[...])
        total = (total + dot(window_matrix(w, True), down[...])).astype(BF)
        pay[0:WIN, :] = total[:, :XD]
        pay[WIN : 2 * WIN, :] = total[:, XD:]
        pay[2 * WIN :, :] = pre[plane]


def decode_kernel(mine, up, down, below, above, fs, planes, wdec, enc, idx, out, bp, x, ns):
    slab, part = idx[0], idx[1]
    split = split_columns()
    merge = merge_columns()
    row, col = iota((C1 * YD, C1 * YD), 0), iota((C1 * YD, C1 * YD), 1)
    perm = (col == (row % YD) * C1 + row // YD).astype(BF)
    centre = mine[WIN : 2 * WIN] + dot(window_matrix(1, False), up[...])
    centre = centre + dot(window_matrix(1, True), down[...])
    for q in range(2):
        rows = slice(q * WIN, (q + 1) * WIN)
        t = centre[:, q * XD : (q + 1) * XD] + below[rows, :].astype(F32) + above[rows, :].astype(F32)
        t = dot(t.astype(BF), split)
        for s in range(2):
            for n in range(ROWS):
                bp[(q * 2 + s) * 8 : (q * 2 + s + 1) * 8, n * XC : (n + 1) * XC] = t[
                    n * 8 : (n + 1) * 8, s * XC : (s + 1) * XC
                ]
    bpb = bp[...].astype(BF)
    lane = iota((C2, XC), 1)
    wlane = iota((C2, 32), 1)
    for a in range(4):
        wb = jnp.zeros((C2, 32), F32)
        for p in range(2):
            for q in range(2):
                for s in range(2):
                    w = enc[p, q, s].astype(F32)[:, C1 : C1 + 1]
                    wb = wb + jnp.where(wlane == (q * 2 + s) * 8 + 2 * a + p, w, 0.0)
        pb = dot(wb.astype(BF), bpb)
        inside = True
        if a == 0:
            inside = slab > 0
        if a == 3:
            inside = slab < 63
        for n in range(ROWS):
            lanes = slice(n * XC, (n + 1) * XC)
            if a in (1, 2):
                v = fs[a - 1, :, lanes]
            else:
                src = below if a == 0 else above
                r0 = 2 * WIN + (n // 2) * C2
                v = src[r0 : r0 + C2, (n % 2) * XC : (n % 2 + 1) * XC].astype(F32)
            v = v + pb[:, lanes]
            v = 0.5 * v * (1.0 + jnp.tanh(0.79788456 * (v + 0.044715 * (v * v * v))))
            ok = inside
            if n == 0:
                ok = (part > 0) & ok
            if n == 9:
                ok = (part < 3) & ok
            if ok is not True:
                v = jnp.where(ok, v, 0.0)
            shifts = (
                jnp.where(lane == 0, 0.0, pltpu.roll(v, 1, 1)).astype(BF),
                v.astype(BF),
                jnp.where(lane == XC - 1, 0.0, pltpu.roll(v, XC - 1, 1)).astype(BF),
            )
            for dy in range(3):
                m = n - dy
                if 0 <= m < 8:
                    for dx in range(3):
                        r0 = a * 576 + dy * 192 + dx * C2
                        x[r0 : r0 + C2, m * XC : (m + 1) * XC] = shifts[dx]
    for f in range(ZD):
        start = (f + 1) // 2 * 576
        d = dot(wdec[f % 2], x[start : start + 1152, :])
        for py in range(2):
            for px in range(2):
                r0 = (py * 2 + px) * C1
                lanes = slice(px * XC, (px + 1) * XC)
                for m in range(8):
                    y = (2 * m + py) * C1
                    old = planes[f, y : y + C1, lanes].astype(F32)
                    ns[y : y + C1, lanes] = (old + d[r0 : r0 + C1, m * XC : (m + 1) * XC]).astype(BF)
        new = dot(dot(perm, ns[...]).astype(BF), merge).astype(BF)
        out[:, f] = new.reshape(C1, YD, XD)


V = pltpu.VMEM
SM = pl.BlockSpec(memory_space=pltpu.SMEM)
VM = pl.BlockSpec(memory_space=pltpu.VMEM)


def shape(dims, dtype=BF):
    return jax.ShapeDtypeStruct(dims, dtype)


def call(kernel, ins, outs, scratch=(), cost=None, vlim=VLIM, **more):
    return pl.pallas_call(
        kernel,
        in_specs=ins,
        out_specs=[VM] * len(outs) if "grid" not in more else more.pop("specs"),
        out_shape=outs,
        scratch_shapes=scratch,
        compiler_params=pltpu.CompilerParams(vmem_limit_bytes=vlim),
        cost_estimate=cost,
        **more,
    )


def cost(us):
    return pl.CostEstimate(flops=int(us * 1e9), bytes_accessed=int(us * 3e6), transcendentals=0)


def shifted(block, axis, distance):
    n = lax.axis_size(axis)
    return lax.ppermute(block, axis, [(i, (i + distance) % n) for i in range(n)])


def per_device(
    state, residual, projector, pair_counts, pair_block, pair_tile, pair_view, enc_weight, dec_weight
):
    idx = jnp.stack([lax.axis_index("gz"), lax.axis_index("gy")]).astype(I32)
    up, down, own = call(
        edge_kernel,
        [SM, VM, VM, VM, VM, SM],
        [shape((272, XD)), shape((272, XD)), shape((8, KL), I32)],
        [V((16, KL), F32)],
        cost=cost(1.0),
        name="edge",
    )(pair_counts, pair_block, pair_tile, pair_view, state, idx)
    left = shifted(up, "gy", 1)
    right = shifted(down, "gy", -1)
    rays = jnp.transpose(residual, (1, 0, 2))
    high, low = call(
        project_kernel,
        [
            pl.BlockSpec((4, NB, DC), lambda v: (0, 0, 0)),
            pl.BlockSpec((1, DC, TILE), lambda v: (v, 0, 0)),
        ],
        [shape((4, VIEWS * NB, TILE)), shape((4, VIEWS * NB, TILE))],
        cost=cost(3.0),
        grid=(VIEWS,),
        specs=[pl.BlockSpec((4, NB, TILE), lambda v: (0, v, 0))] * 2,
        name="project",
    )(rays, projector)
    mine, msg_up, msg_down = call(
        place_kernel,
        [VM, VM, VM, VM, VM, SM],
        [shape((3 * WIN, TILE), F32), shape((MSG, TILE)), shape((MSG, TILE))],
        [V((8, 3 * KL), F32)],
        cost=cost(2.0),
        name="place",
    )(own, left, right, high, low, idx)
    got_up = shifted(msg_up, "gz", 3)
    got_down = shifted(msg_down, "gz", -3)
    fs, pre, planes, wdec = call(
        encode_kernel,
        [VM] * 5,
        [
            shape((2, C2, NL), F32),
            shape((2, 5 * C2, XD)),
            shape((ZD, C1 * YD, XD)),
            shape((2, 128, 1152)),
        ],
        [V((8 * C1, NL), BF), V((C2, 8 * C1), BF)],
        cost=cost(4.0),
        name="encode",
    )(state, left, right, enc_weight, dec_weight)
    pay_up, pay_down = call(
        relay_kernel,
        [VM] * 4,
        [shape((PAYR, XD)), shape((PAYR, XD))],
        cost=cost(1.0),
        name="relay",
    )(mine, got_up, got_down, pre)
    below = shifted(pay_up, "gz", 1)
    above = shifted(pay_down, "gz", -1)
    return call(
        decode_kernel,
        [VM] * 9 + [SM],
        [shape((C1, ZD, YD, XD))],
        [V((32, NL), F32), V((2304, 8 * XC), BF), V((C1 * YD, XD), BF)],
        cost=cost(6.0),
        name="decode",
    )(mine, got_up, got_down, below, above, fs, planes, wdec, enc_weight, idx)[0]


def solution(mesh):
    in_specs = (
        P(None, "gz", "gy", None),
        P("gz", None, None),
        P(),
        P("gy", None, None),
        P("gy", None, None),
        P("gy", None, None),
        P("gy", None, None),
        P(),
        P(),
    )
    out_specs = P(None, "gz", "gy", None)
    return jax.shard_map(
        per_device, mesh=mesh, in_specs=in_specs, out_specs=out_specs, check_vma=False
    )
```

time: 272 us -> 47.3 us (0.17)
  the two profiles are of different devices: /device:TPU:31 before, /device:TPU:6 now
where the time goes in v1:
time: 47.3 us; the launch traced here: 47 us
  Pallas kernels  15.1 us (32%)
  starting transfers between devices  13.4 us (28%)
  local copies, waits for them, and re-layouts  9.28 us (20%)
  waiting for transfers between devices  9.02 us (19%)
    ppermute x6, starting transfers between devices, shifted(): lax.ppermute(block, axis, [(i, (i + distance) % n) for i in range(n)])  13.4 us
    unnamed x29, local copies, waits for them, and re-layouts  9.28 us
    ppermute x6, waiting for transfers between devices, shifted(): lax.ppermute(block, axis, [(i, (i + distance) % n) for i in range(n)])  9.02 us
    pallas_call x1, Pallas kernels, per_device(): call(decode_kernel, [VM] * 9 + [SM], [shape((C1, ZD, YD, XD))], [V((32, N...  5.85 us
    pallas_call x1, Pallas kernels, per_device(): call(edge_kernel, [SM, VM, VM, VM, VM, SM], [shape((272, XD)), shape((272...  2.67 us
    pallas_call x1, Pallas kernels, per_device(): call(place_kernel, [VM, VM, VM, VM, VM, SM], [shape((3 * WIN, TILE), F32)...  2.56 us
    pallas_call x1, Pallas kernels, per_device(): call(encode_kernel, [VM] * 5, [shape((2, C2, NL), F32), shape((2, 5 * C2,...  2.11 us
    pallas_call x1, Pallas kernels, per_device(): call(project_kernel, [pl.BlockSpec((4, NB, DC), lambda v: (0, 0, 0)), pl....  1.69 us
  transfers between devices with their start and end apart: 6, of which 4 were waited for; matrix products, arithmetic and copies ran while one was open for 0% of the time, Pallas kernels for 8%

profile of v1, /device:TPU:6, one launch (start us, length us, event | category | flops | bytes accessed | tf_op | source)
XLA Modules:
  0.0 47.0 jit_solution(11553661358004650911)
XLA Ops:
  0.0 0.0 copy-start
  0.0 0.9 %copy.10.counts = s32[1,64,7]{2,1,0:T(8,128)S(1)} copy(s32[1,64,7]{1,0,2:T(1,128)} %param.12) | data formatting | bytes 3584 | tf_op args[3]
  0.9 0.1 pad_add_fusion.idx
  1.0 0.0 copy-start.1
  1.0 1.2 %copy-done.1 = bf16[32,4,16,256]{3,2,1,0:T(8,128)(2,1)S(1)} copy-done((bf16[32,4,16,256]{3,2,1,0:T(8,128)(2,1)S(1)}, bf16[32,4,16,256]{3,2,1,0:T(8,128)(2,1)}, u32[]{:S(2)}) %copy-start.1) | copy-done | bytes 1048600
  2.2 0.0 copy-start.4
  2.2 0.8 %copy-done.4 = s32[1,64,224]{2,1,0:T(8,128)S(1)} copy-done((s32[1,64,224]{2,1,0:T(8,128)S(1)}, s32[1,64,224]{2,1,0:T(8,128)}, u32[]{:S(2)}) %copy-start.4) | copy-done | bytes 57368
  3.1 0.0 copy-start.5
  3.1 0.8 %copy-done.5 = s32[1,64,224]{2,1,0:T(8,128)S(1)} copy-done((s32[1,64,224]{2,1,0:T(8,128)S(1)}, s32[1,64,224]{2,1,0:T(8,128)}, u32[]{:S(2)}) %copy-start.5) | copy-done | bytes 57368
  3.9 0.0 copy-start.6
  3.9 0.8 %copy-done.6 = s32[1,64,224]{2,1,0:T(8,128)S(1)} copy-done((s32[1,64,224]{2,1,0:T(8,128)S(1)}, s32[1,64,224]{2,1,0:T(8,128)}, u32[]{:S(2)}) %copy-start.6) | copy-done | bytes 57368
  4.7 0.0 copy-start.11
  4.7 2.7 %edge.1 = (bf16[272,256]{1,0:T(8,128)(2,1)}, bf16[272,256]{1,0:T(8,128)(2,1)}, s32[8,256]{1,0:T(8,128)S(1)}) custom-call(s32[1,64,7]{2,1,0:T(8,128)S(1)} %copy.10.counts, s32[1,64,224]{2,1,0:T(8,128)S(1)} %copy-done.4, s32[1,64,224]{2,1,0:T(8,128)S(1)} %copy-done.5, s32[1,64,224]{2,1,0:T(8,128)S(1)} %copy-done.6, bf16[32,4,16,256]{3,2,1,0:T(8,128)(2,1)S(1)} %copy-done.1, ...), custom_call_target="tpu_custom_call" | custom-call | flops 1000000000 | bytes 3000000 | tf_op jit(solution)/shard_map/edge/pallas_call | solution.py:309
  7.4 2.2 %collective-permute-start = (bf16[272,256]{1,0:T(8,128)(2,1)}, bf16[272,256]{1,0:T(8,128)(2,1)S(1)}, u32[]{:S(2)}, u32[]{:S(2)}) collective-permute-start(bf16[272,256]{1,0:T(8,128)(2,1)} %get-tuple-element.20), channel_id=1, source_target_pairs={{0,1},{1,2},{2,3},{3,0},{4,5},{5,6},{6,7},{7,4},{8,9},{9,10},{10,1... | collective-permute-start | bytes 417800 | tf_op jit(solution)/shard_map/ppermute | solution.py:302
  9.6 0.0 collective-permute-start.1
  9.6 0.0 copy-done.11
  9.7 0.0 copy-done
  9.7 0.0 copy-start.12
  9.7 1.7 %project.1 = (bf16[4,256,512]{2,1,0:T(8,128)(2,1)S(1)}, bf16[4,256,512]{2,1,0:T(8,128)(2,1)S(1)}) custom-call(bf16[4,64,768]{2,1,0:T(8,128)(2,1)S(1)} %bitcast.5, bf16[4,768,512]{2,1,0:T(8,128)(2,1)S(1)} %copy-done), custom_call_target="tpu_custom_call" | custom-call | flops 3000000000 | bytes 9000000 | tf_op jit(solution)/shard_map/project/pallas_call | solution.py:320
  11.4 0.0 copy-start.7
  11.4 1.0 %copy-done.7 = bf16[4,256,512]{2,1,0:T(8,128)(2,1)} copy-done((bf16[4,256,512]{2,1,0:T(8,128)(2,1)}, bf16[4,256,512]{2,1,0:T(8,128)(2,1)S(1)}, u32[]{:S(2)}) %copy-start.7) | copy-done | bytes 1048600
  12.4 0.0 copy-start.9
  12.4 1.0 %copy-done.9 = bf16[4,256,512]{2,1,0:T(8,128)(2,1)} copy-done((bf16[4,256,512]{2,1,0:T(8,128)(2,1)}, bf16[4,256,512]{2,1,0:T(8,128)(2,1)S(1)}, u32[]{:S(2)}) %copy-start.9) | copy-done | bytes 1048600
  13.4 0.0 copy-done.12
  13.4 0.1 copy.12.enc
  13.5 0.0 collective-permute-done.left
  13.5 2.6 %collective-permute-done.1.right = bf16[272,256]{1,0:T(8,128)(2,1)S(1)} collective-permute-done((bf16[272,256]{1,0:T(8,128)(2,1)}, bf16[272,256]{1,0:T(8,128)(2,1)S(1)}, u32[]{:S(2)}, u32[]{:S(2)}) %collective-permute-start.1) | collective-permute-done | bytes 139296 | tf_op jit(solution)/shard_map/ppermute | solution.py:302
  16.1 0.0 copy-start.8
  16.1 1.2 %copy-done.8 = bf16[4,256,512]{2,1,0:T(8,128)(2,1)S(1)} copy-done((bf16[4,256,512]{2,1,0:T(8,128)(2,1)S(1)}, bf16[4,256,512]{2,1,0:T(8,128)(2,1)}, u32[]{:S(2)}) %copy-start.8) | copy-done | bytes 1048600
  17.3 0.0 copy-start.10
  17.3 1.2 %copy-done.10 = bf16[4,256,512]{2,1,0:T(8,128)(2,1)S(1)} copy-done((bf16[4,256,512]{2,1,0:T(8,128)(2,1)S(1)}, bf16[4,256,512]{2,1,0:T(8,128)(2,1)}, u32[]{:S(2)}) %copy-start.10) | copy-done | bytes 1048600
  18.6 0.0 copy-start.2
  18.6 0.0 copy-start.3
  18.6 2.6 %place.1 = (f32[240,512]{1,0:T(8,128)S(1)}, bf16[112,512]{1,0:T(8,128)(2,1)S(1)}, bf16[112,512]{1,0:T(8,128)(2,1)S(1)}) custom-call(s32[8,256]{1,0:T(8,128)S(1)} %get-tuple-element.19.own, bf16[272,256]{1,0:T(8,128)(2,1)S(1)} %collective-permute-done.left, bf16[272,256]{1,0:T(8,128)(2,1)S(1)} %collective-permute-done.1.right, ...), custom_call_target="tpu_custom_call" | custom-call | flops 2000000000 | bytes 6000000 | tf_op jit(solution)/shard_map/place/pallas_call | solution.py:332
  21.1 0.1 collective-permute-start.2
  21.2 6.0 %collective-permute-start.3 = (bf16[112,512]{1,0:T(8,128)(2,1)S(1)}, bf16[112,512]{1,0:T(8,128)(2,1)S(1)}, u32[]{:S(2)}, u32[]{:S(2)}) collective-permute-start(bf16[112,512]{1,0:T(8,128)(2,1)S(1)} %get-tuple-element.26), channel_id=1, source_target_pairs={{0,244},{4,248},{8,252},{12,0},{16,4},{20,8},{24,12},{28,16},{32,2... | collective-permute-start | bytes 344072 | tf_op jit(solution)/shard_map/ppermute | solution.py:302
  27.2 0.0 copy-done.2
  27.2 0.0 copy-done.3
  27.2 2.1 %encode.1 = (f32[2,64,1280]{2,1,0:T(8,128)S(1)}, bf16[2,320,256]{2,1,0:T(8,128)(2,1)S(1)}, bf16[4,512,256]{2,1,0:T(8,128)(2,1)S(1)}, bf16[2,128,1152]{2,1,0:T(8,128)(2,1)S(1)}) custom-call(bf16[32,4,16,256]{3,2,1,0:T(8,128)(2,1)S(1)} %copy-done.2, bf16[272,256]{1,0:T(8,128)(2,1)S(1)} %collective-permute-done.left, ...), custom_call_target="tpu_custom_call" | custom-call | flops 4000000000 | bytes 12000000 | tf_op jit(solution)/shard_map/encode/pallas_call | solution.py:342
  29.3 0.5 collective-permute-done.2.up
  29.7 2.1 %collective-permute-done.3.down = bf16[112,512]{1,0:T(8,128)(2,1)S(1)} collective-permute-done((bf16[112,512]{1,0:T(8,128)(2,1)S(1)}, bf16[112,512]{1,0:T(8,128)(2,1)S(1)}, u32[]{:S(2)}, u32[]{:S(2)}) %collective-permute-start.3) | collective-permute-done | bytes 114720 | tf_op jit(solution)/shard_map/ppermute | solution.py:302
  31.8 0.2 relay.1
  32.1 0.2 collective-permute-start.4
  32.3 4.9 %collective-permute-start.5 = (bf16[480,256]{1,0:T(8,128)(2,1)S(1)}, bf16[480,256]{1,0:T(8,128)(2,1)S(1)}, u32[]{:S(2)}, u32[]{:S(2)}) collective-permute-start(bf16[480,256]{1,0:T(8,128)(2,1)S(1)} %get-tuple-element.29), channel_id=1, source_target_pairs={{0,252},{4,0},{8,4},{12,8},{16,12},{20,16},{24,20},{28,24},{32,28}... | collective-permute-start | bytes 737288 | tf_op jit(solution)/shard_map/ppermute | solution.py:302
  37.2 3.9 %collective-permute-done.4.below = bf16[480,256]{1,0:T(8,128)(2,1)S(1)} collective-permute-done((bf16[480,256]{1,0:T(8,128)(2,1)S(1)}, bf16[480,256]{1,0:T(8,128)(2,1)S(1)}, u32[]{:S(2)}, u32[]{:S(2)}) %collective-permute-start.4) | collective-permute-done | bytes 245792 | tf_op jit(solution)/shard_map/ppermute | solution.py:302
  41.1 0.0 collective-permute-done.5.above
  41.1 5.8 %decode.1 = bf16[32,4,16,256]{3,2,1,0:T(8,128)(2,1)} custom-call(f32[240,512]{1,0:T(8,128)S(1)} %get-tuple-element.24.mine, bf16[112,512]{1,0:T(8,128)(2,1)S(1)} %collective-permute-done.2.up, bf16[112,512]{1,0:T(8,128)(2,1)S(1)} %collective-permute-done.3.down, bf16[480,256]{1,0:T(8,128)(2,1)S(1)} %collective-permute-done.4.below, ...), custom_call_target="tpu_custom_call" | custom-call | flops 6000000000 | bytes 18000000 | tf_op jit(solution)/shard_map/decode/pallas_call | solution.py:364
  (1 shorter events, 0.0 us)
Async XLA Ops:
  0.0 9.7 %copy-start = (bf16[4,768,512]{2,1,0:T(8,128)(2,1)S(1)}, bf16[4,768,512]{2,1,0:T(8,128)(2,1)}, u32[]{:S(2)}) copy-start(bf16[4,768,512]{2,1,0:T(8,128)(2,1)} %proj.1) | copy-start | bytes 9437188
  1.0 1.2 %copy-start.1 = (bf16[32,4,16,256]{3,2,1,0:T(8,128)(2,1)S(1)}, bf16[32,4,16,256]{3,2,1,0:T(8,128)(2,1)}, u32[]{:S(2)}) copy-start(bf16[32,4,16,256]{3,2,1,0:T(8,128)(2,1)} %state.3) | copy-start | bytes 3145732
  2.2 0.8 %copy-start.4 = (s32[1,64,224]{2,1,0:T(8,128)S(1)}, s32[1,64,224]{2,1,0:T(8,128)}, u32[]{:S(2)}) copy-start(s32[1,64,224]{2,1,0:T(8,128)} %block.1) | copy-start | bytes 172036
  3.1 0.8 %copy-start.5 = (s32[1,64,224]{2,1,0:T(8,128)S(1)}, s32[1,64,224]{2,1,0:T(8,128)}, u32[]{:S(2)}) copy-start(s32[1,64,224]{2,1,0:T(8,128)} %tile.1) | copy-start | bytes 172036
  3.9 0.8 %copy-start.6 = (s32[1,64,224]{2,1,0:T(8,128)S(1)}, s32[1,64,224]{2,1,0:T(8,128)}, u32[]{:S(2)}) copy-start(s32[1,64,224]{2,1,0:T(8,128)} %view.1) | copy-start | bytes 172036
  4.7 4.9 %copy-start.11 = (bf16[64,4,768]{2,1,0:T(4,128)(2,1)S(1)}, bf16[64,4,768]{2,1,0:T(4,128)(2,1)}, u32[]{:S(2)}) copy-start(bf16[64,4,768]{2,1,0:T(4,128)(2,1)} %param.10) | copy-start | bytes 1179652
  7.4 6.1 %collective-permute-start = (bf16[272,256]{1,0:T(8,128)(2,1)}, bf16[272,256]{1,0:T(8,128)(2,1)S(1)}, u32[]{:S(2)}, u32[]{:S(2)}) collective-permute-start(bf16[272,256]{1,0:T(8,128)(2,1)} %get-tuple-element.20), channel_id=1, source_target_pairs={{0,1},{1,2},{2,3},{3,0},{4,5},{5,6},{6,7},{7,4},{8,9},{9,10},{10,1... | collective-permute-start | bytes 417800 | tf_op jit(solution)/shard_map/ppermute | solution.py:302
  9.6 6.5 %collective-permute-start.1 = (bf16[272,256]{1,0:T(8,128)(2,1)}, bf16[272,256]{1,0:T(8,128)(2,1)S(1)}, u32[]{:S(2)}, u32[]{:S(2)}) collective-permute-start(bf16[272,256]{1,0:T(8,128)(2,1)} %get-tuple-element.21), channel_id=1, source_target_pairs={{0,3},{1,0},{2,1},{3,2},{4,7},{5,4},{6,5},{7,6},{8,11},{9,8},{10,9... | collective-permute-start | bytes 417800 | tf_op jit(solution)/shard_map/ppermute | solution.py:302
  9.7 3.7 %copy-start.12 = (bf16[2,2,2,64,33]{3,2,4,1,0:T(2,128)(2,1)S(1)}, bf16[2,2,2,64,33]{3,2,4,1,0:T(2,128)(2,1)}, u32[]{:S(2)}) copy-start(bf16[2,2,2,64,33]{3,2,4,1,0:T(2,128)(2,1)} %param.16) | copy-start | bytes 101380
  11.4 1.0 %copy-start.7 = (bf16[4,256,512]{2,1,0:T(8,128)(2,1)}, bf16[4,256,512]{2,1,0:T(8,128)(2,1)S(1)}, u32[]{:S(2)}) copy-start(bf16[4,256,512]{2,1,0:T(8,128)(2,1)S(1)} %get-tuple-element.22.high) | copy-start | bytes 3145732
  12.4 1.0 %copy-start.9 = (bf16[4,256,512]{2,1,0:T(8,128)(2,1)}, bf16[4,256,512]{2,1,0:T(8,128)(2,1)S(1)}, u32[]{:S(2)}) copy-start(bf16[4,256,512]{2,1,0:T(8,128)(2,1)S(1)} %get-tuple-element.23.low) | copy-start | bytes 3145732
  16.1 1.2 %copy-start.8 = (bf16[4,256,512]{2,1,0:T(8,128)(2,1)S(1)}, bf16[4,256,512]{2,1,0:T(8,128)(2,1)}, u32[]{:S(2)}) copy-start(bf16[4,256,512]{2,1,0:T(8,128)(2,1)} %copy-done.7) | copy-start | bytes 3145732
  17.3 1.2 %copy-start.10 = (bf16[4,256,512]{2,1,0:T(8,128)(2,1)S(1)}, bf16[4,256,512]{2,1,0:T(8,128)(2,1)}, u32[]{:S(2)}) copy-start(bf16[4,256,512]{2,1,0:T(8,128)(2,1)} %copy-done.9) | copy-start | bytes 3145732
  18.6 8.6 %copy-start.2 = (bf16[32,4,16,256]{3,2,1,0:T(8,128)(2,1)S(1)}, bf16[32,4,16,256]{3,2,1,0:T(8,128)(2,1)}, u32[]{:S(2)}) copy-start(bf16[32,4,16,256]{3,2,1,0:T(8,128)(2,1)} %state.3) | copy-start | bytes 3145732
  18.6 8.6 %copy-start.3 = (bf16[4,4,4,32,64]{4,3,2,1,0:T(8,128)(2,1)S(1)}, bf16[4,4,4,32,64]{4,3,2,1,0:T(8,128)(2,1)}, u32[]{:S(2)}) copy-start(bf16[4,4,4,32,64]{4,3,2,1,0:T(8,128)(2,1)} %dec.1) | copy-start | bytes 786436
  21.1 8.6 %collective-permute-start.2 = (bf16[112,512]{1,0:T(8,128)(2,1)S(1)}, bf16[112,512]{1,0:T(8,128)(2,1)S(1)}, u32[]{:S(2)}, u32[]{:S(2)}) collective-permute-start(bf16[112,512]{1,0:T(8,128)(2,1)S(1)} %get-tuple-element.25), channel_id=1, source_target_pairs={{0,12},{4,16},{8,20},{12,24},{16,28},{20,32},{24,36},{28,40},{32,4... | collective-permute-start | bytes 344072 | tf_op jit(solution)/shard_map/ppermute | solution.py:302
  21.2 10.6 %collective-permute-start.3 = (bf16[112,512]{1,0:T(8,128)(2,1)S(1)}, bf16[112,512]{1,0:T(8,128)(2,1)S(1)}, u32[]{:S(2)}, u32[]{:S(2)}) collective-permute-start(bf16[112,512]{1,0:T(8,128)(2,1)S(1)} %get-tuple-element.26), channel_id=1, source_target_pairs={{0,244},{4,248},{8,252},{12,0},{16,4},{20,8},{24,12},{28,16},{32,2... | collective-permute-start | bytes 344072 | tf_op jit(solution)/shard_map/ppermute | solution.py:302
  32.1 9.0 %collective-permute-start.4 = (bf16[480,256]{1,0:T(8,128)(2,1)S(1)}, bf16[480,256]{1,0:T(8,128)(2,1)S(1)}, u32[]{:S(2)}, u32[]{:S(2)}) collective-permute-start(bf16[480,256]{1,0:T(8,128)(2,1)S(1)} %get-tuple-element.28), channel_id=1, source_target_pairs={{0,4},{4,8},{8,12},{12,16},{16,20},{20,24},{24,28},{28,32},{32,36}... | collective-permute-start | bytes 737288 | tf_op jit(solution)/shard_map/ppermute | solution.py:302
  32.3 8.8 %collective-permute-start.5 = (bf16[480,256]{1,0:T(8,128)(2,1)S(1)}, bf16[480,256]{1,0:T(8,128)(2,1)S(1)}, u32[]{:S(2)}, u32[]{:S(2)}) collective-permute-start(bf16[480,256]{1,0:T(8,128)(2,1)S(1)} %get-tuple-element.29), channel_id=1, source_target_pairs={{0,252},{4,0},{8,4},{12,8},{16,12},{20,16},{24,20},{28,24},{32,28}... | collective-permute-start | bytes 737288 | tf_op jit(solution)/shard_map/ppermute | solution.py:302

commit v2 on v1

v2 whole, which is shorter than its diff:
```python
import jax
import jax.numpy as jnp
from jax import lax
from jax.experimental import pallas as pl
from jax.experimental.pallas import tpu as pltpu
from jax.sharding import PartitionSpec as P

C1, C2 = 32, 64
ZD, YD, XD = 4, 16, 256
XC = XD // 2
SPAN = 7
NPD = 224
VIEWS = 4
NB = 64
DC = 768
TILE = 512
KL = 256
ROWS = 10
NL = ROWS * XC
CHIP = 12 * ROWS
OWN = 8 * ROWS
FAR = 6 * ROWS
MATE = 10 * ROWS
LIST = 256
BF, F32, I32 = jnp.bfloat16, jnp.float32, jnp.int32
MIB = 1024 * 1024


def dot(a, b):
    return jnp.dot(a, b, preferred_element_type=F32)


def iota(shape, dim):
    return lax.broadcasted_iota(I32, shape, dim)


def split_columns():
    row, col = iota((XD, XD), 0), iota((XD, XD), 1)
    return (row == 2 * (col % XC) + col // XC).astype(BF)


def merge_columns():
    row, col = iota((XD, XD), 0), iota((XD, XD), 1)
    return (col == 2 * (row % XC) + row // XC).astype(BF)


def edge_kernel(counts, block, tile, view, state, idx, up, down, own, lists, cs, pairs, planes, sems):
    slab = idx[0]
    at = pl.multiple_of((slab // 8) * 8, 8)
    copies = [pltpu.make_async_copy(counts, cs, sems.at[0])]
    for i, ref in enumerate((block, tile, view)):
        copies.append(pltpu.make_async_copy(ref.at[0, pl.ds(at, 8)], pairs.at[i], sems.at[1 + i]))
    for z in range(ZD):
        copies.append(pltpu.make_async_copy(state.at[:, z], planes.at[z], sems.at[4 + z]))
    for copy in copies:
        copy.start()
    split = split_columns()
    row, col = iota((4 * C1, C1 * YD), 0), iota((4 * C1, C1 * YD), 1)
    y = row // C1
    y = jnp.where(y < 2, y, y + YD - 4)
    pick = (col == (row % C1) * YD + y).astype(BF)
    lists[...] = jnp.full((16, KL), -1.0, F32)
    own[...] = jnp.full((8, KL), -1, I32)
    for copy in copies[:4]:
        copy.wait()
    slot = iota((1, NPD), 1)
    group = jnp.zeros((1, NPD), I32)
    end = 0
    for o in range(SPAN):
        end = end + cs[o, 0, slab]
        group = group + (slot >= end).astype(I32)
    valid = group < SPAN
    rest = pl.ds(slab % 8, 1)
    b, t, v = pairs[0, rest, :], pairs[1, rest, :], pairs[2, rest, :]
    key = v * NB + b
    own[0:1, :NPD] = key
    own[1:2, :NPD] = jnp.where(valid, group * 16 + t + 1, -1)
    lists[0:1, :NPD] = key.astype(F32)
    lists[1:2, :NPD] = jnp.where(valid & (t == 7), group, -1).astype(F32)
    up[LIST:, :] = lists[...].astype(BF)
    lists[1:2, :NPD] = jnp.where(valid & (t == 0), group, -1).astype(F32)
    down[LIST:, :] = lists[...].astype(BF)
    for z in range(ZD):
        copies[4 + z].wait()
        rows = dot(dot(pick, planes[z].reshape(C1 * YD, XD)).astype(BF), split).astype(BF)
        down[z * 64 : z * 64 + 64, :] = rows[:64]
        up[z * 64 : z * 64 + 64, :] = rows[64:]


def project_kernel(res, proj, high, low):
    rays = res[...].reshape(4 * NB, DC)
    y = dot(rays, proj[0])
    hi = y.astype(BF)
    lo = (y - hi.astype(F32)).astype(BF)
    for r in range(4):
        high[r] = hi[r * NB : (r + 1) * NB]
        low[r] = lo[r * NB : (r + 1) * NB]


def place_kernel(own, left, right, high, low, we, idx, win, near, far, mate, fh, keys, x):
    slab, part = idx[0], idx[1]
    core = slab % 2
    keys[0:1, 0:KL] = own[0:1, :].astype(F32)
    keys[1:2, 0:KL] = own[1:2, :].astype(F32)
    lk = left[LIST:, :].astype(F32)
    rk = right[LIST:, :].astype(F32)
    keys[0:1, KL : 2 * KL] = lk[0:1]
    keys[0:1, 2 * KL :] = rk[0:1]
    lg, rg = lk[1:2], rk[1:2]
    keys[1:2, KL : 2 * KL] = jnp.where((lg >= 0) & (part > 0), lg * 16, -1.0)
    keys[1:2, 2 * KL :] = jnp.where((rg >= 0) & (part < 3), rg * 16 + 9, -1.0)
    key = keys[0:1, :].astype(I32)
    skey = keys[1:2, :].astype(I32)
    total = 416
    row = iota((total, 1), 0)

    def pieces(values):
        w, n, m, f = values
        return jnp.where(row < 120, w, jnp.where(row < 240, n, jnp.where(row < 352, m, f)))

    k = row - pieces((0, 120, 240, 352))
    t = k // ROWS
    n = k % ROWS
    even = core == 0
    first = jnp.where(even, pieces((-2, 1, 6, -7)), pieces((5, 2, -3, 10)))
    step = jnp.where(even, pieces((1, -1, 1, -1)), pieces((-1, 1, -1, 1)))
    s = first + step * t + 12
    rkey = jnp.where(t < pieces((12, 12, 10, 6)), (s // 4) * 16 + n, -2)
    r = s % 4
    a = (rkey == skey).astype(BF)
    bk = (iota((VIEWS * NB, 1), 0) == key).astype(BF)
    count = lax.dot_general(a, bk, (((1,), (1,)), ((), ())), preferred_element_type=F32)
    acc = jnp.zeros((total, TILE), F32)
    for q in range(4):
        c = jnp.where(r == q, count, 0.0).astype(BF)
        acc = acc + dot(c, high[q]) + dot(c, low[q])
    win[...] = acc[:120]
    near[...] = acc[120:240]
    mate[...] = acc[240:352].astype(BF)
    far[...] = acc[352:]
    for a in range(2):
        for p in range(2):
            for q in range(2):
                for s in range(2):
                    k = (p * 4 + q * 2 + s) * C1
                    lanes = slice(s * XC, (s + 1) * XC)
                    h = (2 * a + p) * 64 + q * C1
                    x[k : k + C1, 2 * a * XC : (2 * a + 1) * XC] = left[h : h + C1, lanes]
                    x[k : k + C1, (2 * a + 1) * XC : (2 * a + 2) * XC] = right[h : h + C1, lanes]
    f = lax.dot_general(we[...], x[...], (((0,), (0,)), ((), ())), preferred_element_type=F32)
    fh[0] = f[:, :XD]
    fh[1] = f[:, XD:]


def encode_kernel(state, enc, fs, planes, we, wb, x):
    split = split_columns()
    row, col = iota((C1 * YD, C1 * YD), 0), iota((C1 * YD, C1 * YD), 1)
    perm = (col == (row % C1) * YD + row // C1).astype(BF)
    rows = iota((32, C2), 0)
    bias = [jnp.zeros((32, C2), F32) for _ in range(4)]
    for p in range(2):
        for q in range(2):
            e = enc[p, q].astype(F32)
            for s in range(2):
                k = p * 4 + q * 2 + s
                es = e[:, s, :]
                we[k * C1 : (k + 1) * C1, :] = es[:C1].astype(BF)
                for a in range(4):
                    bias[a] = bias[a] + jnp.where(rows == (q * 2 + s) * 8 + 2 * a + p, es[C1 : C1 + 1], 0.0)
    for a in range(4):
        wb[a] = bias[a].astype(BF)
    for a in range(2):
        for p in range(2):
            z = 2 * a + p
            plane = state[:, z].reshape(C1 * YD, XD)
            d = dot(dot(perm, plane).astype(BF), split).astype(BF)
            planes[z] = d
            for q in range(2):
                for s in range(2):
                    k = (p * 4 + q * 2 + s) * C1
                    for b in range(8):
                        y = (2 * b + q) * C1
                        x[k : k + C1, b * XC : (b + 1) * XC] = d[y : y + C1, s * XC : (s + 1) * XC]
        fs[a] = lax.dot_general(we[...], x[...], (((0,), (0,)), ((), ())), preferred_element_type=F32)


def weights_kernel(dec, wdec):
    wdec[...] = jnp.zeros_like(wdec)
    taps = (((0, 3), (1, 1)), ((1, 2), (2, 0)))
    for pz in range(2):
        for sel in range(2):
            kz = taps[pz][sel][1]
            for py in range(2):
                for dy, ky in taps[py]:
                    for px in range(2):
                        for dx, kx in taps[px]:
                            r0 = (py * 2 + px) * C1
                            c0 = (sel * 9 + dy * 3 + dx) * C2
                            wdec[pz, r0 : r0 + C1, c0 : c0 + C2] = dec[kz, ky, kx]


def put_plane(pay, start, fs, fh, plane):
    for n in range(ROWS):
        if n == 0:
            f = fh[plane, :, :XC]
        elif n == 9:
            f = fh[plane, :, XC:]
        else:
            f = fs[plane, :, (n - 1) * XC : n * XC]
        r0 = start + (n // 2) * C2
        pay[r0 : r0 + C2, (n % 2) * XC : (n % 2 + 1) * XC] = f.astype(BF)


def out_kernel(near, far, got, fs, fh, idx, pay, pay_far, tmp):
    tmp[0:CHIP] = near[...]
    tmp[CHIP:128] = jnp.zeros((8, TILE), F32)
    tmp[0:MATE] += got[...].astype(F32)[:MATE]
    total = tmp[...].astype(BF)
    pay[0:128, :] = total[:, :XD]
    pay[128:256, :] = total[:, XD:]
    tmp[0:64] = far[...]
    tmp[0 : 2 * ROWS] += got[...].astype(F32)[8 * ROWS : MATE]
    pay_far[...] = tmp[0:64].astype(BF)
    put_plane(pay, 256, fs, fh, idx[0] % 2)


def window(win, near, far):
    left = win[:, :XD] + near[0:128, :].astype(F32)[:CHIP]
    right = win[:, XD:] + near[128:256, :].astype(F32)[:CHIP]
    return left, right, far[...].astype(F32)


def mate_kernel(win, near, far, fs, fh, idx, pay, tmp):
    for q, half in enumerate(window(win, near, far)[:2]):
        tmp[...] = half
        tmp[0:64] += far[:, q * XD : (q + 1) * XD].astype(F32)
        pay[q * OWN : (q + 1) * OWN, :] = tmp[CHIP - OWN :, :].astype(BF)
    put_plane(pay, 2 * OWN, fs, fh, 1 - idx[0] % 2)


def decode_kernel(win, near, far, mate, fs, fh, planes, wdec, wb, idx, out, bp, x, ns, tmp):
    slab, part = idx[0], idx[1]
    core = slab % 2
    split = split_columns()
    merge = merge_columns()
    row, col = iota((C1 * YD, C1 * YD), 0), iota((C1 * YD, C1 * YD), 1)
    perm = (col == (row % YD) * C1 + row // YD).astype(BF)
    row, col = iota((OWN, OWN), 0), iota((OWN, OWN), 1)
    turn = ((col % ROWS == row % ROWS) & (col // ROWS == 7 - row // ROWS)).astype(BF)
    z = row % 8
    z = jnp.where(core == 0, z, 7 - z)
    sort = ((col % ROWS == row // 8) & (col // ROWS == z)).astype(BF)
    for q, half in enumerate(window(win, near, far)[:2]):
        tmp[...] = half
        tmp[0:64] += far[:, q * XD : (q + 1) * XD].astype(F32)
        t = tmp[0:OWN] + dot(turn, mate[q * OWN : (q + 1) * OWN, :])
        t = dot(dot(sort, t.astype(BF)).astype(BF), split)
        for s in range(2):
            for n in range(ROWS):
                bp[(q * 2 + s) * 8 : (q * 2 + s + 1) * 8, n * XC : (n + 1) * XC] = t[
                    n * 8 : (n + 1) * 8, s * XC : (s + 1) * XC
                ]
    bpb = bp[...].astype(BF)
    lane = iota((C2, XC), 1)
    for a in range(4):
        pb = lax.dot_general(wb[a], bpb, (((0,), (0,)), ((), ())), preferred_element_type=F32)
        inside = True
        if a == 0:
            inside = slab > 0
        if a == 3:
            inside = slab < 63
        for n in range(ROWS):
            lanes = slice(n * XC, (n + 1) * XC)
            if a in (1, 2):
                if n == 0:
                    v = fh[a - 1, :, :XC]
                elif n == 9:
                    v = fh[a - 1, :, XC:]
                else:
                    v = fs[a - 1, :, (n - 1) * XC : n * XC]
            else:
                half = slice((n % 2) * XC, (n % 2 + 1) * XC)
                r0 = (n // 2) * C2
                v1 = near[256 + r0 : 256 + r0 + C2, half].astype(F32)
                v2 = mate[2 * OWN + r0 : 2 * OWN + r0 + C2, half].astype(F32)
                v = jnp.where(core == (0 if a == 0 else 1), v1, v2)
            v = v + pb[:, lanes]
            v = 0.5 * v * (1.0 + jnp.tanh(0.79788456 * (v + 0.044715 * (v * v * v))))
            ok = inside
            if n == 0:
                ok = (part > 0) & ok
            if n == 9:
                ok = (part < 3) & ok
            if ok is not True:
                v = jnp.where(ok, v, 0.0)
            shifts = (
                jnp.where(lane == 0, 0.0, pltpu.roll(v, 1, 1)).astype(BF),
                v.astype(BF),
                jnp.where(lane == XC - 1, 0.0, pltpu.roll(v, XC - 1, 1)).astype(BF),
            )
            for dy in range(3):
                m = n - dy
                if 0 <= m < 8:
                    for dx in range(3):
                        r0 = a * 576 + dy * 192 + dx * C2
                        x[r0 : r0 + C2, m * XC : (m + 1) * XC] = shifts[dx]
    for f in range(ZD):
        start = (f + 1) // 2 * 576
        d = dot(wdec[f % 2], x[start : start + 1152, :])
        for py in range(2):
            for px in range(2):
                r0 = (py * 2 + px) * C1
                lanes = slice(px * XC, (px + 1) * XC)
                for m in range(8):
                    y = (2 * m + py) * C1
                    old = planes[f, y : y + C1, lanes].astype(F32)
                    ns[y : y + C1, lanes] = (old + d[r0 : r0 + C1, m * XC : (m + 1) * XC]).astype(BF)
        new = dot(dot(perm, ns[...]).astype(BF), merge).astype(BF)
        out[:, f] = new.reshape(C1, YD, XD)


V = pltpu.VMEM
SM = pl.BlockSpec(memory_space=pltpu.SMEM)
VM = pl.BlockSpec(memory_space=pltpu.VMEM)
ANY = pl.BlockSpec(memory_space=pl.ANY)


def shape(dims, dtype=BF):
    return jax.ShapeDtypeStruct(dims, dtype)


def call(kernel, ins, outs, scratch=(), cost=None, vlim=16 * MIB, **more):
    return pl.pallas_call(
        kernel,
        in_specs=ins,
        out_specs=[VM] * len(outs) if "grid" not in more else more.pop("specs"),
        out_shape=outs,
        scratch_shapes=scratch,
        compiler_params=pltpu.CompilerParams(vmem_limit_bytes=vlim),
        cost_estimate=cost,
        **more,
    )


def cost(us):
    return pl.CostEstimate(flops=int(us * 1e9), bytes_accessed=int(us * 3e6), transcendentals=0)


def shifted(block, axis, distance):
    n = lax.axis_size(axis)
    return lax.ppermute(block, axis, [(i, (i + distance) % n) for i in range(n)])


def swapped(block, distance):
    n = lax.axis_size("gz")
    route = []
    for i in range(0, n, 2):
        j = (i + distance) % n
        route += [(i, j), (j, i)]
    return lax.ppermute(block, "gz", route)


def per_device(
    state, residual, projector, pair_counts, pair_block, pair_tile, pair_view, enc_weight, dec_weight
):
    idx = jnp.stack([lax.axis_index("gz"), lax.axis_index("gy")]).astype(I32)
    up, down, own = call(
        edge_kernel,
        [ANY] * 5 + [SM],
        [shape((272, XD)), shape((272, XD)), shape((8, KL), I32)],
        [
            V((16, KL), F32),
            pltpu.SMEM((SPAN, 1, 64), I32),
            V((3, 8, NPD), I32),
            V((ZD, C1, YD, XD), BF),
            pltpu.SemaphoreType.DMA((8,)),
        ],
        cost=cost(1.0),
        vlim=56 * MIB,
        name="edge",
    )(jnp.transpose(pair_counts, (2, 0, 1)), pair_block, pair_tile, pair_view, state, idx)
    left = shifted(up, "gy", 1)
    right = shifted(down, "gy", -1)
    rays = jnp.transpose(residual, (1, 0, 2))
    high, low = call(
        project_kernel,
        [
            pl.BlockSpec((4, NB, DC), lambda v: (0, 0, 0)),
            pl.BlockSpec((1, DC, TILE), lambda v: (v, 0, 0)),
        ],
        [shape((4, VIEWS * NB, TILE)), shape((4, VIEWS * NB, TILE))],
        cost=cost(2.0),
        grid=(VIEWS,),
        specs=[pl.BlockSpec((4, NB, TILE), lambda v: (0, v, 0))] * 2,
        name="project",
    )(rays, projector)
    fs, planes, we, wb = call(
        encode_kernel,
        [VM] * 2,
        [
            shape((2, C2, 8 * XC), F32),
            shape((ZD, C1 * YD, XD)),
            shape((8 * C1, C2)),
            shape((4, 32, C2)),
        ],
        [V((8 * C1, 8 * XC), BF)],
        cost=cost(2.0),
        name="encode",
    )(state, jnp.transpose(enc_weight, (0, 1, 4, 2, 3)))
    win, near, far, mate, fh = call(
        place_kernel,
        [VM] * 6 + [SM],
        [
            shape((CHIP, TILE), F32),
            shape((CHIP, TILE), F32),
            shape((64, TILE), F32),
            shape((112, TILE)),
            shape((2, C2, XD), F32),
        ],
        [V((8, 3 * KL), F32), V((8 * C1, 4 * XC), BF)],
        cost=cost(2.5),
        name="place",
    )(own, left, right, high, low, we, idx)
    got = swapped(mate, 1)
    pay, pay_far = call(
        out_kernel,
        [VM] * 5 + [SM],
        [shape((576, XD)), shape((64, TILE))],
        [V((128, TILE), F32)],
        cost=cost(0.4),
        name="outward",
    )(near, far, got, fs, fh, idx)
    got_near = swapped(pay, -1)
    got_far = swapped(pay_far, -3)
    wdec = call(
        weights_kernel, [VM], [shape((2, 128, 1152))], cost=cost(3.0), name="weights"
    )(dec_weight)[0]
    pay_mate = call(
        mate_kernel,
        [VM] * 5 + [SM],
        [shape((2 * OWN + 5 * C2, XD))],
        [V((CHIP, XD), F32)],
        cost=cost(0.4),
        name="inward",
    )(win, got_near, got_far, fs, fh, idx)[0]
    got_mate = swapped(pay_mate, 1)
    return call(
        decode_kernel,
        [VM] * 9 + [SM],
        [shape((C1, ZD, YD, XD))],
        [V((32, NL), F32), V((2304, 8 * XC), BF), V((C1 * YD, XD), BF), V((CHIP, XD), F32)],
        cost=cost(6.0),
        vlim=24 * MIB,
        name="decode",
    )(win, got_near, got_far, got_mate, fs, fh, planes, wdec, wb, idx)[0]


def solution(mesh):
    in_specs = (
        P(None, "gz", "gy", None),
        P("gz", None, None),
        P(),
        P("gy", None, None),
        P("gy", None, None),
        P("gy", None, None),
        P("gy", None, None),
        P(),
        P(),
    )
    out_specs = P(None, "gz", "gy", None)
    return jax.shard_map(
        per_device, mesh=mesh, in_specs=in_specs, out_specs=out_specs, check_vma=False
    )
```

time: 47.3 us -> 42 us (0.89)
  the two profiles are of different devices: /device:TPU:6 before, /device:TPU:1 now
where the time goes in v2:
time: 42 us; the launch traced here: 41.9 us
  Pallas kernels  17.6 us (42%)
  starting transfers between devices  16.3 us (39%)
  waiting for transfers between devices  7.15 us (17%)
  other arithmetic  0.65 us (2%)
    ppermute x4, starting transfers between devices, swapped(): return lax.ppermute(block, 'gz', route)  12.8 us
    ppermute x4, waiting for transfers between devices, swapped(): return lax.ppermute(block, 'gz', route)  7.15 us
    pallas_call x1, Pallas kernels, per_device(): call(decode_kernel, [VM] * 9 + [SM], [shape((C1, ZD, YD, XD))], [V((32, N...  6.25 us
    pallas_call x1, Pallas kernels, per_device(): call(edge_kernel, [ANY] * 5 + [SM], [shape((272, XD)), shape((272, XD)),...  3.78 us
    ppermute x2, starting transfers between devices, shifted(): lax.ppermute(block, axis, [(i, (i + distance) % n) for i in range(n)])  3.48 us
    pallas_call x1, Pallas kernels, per_device(): call(place_kernel, [VM] * 6 + [SM], [shape((CHIP, TILE), F32), shape((CHI...  2.36 us
    pallas_call x1, Pallas kernels, per_device(): call(encode_kernel, [VM] * 2, [shape((2, C2, 8 * XC), F32), shape((ZD, C1...  2.12 us
    pallas_call x1, Pallas kernels, per_device(): call(project_kernel, [pl.BlockSpec((4, NB, DC), lambda v: (0, 0, 0)), pl....  1.69 us
  transfers between devices with their start and end apart: 6, of which 4 were waited for; matrix products, arithmetic and copies ran while one was open for 0% of the time, Pallas kernels for 10%

profile of v2, /device:TPU:1, one launch (start us, length us, event | category | flops | bytes accessed | tf_op | source)
XLA Modules:
  0.0 41.9 jit_solution(11914075391766034471)
XLA Ops:
  0.0 0.0 copy-start.2
  0.0 0.0 copy-start.4
  0.0 0.6 %pad_add_fusion.idx = s32[2]{0:T(128)} fusion(s32[1]{0:T(128)} %bitcast.2, s32[1]{0:T(128)} %bitcast.1), kind=kLoop, calls=%fused_computation.1 | loop fusion | flops 2 | bytes 16 | tf_op jit(solution)/shard_map/stack | solution.py:366
  0.7 3.8 %edge.1 = (bf16[272,256]{1,0:T(8,128)(2,1)}, bf16[272,256]{1,0:T(8,128)(2,1)}, s32[8,256]{1,0:T(8,128)}) custom-call(s32[7,1,64]{2,1,0:T(1,128)} %bitcast.9, s32[1,64,224]{2,1,0:T(8,128)} %block.1, s32[1,64,224]{2,1,0:T(8,128)} %tile.1, s32[1,64,224]{2,1,0:T(8,128)} %view.1, bf16[32,4,16,256]{3,2,1,0:T(8,128)(2,1)} %state.3, s32[2]{0:T(128)} %pad_add_fusion.idx), custom_call_target="tpu_custom_call" | custom-call | flops 1000000000 | bytes 3000000 | tf_op jit(solution)/shard_map/edge/pallas_call | solution.py:367
  4.4 2.1 %collective-permute-start = (bf16[272,256]{1,0:T(8,128)(2,1)}, bf16[272,256]{1,0:T(8,128)(2,1)S(1)}, u32[]{:S(2)}, u32[]{:S(2)}) collective-permute-start(bf16[272,256]{1,0:T(8,128)(2,1)} %get-tuple-element.22), channel_id=1, source_target_pairs={{0,1},{1,2},{2,3},{3,0},{4,5},{5,6},{6,7},{7,4},{8,9},{9,10},{10,1... | collective-permute-start | bytes 417800 | tf_op jit(solution)/shard_map/ppermute | solution.py:351
  6.6 1.4 %collective-permute-start.1 = (bf16[272,256]{1,0:T(8,128)(2,1)}, bf16[272,256]{1,0:T(8,128)(2,1)S(1)}, u32[]{:S(2)}, u32[]{:S(2)}) collective-permute-start(bf16[272,256]{1,0:T(8,128)(2,1)} %get-tuple-element.23), channel_id=1, source_target_pairs={{0,3},{1,0},{2,1},{3,2},{4,7},{5,4},{6,5},{7,6},{8,11},{9,8},{10,9... | collective-permute-start | bytes 417800 | tf_op jit(solution)/shard_map/ppermute | solution.py:351
  7.9 0.0 copy-done.2
  7.9 0.0 copy-done.4
  7.9 0.0 copy-start.6
  7.9 0.0 copy-start.1
  7.9 2.1 %encode.1 = (f32[2,64,1024]{2,1,0:T(8,128)S(1)}, bf16[4,512,256]{2,1,0:T(8,128)(2,1)S(1)}, bf16[256,64]{1,0:T(8,128)(2,1)S(1)}, bf16[4,32,64]{2,1,0:T(8,128)(2,1)S(1)}) custom-call(bf16[32,4,16,256]{3,2,1,0:T(8,128)(2,1)S(1)} %copy-done.2, bf16[2,2,33,2,64]{4,3,2,1,0:T(2,128)(2,1)S(1)} %bitcast.8), custom_call_target="tpu_custom_call" | custom-call | flops 2000000000 | bytes 6000000 | tf_op jit(solution)/shard_map/encode/pallas_call | solution.py:397
  10.1 0.0 copy-done.6
  10.1 0.0 copy-done.1
  10.1 0.0 copy-start
  10.1 0.0 copy-start.5
  10.2 1.7 %project.1 = (bf16[4,256,512]{2,1,0:T(8,128)(2,1)S(1)}, bf16[4,256,512]{2,1,0:T(8,128)(2,1)S(1)}) custom-call(bf16[4,64,768]{2,1,0:T(8,128)(2,1)S(1)} %bitcast.7, bf16[4,768,512]{2,1,0:T(8,128)(2,1)S(1)} %copy-done.1), custom_call_target="tpu_custom_call" | custom-call | flops 2000000000 | bytes 6000000 | tf_op jit(solution)/shard_map/project/pallas_call | solution.py:385
  11.8 0.0 collective-permute-done.left
  11.9 0.0 collective-permute-done.1.right
  11.9 0.0 copy-done
  11.9 0.0 copy-done.5
  11.9 0.0 copy-start.3
  11.9 2.4 %place.1 = (f32[120,512]{1,0:T(8,128)S(1)}, f32[120,512]{1,0:T(8,128)S(1)}, f32[64,512]{1,0:T(8,128)S(1)}, bf16[112,512]{1,0:T(8,128)(2,1)S(1)}, f32[2,64,256]{2,1,0:T(8,128)S(1)}) custom-call(s32[8,256]{1,0:T(8,128)S(1)} %copy-done.5, bf16[272,256]{1,0:T(8,128)(2,1)S(1)} %collective-permute-done.left, bf16[272,256]{1,0:T(8,128)(2,1)S(1)} %collective-permute-done.1.right, ...), custom_call_target="tpu_custom_call" | custom-call | flops 2500000000 | bytes 7500000 | tf_op jit(solution)/shard_map/place/pallas_call | solution.py:410
  14.3 3.2 %collective-permute-start.2 = (bf16[112,512]{1,0:T(8,128)(2,1)S(1)}, bf16[112,512]{1,0:T(8,128)(2,1)S(1)}, u32[]{:S(2)}, u32[]{:S(2)}) collective-permute-start(bf16[112,512]{1,0:T(8,128)(2,1)S(1)} %get-tuple-element.30), channel_id=1, source_target_pairs={{0,4},{4,0},{8,12},{12,8},{16,20},{20,16},{24,28},{28,24},{32,36},... | collective-permute-start | bytes 344072 | tf_op jit(solution)/shard_map/ppermute | solution.py:360
  17.4 1.0 %collective-permute-done.2.got = bf16[112,512]{1,0:T(8,128)(2,1)S(1)} collective-permute-done((bf16[112,512]{1,0:T(8,128)(2,1)S(1)}, bf16[112,512]{1,0:T(8,128)(2,1)S(1)}, u32[]{:S(2)}, u32[]{:S(2)}) %collective-permute-start.2) | collective-permute-done | bytes 114720 | tf_op jit(solution)/shard_map/ppermute | solution.py:360
  18.4 0.6 %outward.1 = (bf16[576,256]{1,0:T(8,128)(2,1)S(1)}, bf16[64,512]{1,0:T(8,128)(2,1)S(1)}) custom-call(f32[120,512]{1,0:T(8,128)S(1)} %get-tuple-element.28.near, f32[64,512]{1,0:T(8,128)S(1)} %get-tuple-element.29.far, bf16[112,512]{1,0:T(8,128)(2,1)S(1)} %collective-permute-done.2.got, f32[2,64,1024]{2,1,0:T(8,128)S(1)} %get-tuple-element.31.fs, ...), custom_call_target="tpu_custom_call" | custom-call | flops 400000000 | bytes 1200000 | tf_op jit(solution)/shard_map/outward/pallas_call | solution.py:425
  19.0 0.2 collective-permute-start.3
  19.2 1.5 %collective-permute-start.4 = (bf16[64,512]{1,0:T(8,128)(2,1)S(1)}, bf16[64,512]{1,0:T(8,128)(2,1)S(1)}, u32[]{:S(2)}, u32[]{:S(2)}) collective-permute-start(bf16[64,512]{1,0:T(8,128)(2,1)S(1)} %get-tuple-element.34), channel_id=1, source_target_pairs={{0,244},{244,0},{8,252},{252,8},{16,4},{4,16},{24,12},{12,24},{32,... | collective-permute-start | bytes 196616 | tf_op jit(solution)/shard_map/ppermute | solution.py:360
  20.7 5.1 %collective-permute-done.4.far = bf16[64,512]{1,0:T(8,128)(2,1)S(1)} collective-permute-done((bf16[64,512]{1,0:T(8,128)(2,1)S(1)}, bf16[64,512]{1,0:T(8,128)(2,1)S(1)}, u32[]{:S(2)}, u32[]{:S(2)}) %collective-permute-start.4) | collective-permute-done | bytes 65568 | tf_op jit(solution)/shard_map/ppermute | solution.py:360
  25.8 0.1 collective-permute-done.3.near
  26.0 0.6 %inward.1 = bf16[480,256]{1,0:T(8,128)(2,1)S(1)} custom-call(f32[120,512]{1,0:T(8,128)S(1)} %get-tuple-element.27.win, bf16[576,256]{1,0:T(8,128)(2,1)S(1)} %collective-permute-done.3.near, bf16[64,512]{1,0:T(8,128)(2,1)S(1)} %collective-permute-done.4.far, f32[2,64,1024]{2,1,0:T(8,128)S(1)} %get-tuple-element.31.fs, ...), custom_call_target="tpu_custom_call" | custom-call | flops 400000000 | bytes 1200000 | tf_op jit(solution)/shard_map/inward/pallas_call | solution.py:438
  26.5 8.0 %collective-permute-start.5 = (bf16[480,256]{1,0:T(8,128)(2,1)S(1)}, bf16[480,256]{1,0:T(8,128)(2,1)S(1)}, u32[]{:S(2)}, u32[]{:S(2)}) collective-permute-start(bf16[480,256]{1,0:T(8,128)(2,1)S(1)} %inward.1), channel_id=1, source_target_pairs={{0,4},{4,0},{8,12},{12,8},{16,20},{20,16},{24,28},{28,24},{32,36},... | collective-permute-start | bytes 737288 | tf_op jit(solution)/shard_map/ppermute | solution.py:360
  34.5 0.0 copy-done.3
  34.5 0.2 weights.1.wdec
  34.7 0.9 %collective-permute-done.5.mate = bf16[480,256]{1,0:T(8,128)(2,1)S(1)} collective-permute-done((bf16[480,256]{1,0:T(8,128)(2,1)S(1)}, bf16[480,256]{1,0:T(8,128)(2,1)S(1)}, u32[]{:S(2)}, u32[]{:S(2)}) %collective-permute-start.5) | collective-permute-done | bytes 245792 | tf_op jit(solution)/shard_map/ppermute | solution.py:360
  35.7 6.2 %decode.1 = bf16[32,4,16,256]{3,2,1,0:T(8,128)(2,1)} custom-call(f32[120,512]{1,0:T(8,128)S(1)} %get-tuple-element.27.win, bf16[576,256]{1,0:T(8,128)(2,1)S(1)} %collective-permute-done.3.near, bf16[64,512]{1,0:T(8,128)(2,1)S(1)} %collective-permute-done.4.far, bf16[480,256]{1,0:T(8,128)(2,1)S(1)} %collective-permute-done.5.mate, ...), custom_call_target="tpu_custom_call" | custom-call | flops 6000000000 | bytes 18000000 | tf_op jit(solution)/shard_map/decode/pallas_call | solution.py:447
  (1 shorter events, 0.0 us)
Async XLA Ops:
  0.0 7.9 %copy-start.2 = (bf16[32,4,16,256]{3,2,1,0:T(8,128)(2,1)S(1)}, bf16[32,4,16,256]{3,2,1,0:T(8,128)(2,1)}, u32[]{:S(2)}) copy-start(bf16[32,4,16,256]{3,2,1,0:T(8,128)(2,1)} %state.3) | copy-start | bytes 3145732
  0.0 7.9 %copy-start.4 = (bf16[2,2,2,64,33]{3,2,4,1,0:T(2,128)(2,1)S(1)}, bf16[2,2,2,64,33]{3,2,4,1,0:T(2,128)(2,1)}, u32[]{:S(2)}) copy-start(bf16[2,2,2,64,33]{3,2,4,1,0:T(2,128)(2,1)} %param.16) | copy-start | bytes 101380
  4.4 7.4 %collective-permute-start = (bf16[272,256]{1,0:T(8,128)(2,1)}, bf16[272,256]{1,0:T(8,128)(2,1)S(1)}, u32[]{:S(2)}, u32[]{:S(2)}) collective-permute-start(bf16[272,256]{1,0:T(8,128)(2,1)} %get-tuple-element.22), channel_id=1, source_target_pairs={{0,1},{1,2},{2,3},{3,0},{4,5},{5,6},{6,7},{7,4},{8,9},{9,10},{10,1... | collective-permute-start | bytes 417800 | tf_op jit(solution)/shard_map/ppermute | solution.py:351
  6.6 5.3 %collective-permute-start.1 = (bf16[272,256]{1,0:T(8,128)(2,1)}, bf16[272,256]{1,0:T(8,128)(2,1)S(1)}, u32[]{:S(2)}, u32[]{:S(2)}) collective-permute-start(bf16[272,256]{1,0:T(8,128)(2,1)} %get-tuple-element.23), channel_id=1, source_target_pairs={{0,3},{1,0},{2,1},{3,2},{4,7},{5,4},{6,5},{7,6},{8,11},{9,8},{10,9... | collective-permute-start | bytes 417800 | tf_op jit(solution)/shard_map/ppermute | solution.py:351
  7.9 2.1 %copy-start.6 = (bf16[64,4,768]{2,1,0:T(4,128)(2,1)S(1)}, bf16[64,4,768]{2,1,0:T(4,128)(2,1)}, u32[]{:S(2)}) copy-start(bf16[64,4,768]{2,1,0:T(4,128)(2,1)} %param.10) | copy-start | bytes 1179652
  7.9 2.2 %copy-start.1 = (bf16[4,768,512]{2,1,0:T(8,128)(2,1)S(1)}, bf16[4,768,512]{2,1,0:T(8,128)(2,1)}, u32[]{:S(2)}) copy-start(bf16[4,768,512]{2,1,0:T(8,128)(2,1)} %proj.1) | copy-start | bytes 9437188
  10.1 1.7 %copy-start = (s32[2]{0:T(128)S(1)}, s32[2]{0:T(128)}, u32[]{:S(2)}) copy-start(s32[2]{0:T(128)} %pad_add_fusion.idx) | copy-start | bytes 28
  10.1 1.7 %copy-start.5 = (s32[8,256]{1,0:T(8,128)S(1)}, s32[8,256]{1,0:T(8,128)}, u32[]{:S(2)}) copy-start(s32[8,256]{1,0:T(8,128)} %get-tuple-element.21.own) | copy-start | bytes 24580
  11.9 22.6 %copy-start.3 = (bf16[4,4,4,32,64]{4,3,2,1,0:T(8,128)(2,1)S(1)}, bf16[4,4,4,32,64]{4,3,2,1,0:T(8,128)(2,1)}, u32[]{:S(2)}) copy-start(bf16[4,4,4,32,64]{4,3,2,1,0:T(8,128)(2,1)} %dec.1) | copy-start | bytes 786436
  14.3 4.1 %collective-permute-start.2 = (bf16[112,512]{1,0:T(8,128)(2,1)S(1)}, bf16[112,512]{1,0:T(8,128)(2,1)S(1)}, u32[]{:S(2)}, u32[]{:S(2)}) collective-permute-start(bf16[112,512]{1,0:T(8,128)(2,1)S(1)} %get-tuple-element.30), channel_id=1, source_target_pairs={{0,4},{4,0},{8,12},{12,8},{16,20},{20,16},{24,28},{28,24},{32,36},... | collective-permute-start | bytes 344072 | tf_op jit(solution)/shard_map/ppermute | solution.py:360
  19.0 6.9 %collective-permute-start.3 = (bf16[576,256]{1,0:T(8,128)(2,1)S(1)}, bf16[576,256]{1,0:T(8,128)(2,1)S(1)}, u32[]{:S(2)}, u32[]{:S(2)}) collective-permute-start(bf16[576,256]{1,0:T(8,128)(2,1)S(1)} %get-tuple-element.33), channel_id=1, source_target_pairs={{0,252},{252,0},{8,4},{4,8},{16,12},{12,16},{24,20},{20,24},{32,28... | collective-permute-start | bytes 884744 | tf_op jit(solution)/shard_map/ppermute | solution.py:360
  19.2 6.6 %collective-permute-start.4 = (bf16[64,512]{1,0:T(8,128)(2,1)S(1)}, bf16[64,512]{1,0:T(8,128)(2,1)S(1)}, u32[]{:S(2)}, u32[]{:S(2)}) collective-permute-start(bf16[64,512]{1,0:T(8,128)(2,1)S(1)} %get-tuple-element.34), channel_id=1, source_target_pairs={{0,244},{244,0},{8,252},{252,8},{16,4},{4,16},{24,12},{12,24},{32,... | collective-permute-start | bytes 196616 | tf_op jit(solution)/shard_map/ppermute | solution.py:360
  26.5 9.1 %collective-permute-start.5 = (bf16[480,256]{1,0:T(8,128)(2,1)S(1)}, bf16[480,256]{1,0:T(8,128)(2,1)S(1)}, u32[]{:S(2)}, u32[]{:S(2)}) collective-permute-start(bf16[480,256]{1,0:T(8,128)(2,1)S(1)} %inward.1), channel_id=1, source_target_pairs={{0,4},{4,0},{8,12},{12,8},{16,20},{20,16},{24,28},{28,24},{32,36},... | collective-permute-start | bytes 737288 | tf_op jit(solution)/shard_map/ppermute | solution.py:360

commit v3 on v2

--- a/solution.py
+++ b/solution.py
@@ -44,8 +44,8 @@
     return (col == 2 * (row % XC) + row // XC).astype(BF)
 
 
-def edge_kernel(counts, block, tile, view, state, idx, up, down, own, lists, cs, pairs, planes, sems):
-    slab = idx[0]
+def edge_kernel(counts, block, tile, view, state, up, down, own, lists, cs, pairs, planes, some, sems):
+    slab = lax.axis_index("gz")
     at = pl.multiple_of((slab // 8) * 8, 8)
     copies = [pltpu.make_async_copy(counts, cs, sems.at[0])]
     for i, ref in enumerate((block, tile, view)):
@@ -82,9 +82,11 @@
     down[LIST:, :] = lists[...].astype(BF)
     for z in range(ZD):
         copies[4 + z].wait()
-        rows = dot(dot(pick, planes[z].reshape(C1 * YD, XD)).astype(BF), split).astype(BF)
-        down[z * 64 : z * 64 + 64, :] = rows[:64]
-        up[z * 64 : z * 64 + 64, :] = rows[64:]
+        some[z * 128 : (z + 1) * 128, :] = dot(pick, planes[z].reshape(C1 * YD, XD)).astype(BF)
+    rows = dot(some[...], split).astype(BF)
+    for z in range(ZD):
+        down[z * 64 : z * 64 + 64, :] = rows[z * 128 : z * 128 + 64]
+        up[z * 64 : z * 64 + 64, :] = rows[z * 128 + 64 : z * 128 + 128]
 
 
 def project_kernel(res, proj, high, low):
@@ -97,8 +99,8 @@
         low[r] = lo[r * NB : (r + 1) * NB]
 
 
-def place_kernel(own, left, right, high, low, we, idx, win, near, far, mate, fh, keys, x):
-    slab, part = idx[0], idx[1]
+def place_kernel(own, left, right, high, low, we, win, near, far, mate, fh, keys, x):
+    slab, part = lax.axis_index("gz"), lax.axis_index("gy")
     core = slab % 2
     keys[0:1, 0:KL] = own[0:1, :].astype(F32)
     keys[1:2, 0:KL] = own[1:2, :].astype(F32)
@@ -130,10 +132,8 @@
     a = (rkey == skey).astype(BF)
     bk = (iota((VIEWS * NB, 1), 0) == key).astype(BF)
     count = lax.dot_general(a, bk, (((1,), (1,)), ((), ())), preferred_element_type=F32)
-    acc = jnp.zeros((total, TILE), F32)
-    for q in range(4):
-        c = jnp.where(r == q, count, 0.0).astype(BF)
-        acc = acc + dot(c, high[q]) + dot(c, low[q])
+    each = jnp.concatenate([jnp.where(r == q, count, 0.0).astype(BF) for q in range(4)], axis=1)
+    acc = dot(each, high[...].reshape(4 * VIEWS * NB, TILE)) + dot(each, low[...].reshape(4 * VIEWS * NB, TILE))
     win[...] = acc[:120]
     near[...] = acc[120:240]
     mate[...] = acc[240:352].astype(BF)
@@ -184,7 +184,17 @@
         fs[a] = lax.dot_general(we[...], x[...], (((0,), (0,)), ((), ())), preferred_element_type=F32)
 
 
-def weights_kernel(dec, wdec):
+def prepare_kernel(dec, wdec, mats, small):
+    mats[0:XD, 0:XD] = split_columns()
+    mats[0:XD, XD : 2 * XD] = merge_columns()
+    row, col = iota((C1 * YD, C1 * YD), 0), iota((C1 * YD, C1 * YD), 1)
+    mats[XD:, :] = (col == (row % YD) * C1 + row // YD).astype(BF)
+    core = lax.axis_index("gz") % 2
+    row, col = iota((OWN, OWN), 0), iota((OWN, OWN), 1)
+    small[0] = ((col % ROWS == row % ROWS) & (col // ROWS == 7 - row // ROWS)).astype(BF)
+    z = row % 8
+    z = jnp.where(core == 0, z, 7 - z)
+    small[1] = ((col % ROWS == row // 8) & (col // ROWS == z)).astype(BF)
     wdec[...] = jnp.zeros_like(wdec)
     taps = (((0, 3), (1, 1)), ((1, 2), (2, 0)))
     for pz in range(2):
@@ -211,7 +221,7 @@
         pay[r0 : r0 + C2, (n % 2) * XC : (n % 2 + 1) * XC] = f.astype(BF)
 
 
-def out_kernel(near, far, got, fs, fh, idx, pay, pay_far, tmp):
+def out_kernel(near, far, got, fs, fh, pay, pay_far, tmp):
     tmp[0:CHIP] = near[...]
     tmp[CHIP:128] = jnp.zeros((8, TILE), F32)
     tmp[0:MATE] += got[...].astype(F32)[:MATE]
@@ -221,7 +231,7 @@
     tmp[0:64] = far[...]
     tmp[0 : 2 * ROWS] += got[...].astype(F32)[8 * ROWS : MATE]
     pay_far[...] = tmp[0:64].astype(BF)
-    put_plane(pay, 256, fs, fh, idx[0] % 2)
+    put_plane(pay, 256, fs, fh, lax.axis_index("gz") % 2)
 
 
 def window(win, near, far):
@@ -230,26 +240,21 @@
     return left, right, far[...].astype(F32)
 
 
-def mate_kernel(win, near, far, fs, fh, idx, pay, tmp):
+def mate_kernel(win, near, far, fs, fh, mats, pay, tmp):
     for q, half in enumerate(window(win, near, far)[:2]):
         tmp[...] = half
         tmp[0:64] += far[:, q * XD : (q + 1) * XD].astype(F32)
         pay[q * OWN : (q + 1) * OWN, :] = tmp[CHIP - OWN :, :].astype(BF)
-    put_plane(pay, 2 * OWN, fs, fh, 1 - idx[0] % 2)
-
-
-def decode_kernel(win, near, far, mate, fs, fh, planes, wdec, wb, idx, out, bp, x, ns, tmp):
-    slab, part = idx[0], idx[1]
+    put_plane(pay, 2 * OWN, fs, fh, 1 - lax.axis_index("gz") % 2)
+
+
+def decode_kernel(win, near, far, mate, fs, fh, planes, wdec, wb, mats, small, out, bp, x, ns, tmp, stage, sems):
+    slab, part = lax.axis_index("gz"), lax.axis_index("gy")
     core = slab % 2
-    split = split_columns()
-    merge = merge_columns()
-    row, col = iota((C1 * YD, C1 * YD), 0), iota((C1 * YD, C1 * YD), 1)
-    perm = (col == (row % YD) * C1 + row // YD).astype(BF)
-    row, col = iota((OWN, OWN), 0), iota((OWN, OWN), 1)
-    turn = ((col % ROWS == row % ROWS) & (col // ROWS == 7 - row // ROWS)).astype(BF)
-    z = row % 8
-    z = jnp.where(core == 0, z, 7 - z)
-    sort = ((col % ROWS == row // 8) & (col // ROWS == z)).astype(BF)
+    split = mats[0:XD, 0:XD]
+    merge = mats[0:XD, XD : 2 * XD]
+    perm = mats[XD:, :]
+    turn, sort = small[0], small[1]
     for q, half in enumerate(window(win, near, far)[:2]):
         tmp[...] = half
         tmp[0:64] += far[:, q * XD : (q + 1) * XD].astype(F32)
@@ -316,11 +321,13 @@
                     old = planes[f, y : y + C1, lanes].astype(F32)
                     ns[y : y + C1, lanes] = (old + d[r0 : r0 + C1, m * XC : (m + 1) * XC]).astype(BF)
         new = dot(dot(perm, ns[...]).astype(BF), merge).astype(BF)
-        out[:, f] = new.reshape(C1, YD, XD)
+        stage[f] = new.reshape(C1, YD, XD)
+        pltpu.make_async_copy(stage.at[f], out.at[:, f], sems.at[f]).start()
+    for f in range(ZD):
+        pltpu.make_async_copy(stage.at[f], out.at[:, f], sems.at[f]).wait()
 
 
 V = pltpu.VMEM
-SM = pl.BlockSpec(memory_space=pltpu.SMEM)
 VM = pl.BlockSpec(memory_space=pltpu.VMEM)
 ANY = pl.BlockSpec(memory_space=pl.ANY)
 
@@ -329,11 +336,11 @@
     return jax.ShapeDtypeStruct(dims, dtype)
 
 
-def call(kernel, ins, outs, scratch=(), cost=None, vlim=16 * MIB, **more):
+def call(kernel, ins, outs, scratch=(), cost=None, vlim=16 * MIB, outs_in=VM, **more):
     return pl.pallas_call(
         kernel,
         in_specs=ins,
-        out_specs=[VM] * len(outs) if "grid" not in more else more.pop("specs"),
+        out_specs=[outs_in] * len(outs) if "grid" not in more else more.pop("specs"),
         out_shape=outs,
         scratch_shapes=scratch,
         compiler_params=pltpu.CompilerParams(vmem_limit_bytes=vlim),
@@ -353,32 +360,34 @@
 
 def swapped(block, distance):
     n = lax.axis_size("gz")
-    route = []
-    for i in range(0, n, 2):
-        j = (i + distance) % n
-        route += [(i, j), (j, i)]
+    pairs = {(i, i + distance) for i in range(0, n, 2) if 0 <= i + distance < n}
+    if distance == -1:
+        pairs |= {(0, 0), (n - 1, n - 1)}
+    if distance == -3:
+        pairs |= {(0, 2), (n - 3, n - 1)}
+    route = sorted(pairs | {(j, i) for i, j in pairs})
     return lax.ppermute(block, "gz", route)
 
 
 def per_device(
     state, residual, projector, pair_counts, pair_block, pair_tile, pair_view, enc_weight, dec_weight
 ):
-    idx = jnp.stack([lax.axis_index("gz"), lax.axis_index("gy")]).astype(I32)
     up, down, own = call(
         edge_kernel,
-        [ANY] * 5 + [SM],
+        [ANY] * 5,
         [shape((272, XD)), shape((272, XD)), shape((8, KL), I32)],
         [
             V((16, KL), F32),
             pltpu.SMEM((SPAN, 1, 64), I32),
             V((3, 8, NPD), I32),
             V((ZD, C1, YD, XD), BF),
+            V((ZD * 128, XD), BF),
             pltpu.SemaphoreType.DMA((8,)),
         ],
         cost=cost(1.0),
         vlim=56 * MIB,
         name="edge",
-    )(jnp.transpose(pair_counts, (2, 0, 1)), pair_block, pair_tile, pair_view, state, idx)
+    )(jnp.transpose(pair_counts, (2, 0, 1)), pair_block, pair_tile, pair_view, state)
     left = shifted(up, "gy", 1)
     right = shifted(down, "gy", -1)
     rays = jnp.transpose(residual, (1, 0, 2))
@@ -409,7 +418,7 @@
     )(state, jnp.transpose(enc_weight, (0, 1, 4, 2, 3)))
     win, near, far, mate, fh = call(
         place_kernel,
-        [VM] * 6 + [SM],
+        [VM] * 6,
         [
             shape((CHIP, TILE), F32),
             shape((CHIP, TILE), F32),
@@ -420,39 +429,51 @@
         [V((8, 3 * KL), F32), V((8 * C1, 4 * XC), BF)],
         cost=cost(2.5),
         name="place",
-    )(own, left, right, high, low, we, idx)
+    )(own, left, right, high, low, we)
     got = swapped(mate, 1)
     pay, pay_far = call(
         out_kernel,
-        [VM] * 5 + [SM],
+        [VM] * 5,
         [shape((576, XD)), shape((64, TILE))],
         [V((128, TILE), F32)],
         cost=cost(0.4),
         name="outward",
-    )(near, far, got, fs, fh, idx)
+    )(near, far, got, fs, fh)
     got_near = swapped(pay, -1)
     got_far = swapped(pay_far, -3)
-    wdec = call(
-        weights_kernel, [VM], [shape((2, 128, 1152))], cost=cost(3.0), name="weights"
-    )(dec_weight)[0]
+    wdec, mats, small = call(
+        prepare_kernel,
+        [VM],
+        [shape((2, 128, 1152)), shape((XD + C1 * YD, 2 * XD)), shape((2, OWN, OWN))],
+        cost=cost(3.0),
+        name="prepare",
+    )(dec_weight)
     pay_mate = call(
         mate_kernel,
-        [VM] * 5 + [SM],
+        [VM] * 5 + [ANY],
         [shape((2 * OWN + 5 * C2, XD))],
         [V((CHIP, XD), F32)],
         cost=cost(0.4),
         name="inward",
-    )(win, got_near, got_far, fs, fh, idx)[0]
+    )(win, got_near, got_far, fs, fh, small)[0]
     got_mate = swapped(pay_mate, 1)
     return call(
         decode_kernel,
-        [VM] * 9 + [SM],
+        [VM] * 11,
         [shape((C1, ZD, YD, XD))],
-        [V((32, NL), F32), V((2304, 8 * XC), BF), V((C1 * YD, XD), BF), V((CHIP, XD), F32)],
+        [
+            V((32, NL), F32),
+            V((2304, 8 * XC), BF),
+            V((C1 * YD, XD), BF),
+            V((CHIP, XD), F32),
+            V((ZD, C1, YD, XD), BF),
+            pltpu.SemaphoreType.DMA((ZD,)),
+        ],
+        outs_in=ANY,
         cost=cost(6.0),
         vlim=24 * MIB,
         name="decode",
-    )(win, got_near, got_far, got_mate, fs, fh, planes, wdec, wb, idx)[0]
+    )(win, got_near, got_far, got_mate, fs, fh, planes, wdec, wb, mats, small)[0]
 
 
 def solution(mesh):

time: 42 us -> 35.6 us (0.85)
  the two profiles are of different devices: /device:TPU:1 before, /device:TPU:31 now
where the time goes in v3:
time: 35.6 us; the launch traced here: 35.3 us
  Pallas kernels  14.2 us (40%)
  starting transfers between devices  13.7 us (38%)
  waiting for transfers between devices  7.32 us (21%)
    ppermute x4, starting transfers between devices, swapped(): return lax.ppermute(block, 'gz', route)  12.1 us
    ppermute x4, waiting for transfers between devices, swapped(): return lax.ppermute(block, 'gz', route)  6.86 us
    pallas_call x1, Pallas kernels, per_device(): call(decode_kernel, [VM] * 11, [shape((C1, ZD, YD, XD))], [V((32, NL), F3...  5.36 us
    pallas_call x1, Pallas kernels, per_device(): call(edge_kernel, [ANY] * 5, [shape((272, XD)), shape((272, XD)), shape((...  2.86 us
    pallas_call x1, Pallas kernels, per_device(): call(encode_kernel, [VM] * 2, [shape((2, C2, 8 * XC), F32), shape((ZD, C1...  2.11 us
    pallas_call x1, Pallas kernels, per_device(): call(project_kernel, [pl.BlockSpec((4, NB, DC), lambda v: (0, 0, 0)), pl....  1.69 us
    ppermute x2, starting transfers between devices, shifted(): lax.ppermute(block, axis, [(i, (i + distance) % n) for i in range(n)])  1.54 us
    pallas_call x1, Pallas kernels, per_device(): call(place_kernel, [VM] * 6, [shape((CHIP, TILE), F32), shape((CHIP, TILE...  1.52 us
  transfers between devices with their start and end apart: 6, of which 4 were waited for; matrix products, arithmetic and copies ran while one was open for 0% of the time, Pallas kernels for 12%

profile of v3, /device:TPU:31, one launch (start us, length us, event | category | flops | bytes accessed | tf_op | source)
XLA Modules:
  0.0 35.3 jit_solution(6916612063422266815)
XLA Ops:
  0.0 0.0 copy-start.1
  0.0 0.0 copy-start.3
  0.0 2.9 %edge.1 = (bf16[272,256]{1,0:T(8,128)(2,1)}, bf16[272,256]{1,0:T(8,128)(2,1)}, s32[8,256]{1,0:T(8,128)}) custom-call(s32[7,1,64]{2,1,0:T(1,128)} %bitcast.7, s32[1,64,224]{2,1,0:T(8,128)} %block.1, s32[1,64,224]{2,1,0:T(8,128)} %tile.1, s32[1,64,224]{2,1,0:T(8,128)} %view.1, bf16[32,4,16,256]{3,2,1,0:T(8,128)(2,1)} %state.3), custom_call_target="tpu_custom_call" | custom-call | flops 1000000000 | bytes 3000000 | tf_op jit(solution)/shard_map/edge/pallas_call | solution.py:375
  2.9 0.3 collective-permute-start
  3.2 1.3 %collective-permute-start.1 = (bf16[272,256]{1,0:T(8,128)(2,1)}, bf16[272,256]{1,0:T(8,128)(2,1)S(1)}, u32[]{:S(2)}, u32[]{:S(2)}) collective-permute-start(bf16[272,256]{1,0:T(8,128)(2,1)} %get-tuple-element.26), channel_id=1, source_target_pairs={{0,3},{1,0},{2,1},{3,2},{4,7},{5,4},{6,5},{7,6},{8,11},{9,8},{10,9... | collective-permute-start | bytes 417800 | tf_op jit(solution)/shard_map/ppermute | solution.py:358
  4.4 0.0 copy-done.1
  4.4 0.0 copy-done.3
  4.4 0.0 copy-start.5
  4.4 0.0 copy-start
  4.4 2.1 %encode.1 = (f32[2,64,1024]{2,1,0:T(8,128)S(1)}, bf16[4,512,256]{2,1,0:T(8,128)(2,1)S(1)}, bf16[256,64]{1,0:T(8,128)(2,1)S(1)}, bf16[4,32,64]{2,1,0:T(8,128)(2,1)S(1)}) custom-call(bf16[32,4,16,256]{3,2,1,0:T(8,128)(2,1)S(1)} %copy-done.1, bf16[2,2,33,2,64]{4,3,2,1,0:T(2,128)(2,1)S(1)} %bitcast.6), custom_call_target="tpu_custom_call" | custom-call | flops 2000000000 | bytes 6000000 | tf_op jit(solution)/shard_map/encode/pallas_call | solution.py:406
  6.6 0.0 copy-done.5
  6.6 0.0 copy-done
  6.6 0.0 copy-start.4
  6.6 1.7 %project.1 = (bf16[4,256,512]{2,1,0:T(8,128)(2,1)S(1)}, bf16[4,256,512]{2,1,0:T(8,128)(2,1)S(1)}) custom-call(bf16[4,64,768]{2,1,0:T(8,128)(2,1)S(1)} %bitcast.5, bf16[4,768,512]{2,1,0:T(8,128)(2,1)S(1)} %copy-done), custom_call_target="tpu_custom_call" | custom-call | flops 2000000000 | bytes 6000000 | tf_op jit(solution)/shard_map/project/pallas_call | solution.py:394
  8.3 0.0 collective-permute-done.left
  8.3 0.5 %collective-permute-done.1.right = bf16[272,256]{1,0:T(8,128)(2,1)S(1)} collective-permute-done((bf16[272,256]{1,0:T(8,128)(2,1)}, bf16[272,256]{1,0:T(8,128)(2,1)S(1)}, u32[]{:S(2)}, u32[]{:S(2)}) %collective-permute-start.1) | collective-permute-done | bytes 139296 | tf_op jit(solution)/shard_map/ppermute | solution.py:358
  8.8 0.0 copy-done.4
  8.8 0.0 copy-start.2
  8.8 1.5 %place.1 = (f32[120,512]{1,0:T(8,128)S(1)}, f32[120,512]{1,0:T(8,128)S(1)}, f32[64,512]{1,0:T(8,128)S(1)}, bf16[112,512]{1,0:T(8,128)(2,1)S(1)}, f32[2,64,256]{2,1,0:T(8,128)S(1)}) custom-call(s32[8,256]{1,0:T(8,128)S(1)} %copy-done.4, bf16[272,256]{1,0:T(8,128)(2,1)S(1)} %collective-permute-done.left, bf16[272,256]{1,0:T(8,128)(2,1)S(1)} %collective-permute-done.1.right, ...), custom_call_target="tpu_custom_call" | custom-call | flops 2500000000 | bytes 7500000 | tf_op jit(solution)/shard_map/place/pallas_call | solution.py:419
  10.3 1.9 %collective-permute-start.2 = (bf16[112,512]{1,0:T(8,128)(2,1)S(1)}, bf16[112,512]{1,0:T(8,128)(2,1)S(1)}, u32[]{:S(2)}, u32[]{:S(2)}) collective-permute-start(bf16[112,512]{1,0:T(8,128)(2,1)S(1)} %get-tuple-element.33), channel_id=1, source_target_pairs={{0,4},{4,0},{8,12},{12,8},{16,20},{20,16},{24,28},{28,24},{32,36},... | collective-permute-start | bytes 344072 | tf_op jit(solution)/shard_map/ppermute | solution.py:369
  12.3 1.0 %collective-permute-done.2.got = bf16[112,512]{1,0:T(8,128)(2,1)S(1)} collective-permute-done((bf16[112,512]{1,0:T(8,128)(2,1)S(1)}, bf16[112,512]{1,0:T(8,128)(2,1)S(1)}, u32[]{:S(2)}, u32[]{:S(2)}) %collective-permute-start.2) | collective-permute-done | bytes 114720 | tf_op jit(solution)/shard_map/ppermute | solution.py:369
  13.2 0.1 outward.1
  13.3 3.8 %collective-permute-start.3 = (bf16[576,256]{1,0:T(8,128)(2,1)S(1)}, bf16[576,256]{1,0:T(8,128)(2,1)S(1)}, u32[]{:S(2)}, u32[]{:S(2)}) collective-permute-start(bf16[576,256]{1,0:T(8,128)(2,1)S(1)} %get-tuple-element.36), channel_id=1, source_target_pairs={{0,0},{4,8},{8,4},{12,16},{16,12},{20,24},{24,20},{28,32},{32,28},... | collective-permute-start | bytes 884744 | tf_op jit(solution)/shard_map/ppermute | solution.py:369
  17.1 1.5 %collective-permute-start.4 = (bf16[64,512]{1,0:T(8,128)(2,1)S(1)}, bf16[64,512]{1,0:T(8,128)(2,1)S(1)}, u32[]{:S(2)}, u32[]{:S(2)}) collective-permute-start(bf16[64,512]{1,0:T(8,128)(2,1)S(1)} %get-tuple-element.37), channel_id=1, source_target_pairs={{0,8},{4,16},{8,0},{12,24},{16,4},{20,32},{24,12},{28,40},{32,20},... | collective-permute-start | bytes 196616 | tf_op jit(solution)/shard_map/ppermute | solution.py:369
  18.5 0.0 copy-done.2
  18.5 0.5 %prepare.1 = (bf16[2,128,1152]{2,1,0:T(8,128)(2,1)S(1)}, bf16[768,512]{1,0:T(8,128)(2,1)S(1)}, bf16[2,80,80]{2,1,0:T(8,128)(2,1)S(1)}) custom-call(bf16[4,4,4,32,64]{4,3,2,1,0:T(8,128)(2,1)S(1)} %copy-done.2), custom_call_target="tpu_custom_call" | custom-call | flops 3000000000 | bytes 9000000 | tf_op jit(solution)/shard_map/prepare/pallas_call | solution.py:444
  19.1 4.8 %collective-permute-done.4.far = bf16[64,512]{1,0:T(8,128)(2,1)S(1)} collective-permute-done((bf16[64,512]{1,0:T(8,128)(2,1)S(1)}, bf16[64,512]{1,0:T(8,128)(2,1)S(1)}, u32[]{:S(2)}, u32[]{:S(2)}) %collective-permute-start.4) | collective-permute-done | bytes 65568 | tf_op jit(solution)/shard_map/ppermute | solution.py:369
  23.8 0.0 collective-permute-done.3.near
  23.9 4.9 %collective-permute-start.5 = (bf16[480,256]{1,0:T(8,128)(2,1)S(1)}, bf16[480,256]{1,0:T(8,128)(2,1)S(1)}, u32[]{:S(2)}, u32[]{:S(2)}) collective-permute-start(bf16[480,256]{1,0:T(8,128)(2,1)S(1)} %inward.1), channel_id=1, source_target_pairs={{0,4},{4,0},{8,12},{12,8},{16,20},{20,16},{24,28},{28,24},{32,36},... | collective-permute-start | bytes 737288 | tf_op jit(solution)/shard_map/ppermute | solution.py:369
  28.8 1.1 %collective-permute-done.5.mate = bf16[480,256]{1,0:T(8,128)(2,1)S(1)} collective-permute-done((bf16[480,256]{1,0:T(8,128)(2,1)S(1)}, bf16[480,256]{1,0:T(8,128)(2,1)S(1)}, u32[]{:S(2)}, u32[]{:S(2)}) %collective-permute-start.5) | collective-permute-done | bytes 245792 | tf_op jit(solution)/shard_map/ppermute | solution.py:369
  30.0 5.4 %decode.1 = bf16[32,4,16,256]{3,2,1,0:T(8,128)(2,1)} custom-call(f32[120,512]{1,0:T(8,128)S(1)} %get-tuple-element.30.win, bf16[576,256]{1,0:T(8,128)(2,1)S(1)} %collective-permute-done.3.near, bf16[64,512]{1,0:T(8,128)(2,1)S(1)} %collective-permute-done.4.far, bf16[480,256]{1,0:T(8,128)(2,1)S(1)} %collective-permute-done.5.mate, ...), custom_call_target="tpu_custom_call" | custom-call | flops 6000000000 | bytes 18000000 | tf_op jit(solution)/shard_map/decode/pallas_call | solution.py:460
  (2 shorter events, 0.1 us)
Async XLA Ops:
  0.0 4.4 %copy-start.1 = (bf16[32,4,16,256]{3,2,1,0:T(8,128)(2,1)S(1)}, bf16[32,4,16,256]{3,2,1,0:T(8,128)(2,1)}, u32[]{:S(2)}) copy-start(bf16[32,4,16,256]{3,2,1,0:T(8,128)(2,1)} %state.3) | copy-start | bytes 3145732
  0.0 4.4 %copy-start.3 = (bf16[2,2,2,64,33]{3,2,4,1,0:T(2,128)(2,1)S(1)}, bf16[2,2,2,64,33]{3,2,4,1,0:T(2,128)(2,1)}, u32[]{:S(2)}) copy-start(bf16[2,2,2,64,33]{3,2,4,1,0:T(2,128)(2,1)} %param.16) | copy-start | bytes 101380
  2.9 5.5 %collective-permute-start = (bf16[272,256]{1,0:T(8,128)(2,1)}, bf16[272,256]{1,0:T(8,128)(2,1)S(1)}, u32[]{:S(2)}, u32[]{:S(2)}) collective-permute-start(bf16[272,256]{1,0:T(8,128)(2,1)} %get-tuple-element.25), channel_id=1, source_target_pairs={{0,1},{1,2},{2,3},{3,0},{4,5},{5,6},{6,7},{7,4},{8,9},{9,10},{10,1... | collective-permute-start | bytes 417800 | tf_op jit(solution)/shard_map/ppermute | solution.py:358
  3.2 5.6 %collective-permute-start.1 = (bf16[272,256]{1,0:T(8,128)(2,1)}, bf16[272,256]{1,0:T(8,128)(2,1)S(1)}, u32[]{:S(2)}, u32[]{:S(2)}) collective-permute-start(bf16[272,256]{1,0:T(8,128)(2,1)} %get-tuple-element.26), channel_id=1, source_target_pairs={{0,3},{1,0},{2,1},{3,2},{4,7},{5,4},{6,5},{7,6},{8,11},{9,8},{10,9... | collective-permute-start | bytes 417800 | tf_op jit(solution)/shard_map/ppermute | solution.py:358
  4.4 2.1 %copy-start.5 = (bf16[64,4,768]{2,1,0:T(4,128)(2,1)S(1)}, bf16[64,4,768]{2,1,0:T(4,128)(2,1)}, u32[]{:S(2)}) copy-start(bf16[64,4,768]{2,1,0:T(4,128)(2,1)} %param.10) | copy-start | bytes 1179652
  4.4 2.2 %copy-start = (bf16[4,768,512]{2,1,0:T(8,128)(2,1)S(1)}, bf16[4,768,512]{2,1,0:T(8,128)(2,1)}, u32[]{:S(2)}) copy-start(bf16[4,768,512]{2,1,0:T(8,128)(2,1)} %proj.1) | copy-start | bytes 9437188
  6.6 2.2 %copy-start.4 = (s32[8,256]{1,0:T(8,128)S(1)}, s32[8,256]{1,0:T(8,128)}, u32[]{:S(2)}) copy-start(s32[8,256]{1,0:T(8,128)} %get-tuple-element.24.own) | copy-start | bytes 24580
  8.8 9.8 %copy-start.2 = (bf16[4,4,4,32,64]{4,3,2,1,0:T(8,128)(2,1)S(1)}, bf16[4,4,4,32,64]{4,3,2,1,0:T(8,128)(2,1)}, u32[]{:S(2)}) copy-start(bf16[4,4,4,32,64]{4,3,2,1,0:T(8,128)(2,1)} %dec.1) | copy-start | bytes 786436
  10.3 2.9 %collective-permute-start.2 = (bf16[112,512]{1,0:T(8,128)(2,1)S(1)}, bf16[112,512]{1,0:T(8,128)(2,1)S(1)}, u32[]{:S(2)}, u32[]{:S(2)}) collective-permute-start(bf16[112,512]{1,0:T(8,128)(2,1)S(1)} %get-tuple-element.33), channel_id=1, source_target_pairs={{0,4},{4,0},{8,12},{12,8},{16,20},{20,16},{24,28},{28,24},{32,36},... | collective-permute-start | bytes 344072 | tf_op jit(solution)/shard_map/ppermute | solution.py:369
  13.3 10.5 %collective-permute-start.3 = (bf16[576,256]{1,0:T(8,128)(2,1)S(1)}, bf16[576,256]{1,0:T(8,128)(2,1)S(1)}, u32[]{:S(2)}, u32[]{:S(2)}) collective-permute-start(bf16[576,256]{1,0:T(8,128)(2,1)S(1)} %get-tuple-element.36), channel_id=1, source_target_pairs={{0,0},{4,8},{8,4},{12,16},{16,12},{20,24},{24,20},{28,32},{32,28},... | collective-permute-start | bytes 884744 | tf_op jit(solution)/shard_map/ppermute | solution.py:369
  17.1 6.7 %collective-permute-start.4 = (bf16[64,512]{1,0:T(8,128)(2,1)S(1)}, bf16[64,512]{1,0:T(8,128)(2,1)S(1)}, u32[]{:S(2)}, u32[]{:S(2)}) collective-permute-start(bf16[64,512]{1,0:T(8,128)(2,1)S(1)} %get-tuple-element.37), channel_id=1, source_target_pairs={{0,8},{4,16},{8,0},{12,24},{16,4},{20,32},{24,12},{28,40},{32,20},... | collective-permute-start | bytes 196616 | tf_op jit(solution)/shard_map/ppermute | solution.py:369
  23.9 6.1 %collective-permute-start.5 = (bf16[480,256]{1,0:T(8,128)(2,1)S(1)}, bf16[480,256]{1,0:T(8,128)(2,1)S(1)}, u32[]{:S(2)}, u32[]{:S(2)}) collective-permute-start(bf16[480,256]{1,0:T(8,128)(2,1)S(1)} %inward.1), channel_id=1, source_target_pairs={{0,4},{4,0},{8,12},{12,8},{16,20},{20,16},{24,28},{28,24},{32,36},... | collective-permute-start | bytes 737288 | tf_op jit(solution)/shard_map/ppermute | solution.py:369

commit v4 on v3

--- a/solution.py
+++ b/solution.py
@@ -1,3 +1,5 @@
+import functools
+
 import jax
 import jax.numpy as jnp
 from jax import lax
@@ -89,9 +91,8 @@
         up[z * 64 : z * 64 + 64, :] = rows[z * 128 + 64 : z * 128 + 128]
 
 
-def project_kernel(res, proj, high, low):
-    rays = res[...].reshape(4 * NB, DC)
-    y = dot(rays, proj[0])
+def project_kernel(res, proj, flat, high, low):
+    y = dot(res[...].reshape(4 * NB, DC), proj[0])
     hi = y.astype(BF)
     lo = (y - hi.astype(F32)).astype(BF)
     for r in range(4):
@@ -99,7 +100,13 @@
         low[r] = lo[r * NB : (r + 1) * NB]
 
 
-def place_kernel(own, left, right, high, low, we, win, near, far, mate, fh, keys, x):
+def flat_kernel(state, flat):
+    split = split_columns()
+    for z in range(ZD):
+        flat[z] = dot(state[:, z].reshape(C1 * YD, XD), split).astype(BF)
+
+
+def place_kernel(own, left, right, high, low, small, win, near, far, mate, keys):
     slab, part = lax.axis_index("gz"), lax.axis_index("gy")
     core = slab % 2
     keys[0:1, 0:KL] = own[0:1, :].astype(F32)
@@ -138,24 +145,9 @@
     near[...] = acc[120:240]
     mate[...] = acc[240:352].astype(BF)
     far[...] = acc[352:]
-    for a in range(2):
-        for p in range(2):
-            for q in range(2):
-                for s in range(2):
-                    k = (p * 4 + q * 2 + s) * C1
-                    lanes = slice(s * XC, (s + 1) * XC)
-                    h = (2 * a + p) * 64 + q * C1
-                    x[k : k + C1, 2 * a * XC : (2 * a + 1) * XC] = left[h : h + C1, lanes]
-                    x[k : k + C1, (2 * a + 1) * XC : (2 * a + 2) * XC] = right[h : h + C1, lanes]
-    f = lax.dot_general(we[...], x[...], (((0,), (0,)), ((), ())), preferred_element_type=F32)
-    fh[0] = f[:, :XD]
-    fh[1] = f[:, XD:]
-
-
-def encode_kernel(state, enc, fs, planes, we, wb, x):
-    split = split_columns()
-    row, col = iota((C1 * YD, C1 * YD), 0), iota((C1 * YD, C1 * YD), 1)
-    perm = (col == (row % C1) * YD + row // C1).astype(BF)
+
+
+def encode_kernel(flat, left, right, enc, fs, out, keep, wb, we, x, wide):
     rows = iota((32, C2), 0)
     bias = [jnp.zeros((32, C2), F32) for _ in range(4)]
     for p in range(2):
@@ -169,26 +161,37 @@
                     bias[a] = bias[a] + jnp.where(rows == (q * 2 + s) * 8 + 2 * a + p, es[C1 : C1 + 1], 0.0)
     for a in range(4):
         wb[a] = bias[a].astype(BF)
+    for z in range(ZD):
+        for s in range(2):
+            wide[z * 2 + s] = flat[z, :, s * XC : (s + 1) * XC].astype(F32)
     for a in range(2):
         for p in range(2):
             z = 2 * a + p
-            plane = state[:, z].reshape(C1 * YD, XD)
-            d = dot(dot(perm, plane).astype(BF), split).astype(BF)
-            planes[z] = d
             for q in range(2):
                 for s in range(2):
                     k = (p * 4 + q * 2 + s) * C1
+                    lanes = slice(s * XC, (s + 1) * XC)
+                    h = z * 64 + q * C1
+                    x[k : k + C1, 0:XC] = left[h : h + C1, lanes]
+                    x[k : k + C1, 9 * XC : 10 * XC] = right[h : h + C1, lanes]
                     for b in range(8):
-                        y = (2 * b + q) * C1
-                        x[k : k + C1, b * XC : (b + 1) * XC] = d[y : y + C1, s * XC : (s + 1) * XC]
-        fs[a] = lax.dot_general(we[...], x[...], (((0,), (0,)), ((), ())), preferred_element_type=F32)
+                        y = wide[z * 2 + s, pl.ds(2 * b + q, C1, stride=YD), :]
+                        x[k : k + C1, (b + 1) * XC : (b + 2) * XC] = y.astype(BF)
+        f = lax.dot_general(we[...], x[...], (((0,), (0,)), ((), ())), preferred_element_type=F32)
+        fs[a] = f
+
+        def put(ref, f=f):
+            for t in range(5):
+                ref[t * C2 : (t + 1) * C2, :] = f[:, t * XD : (t + 1) * XD].astype(BF)
+
+        mine = lax.axis_index("gz") % 2 == a
+        pl.when(mine)(functools.partial(put, out))
+        pl.when(jnp.logical_not(mine))(functools.partial(put, keep))
 
 
 def prepare_kernel(dec, wdec, mats, small):
     mats[0:XD, 0:XD] = split_columns()
     mats[0:XD, XD : 2 * XD] = merge_columns()
-    row, col = iota((C1 * YD, C1 * YD), 0), iota((C1 * YD, C1 * YD), 1)
-    mats[XD:, :] = (col == (row % YD) * C1 + row // YD).astype(BF)
     core = lax.axis_index("gz") % 2
     row, col = iota((OWN, OWN), 0), iota((OWN, OWN), 1)
     small[0] = ((col % ROWS == row % ROWS) & (col // ROWS == 7 - row // ROWS)).astype(BF)
@@ -209,56 +212,43 @@
                             wdec[pz, r0 : r0 + C1, c0 : c0 + C2] = dec[kz, ky, kx]
 
 
-def put_plane(pay, start, fs, fh, plane):
-    for n in range(ROWS):
-        if n == 0:
-            f = fh[plane, :, :XC]
-        elif n == 9:
-            f = fh[plane, :, XC:]
-        else:
-            f = fs[plane, :, (n - 1) * XC : n * XC]
-        r0 = start + (n // 2) * C2
-        pay[r0 : r0 + C2, (n % 2) * XC : (n % 2 + 1) * XC] = f.astype(BF)
-
-
-def out_kernel(near, far, got, fs, fh, pay, pay_far, tmp):
+def out_kernel(near, far, got, pre, pay, pay_far, tmp):
     tmp[0:CHIP] = near[...]
     tmp[CHIP:128] = jnp.zeros((8, TILE), F32)
     tmp[0:MATE] += got[...].astype(F32)[:MATE]
     total = tmp[...].astype(BF)
     pay[0:128, :] = total[:, :XD]
     pay[128:256, :] = total[:, XD:]
+    pay[256:, :] = pre[...]
     tmp[0:64] = far[...]
     tmp[0 : 2 * ROWS] += got[...].astype(F32)[8 * ROWS : MATE]
     pay_far[...] = tmp[0:64].astype(BF)
-    put_plane(pay, 256, fs, fh, lax.axis_index("gz") % 2)
-
-
-def window(win, near, far):
-    left = win[:, :XD] + near[0:128, :].astype(F32)[:CHIP]
-    right = win[:, XD:] + near[128:256, :].astype(F32)[:CHIP]
-    return left, right, far[...].astype(F32)
-
-
-def mate_kernel(win, near, far, fs, fh, mats, pay, tmp):
-    for q, half in enumerate(window(win, near, far)[:2]):
-        tmp[...] = half
-        tmp[0:64] += far[:, q * XD : (q + 1) * XD].astype(F32)
-        pay[q * OWN : (q + 1) * OWN, :] = tmp[CHIP - OWN :, :].astype(BF)
-    put_plane(pay, 2 * OWN, fs, fh, 1 - lax.axis_index("gz") % 2)
-
-
-def decode_kernel(win, near, far, mate, fs, fh, planes, wdec, wb, mats, small, out, bp, x, ns, tmp, stage, sems):
+
+
+def add_near(tmp, win, near):
+    tmp[:, :XD] = win[:, :XD] + near[0:128, :].astype(F32)[:CHIP]
+    tmp[:, XD:] = win[:, XD:] + near[128:256, :].astype(F32)[:CHIP]
+
+
+def mate_kernel(win, near, far, pre, pay, tmp):
+    add_near(tmp, win, near)
+    tmp[0:64] += far[...].astype(F32)
+    total = tmp[CHIP - OWN :, :].astype(BF)
+    pay[0:OWN, :] = total[:, :XD]
+    pay[OWN : 2 * OWN, :] = total[:, XD:]
+    pay[2 * OWN :, :] = pre[...]
+
+
+def decode_kernel(win, near, far, mate, fs, flat, wdec, wb, mats, small, out, bp, x, ns, tmp, stage, sems):
     slab, part = lax.axis_index("gz"), lax.axis_index("gy")
     core = slab % 2
     split = mats[0:XD, 0:XD]
     merge = mats[0:XD, XD : 2 * XD]
-    perm = mats[XD:, :]
     turn, sort = small[0], small[1]
-    for q, half in enumerate(window(win, near, far)[:2]):
-        tmp[...] = half
-        tmp[0:64] += far[:, q * XD : (q + 1) * XD].astype(F32)
-        t = tmp[0:OWN] + dot(turn, mate[q * OWN : (q + 1) * OWN, :])
+    add_near(tmp, win, near)
+    tmp[0:64] += far[...].astype(F32)
+    for q in range(2):
+        t = tmp[0:OWN, q * XD : (q + 1) * XD] + dot(turn, mate[q * OWN : (q + 1) * OWN, :])
         t = dot(dot(sort, t.astype(BF)).astype(BF), split)
         for s in range(2):
             for n in range(ROWS):
@@ -277,12 +267,7 @@
         for n in range(ROWS):
             lanes = slice(n * XC, (n + 1) * XC)
             if a in (1, 2):
-                if n == 0:
-                    v = fh[a - 1, :, :XC]
-                elif n == 9:
-                    v = fh[a - 1, :, XC:]
-                else:
-                    v = fs[a - 1, :, (n - 1) * XC : n * XC]
+                v = fs[a - 1, :, lanes]
             else:
                 half = slice((n % 2) * XC, (n % 2 + 1) * XC)
                 r0 = (n // 2) * C2
@@ -315,12 +300,10 @@
         for py in range(2):
             for px in range(2):
                 r0 = (py * 2 + px) * C1
-                lanes = slice(px * XC, (px + 1) * XC)
                 for m in range(8):
-                    y = (2 * m + py) * C1
-                    old = planes[f, y : y + C1, lanes].astype(F32)
-                    ns[y : y + C1, lanes] = (old + d[r0 : r0 + C1, m * XC : (m + 1) * XC]).astype(BF)
-        new = dot(dot(perm, ns[...]).astype(BF), merge).astype(BF)
+                    ns[px, pl.ds(2 * m + py, C1, stride=YD), :] = d[r0 : r0 + C1, m * XC : (m + 1) * XC]
+        both = jnp.concatenate([ns[0], ns[1]], axis=1)
+        new = dot((flat[f].astype(F32) + both).astype(BF), merge).astype(BF)
         stage[f] = new.reshape(C1, YD, XD)
         pltpu.make_async_copy(stage.at[f], out.at[:, f], sems.at[f]).start()
     for f in range(ZD):
@@ -359,14 +342,14 @@
 
 
 def swapped(block, distance):
-    n = lax.axis_size("gz")
+    n, m = lax.axis_size("gz"), lax.axis_size("gy")
     pairs = {(i, i + distance) for i in range(0, n, 2) if 0 <= i + distance < n}
-    if distance == -1:
-        pairs |= {(0, 0), (n - 1, n - 1)}
     if distance == -3:
         pairs |= {(0, 2), (n - 3, n - 1)}
-    route = sorted(pairs | {(j, i) for i, j in pairs})
-    return lax.ppermute(block, "gz", route)
+    pairs = {(i * m + k, j * m + k) for i, j in pairs for k in range(m)}
+    if distance == -1:
+        pairs |= {(i * m + k, i * m + k + 1) for i in (0, n - 1) for k in range(0, m, 2)}
+    return lax.ppermute(block, ("gz", "gy"), sorted(pairs | {(j, i) for i, j in pairs}))
 
 
 def per_device(
@@ -384,96 +367,92 @@
             V((ZD * 128, XD), BF),
             pltpu.SemaphoreType.DMA((8,)),
         ],
-        cost=cost(1.0),
+        cost=cost(2.9),
         vlim=56 * MIB,
         name="edge",
     )(jnp.transpose(pair_counts, (2, 0, 1)), pair_block, pair_tile, pair_view, state)
     left = shifted(up, "gy", 1)
     right = shifted(down, "gy", -1)
+    flat = call(flat_kernel, [VM], [shape((ZD, C1 * YD, XD))], cost=cost(0.4), name="flat")(state)[0]
     rays = jnp.transpose(residual, (1, 0, 2))
     high, low = call(
         project_kernel,
         [
             pl.BlockSpec((4, NB, DC), lambda v: (0, 0, 0)),
             pl.BlockSpec((1, DC, TILE), lambda v: (v, 0, 0)),
+            ANY,
         ],
         [shape((4, VIEWS * NB, TILE)), shape((4, VIEWS * NB, TILE))],
-        cost=cost(2.0),
+        cost=cost(1.7),
         grid=(VIEWS,),
         specs=[pl.BlockSpec((4, NB, TILE), lambda v: (0, v, 0))] * 2,
         name="project",
-    )(rays, projector)
-    fs, planes, we, wb = call(
-        encode_kernel,
-        [VM] * 2,
-        [
-            shape((2, C2, 8 * XC), F32),
-            shape((ZD, C1 * YD, XD)),
-            shape((8 * C1, C2)),
-            shape((4, 32, C2)),
-        ],
-        [V((8 * C1, 8 * XC), BF)],
-        cost=cost(2.0),
-        name="encode",
-    )(state, jnp.transpose(enc_weight, (0, 1, 4, 2, 3)))
-    win, near, far, mate, fh = call(
+    )(rays, projector, flat)
+    wdec, mats, small = call(
+        prepare_kernel,
+        [VM],
+        [shape((2, 128, 1152)), shape((XD, 2 * XD)), shape((2, OWN, OWN))],
+        cost=cost(0.3),
+        name="prepare",
+    )(dec_weight)
+    win, near, far, mate = call(
         place_kernel,
-        [VM] * 6,
+        [VM] * 5 + [ANY],
         [
             shape((CHIP, TILE), F32),
             shape((CHIP, TILE), F32),
             shape((64, TILE), F32),
             shape((112, TILE)),
-            shape((2, C2, XD), F32),
         ],
-        [V((8, 3 * KL), F32), V((8 * C1, 4 * XC), BF)],
-        cost=cost(2.5),
+        [V((8, 3 * KL), F32)],
+        cost=cost(1.5),
         name="place",
-    )(own, left, right, high, low, we)
+    )(own, left, right, high, low, small)
     got = swapped(mate, 1)
+    fs, pre_out, pre_mate, wb = call(
+        encode_kernel,
+        [VM] * 4,
+        [shape((2, C2, NL), F32), shape((5 * C2, XD)), shape((5 * C2, XD)), shape((4, 32, C2))],
+        [V((8 * C1, C2), BF), V((8 * C1, NL), BF), V((2 * ZD, C1 * YD, XC), F32)],
+        cost=cost(1.5),
+        name="encode",
+    )(flat, left, right, jnp.transpose(enc_weight, (0, 1, 4, 2, 3)))
     pay, pay_far = call(
         out_kernel,
-        [VM] * 5,
+        [VM] * 4,
         [shape((576, XD)), shape((64, TILE))],
         [V((128, TILE), F32)],
-        cost=cost(0.4),
+        cost=cost(0.1),
         name="outward",
-    )(near, far, got, fs, fh)
+    )(near, far, got, pre_out)
     got_near = swapped(pay, -1)
     got_far = swapped(pay_far, -3)
-    wdec, mats, small = call(
-        prepare_kernel,
-        [VM],
-        [shape((2, 128, 1152)), shape((XD + C1 * YD, 2 * XD)), shape((2, OWN, OWN))],
-        cost=cost(3.0),
-        name="prepare",
-    )(dec_weight)
     pay_mate = call(
         mate_kernel,
-        [VM] * 5 + [ANY],
+        [VM] * 4,
         [shape((2 * OWN + 5 * C2, XD))],
-        [V((CHIP, XD), F32)],
-        cost=cost(0.4),
+        [V((CHIP, TILE), F32)],
+        cost=cost(0.1),
         name="inward",
-    )(win, got_near, got_far, fs, fh, small)[0]
+    )(win, got_near, got_far, pre_mate)[0]
     got_mate = swapped(pay_mate, 1)
     return call(
         decode_kernel,
-        [VM] * 11,
+        [VM] * 10,
         [shape((C1, ZD, YD, XD))],
         [
             V((32, NL), F32),
             V((2304, 8 * XC), BF),
-            V((C1 * YD, XD), BF),
-            V((CHIP, XD), F32),
+            V((2, C1 * YD, XC), F32),
+            V((CHIP, TILE), F32),
             V((ZD, C1, YD, XD), BF),
             pltpu.SemaphoreType.DMA((ZD,)),
         ],
         outs_in=ANY,
-        cost=cost(6.0),
+        cost=cost(5.0),
         vlim=24 * MIB,
         name="decode",
-    )(win, got_near, got_far, got_mate, fs, fh, planes, wdec, wb, mats, small)[0]
+    )(win, got_near, got_far, got_mate, fs, flat, wdec, wb, mats, small)[0]
 
 
 def solution(mesh):

time: 35.6 us -> 33.6 us (0.944)
  starting transfers between devices: 13.7 us -> 11.6 us
  waiting for transfers between devices: 7.32 us -> 8.38 us
  Pallas kernels: 14.2 us -> 13.4 us
    ppermute x4, starting transfers between devices: 12.1 us -> 10.1 us  [swapped(): lax.ppermute(block, ('gz', 'gy'), sorted(pairs | {(j, i) for i, j in pair...]
    ppermute x2, waiting for transfers between devices: 0.46 us -> 1.83 us  [shifted(): lax.ppermute(block, axis, [(i, (i + distance) % n) for i in range(n)])]
    pallas_call x6 -> x7, Pallas kernels: 9.63 us -> 8.76 us  [the longest x1 4.92 us: per_device(): call(decode_kernel, [VM] * 10, [shape((C1, ZD, YD, XD))], [V((32, NL), F3...]
where the time goes in v4:
time: 33.6 us; the launch traced here: 33.5 us
  Pallas kernels  13.4 us (40%)
  starting transfers between devices  11.6 us (35%)
  waiting for transfers between devices  8.38 us (25%)
    ppermute x4, starting transfers between devices, swapped(): lax.ppermute(block, ('gz', 'gy'), sorted(pairs | {(j, i) for i, j in pair...  10.1 us
    ppermute x4, waiting for transfers between devices, swapped(): lax.ppermute(block, ('gz', 'gy'), sorted(pairs | {(j, i) for i, j in pair...  6.54 us
    pallas_call x1, Pallas kernels, per_device(): call(decode_kernel, [VM] * 10, [shape((C1, ZD, YD, XD))], [V((32, NL), F3...  4.92 us
    pallas_call x1, Pallas kernels, per_device(): call(edge_kernel, [ANY] * 5, [shape((272, XD)), shape((272, XD)), shape((...  2.91 us
    ppermute x2, waiting for transfers between devices, shifted(): lax.ppermute(block, axis, [(i, (i + distance) % n) for i in range(n)])  1.83 us
    pallas_call x1, Pallas kernels, per_device(): call(project_kernel, [pl.BlockSpec((4, NB, DC), lambda v: (0, 0, 0)), pl....  1.69 us
    ppermute x2, starting transfers between devices, shifted(): lax.ppermute(block, axis, [(i, (i + distance) % n) for i in range(n)])  1.54 us
    pallas_call x1, Pallas kernels, per_device(): call(place_kernel, [VM] * 5 + [ANY], [shape((CHIP, TILE), F32), shape((CH...  1.52 us
  transfers between devices with their start and end apart: 6, of which 4 were waited for; matrix products, arithmetic and copies ran while one was open for 0% of the time, Pallas kernels for 12%

profile of v4, /device:TPU:31, one launch (start us, length us, event | category | flops | bytes accessed | tf_op | source)
XLA Modules:
  0.0 33.5 jit_solution(12306149617898759062)
XLA Ops:
  0.0 0.0 copy-start
  0.0 0.0 copy-start.5
  0.0 0.0 copy-start.2
  0.0 2.9 %edge.1 = (bf16[272,256]{1,0:T(8,128)(2,1)}, bf16[272,256]{1,0:T(8,128)(2,1)}, s32[8,256]{1,0:T(8,128)}) custom-call(s32[7,1,64]{2,1,0:T(1,128)} %bitcast.7, s32[1,64,224]{2,1,0:T(8,128)} %block.1, s32[1,64,224]{2,1,0:T(8,128)} %tile.1, s32[1,64,224]{2,1,0:T(8,128)} %view.1, bf16[32,4,16,256]{3,2,1,0:T(8,128)(2,1)} %state.3), custom_call_target="tpu_custom_call" | custom-call | flops 2900000000 | bytes 8700000 | tf_op jit(solution)/shard_map/edge/pallas_call | solution.py:358
  2.9 0.0 copy-start.1
  2.9 0.3 collective-permute-start
  3.2 1.3 %collective-permute-start.1 = (bf16[272,256]{1,0:T(8,128)(2,1)}, bf16[272,256]{1,0:T(8,128)(2,1)S(1)}, u32[]{:S(2)}, u32[]{:S(2)}) collective-permute-start(bf16[272,256]{1,0:T(8,128)(2,1)} %get-tuple-element.25), channel_id=1, source_target_pairs={{0,3},{1,0},{2,1},{3,2},{4,7},{5,4},{6,5},{7,6},{8,11},{9,8},{10,9... | collective-permute-start | bytes 417800 | tf_op jit(solution)/shard_map/ppermute | solution.py:341
  4.5 0.0 copy-done
  4.5 0.4 %flat.1 = bf16[4,512,256]{2,1,0:T(8,128)(2,1)S(1)} custom-call(bf16[32,4,16,256]{3,2,1,0:T(8,128)(2,1)S(1)} %copy-done), custom_call_target="tpu_custom_call" | custom-call | flops 400000000 | bytes 1200000 | tf_op jit(solution)/shard_map/flat/pallas_call | solution.py:376
  4.9 0.0 copy-done.5
  5.0 0.0 copy-done.2
  5.0 0.3 prepare.1
  5.3 0.0 copy-done.1
  5.3 0.0 copy-start.4
  5.3 1.7 %project.1 = (bf16[4,256,512]{2,1,0:T(8,128)(2,1)S(1)}, bf16[4,256,512]{2,1,0:T(8,128)(2,1)S(1)}) custom-call(bf16[4,64,768]{2,1,0:T(8,128)(2,1)S(1)} %bitcast.5, bf16[4,768,512]{2,1,0:T(8,128)(2,1)S(1)} %copy-done.1, bf16[4,512,256]{2,1,0:T(8,128)(2,1)S(1)} %flat.1), custom_call_target="tpu_custom_call" | custom-call | flops 1700000000 | bytes 5100000 | tf_op jit(solution)/shard_map/project/pallas_call | solution.py:378
  7.0 0.0 copy-start.3
  7.0 0.7 %collective-permute-done.left = bf16[272,256]{1,0:T(8,128)(2,1)S(1)} collective-permute-done((bf16[272,256]{1,0:T(8,128)(2,1)}, bf16[272,256]{1,0:T(8,128)(2,1)S(1)}, u32[]{:S(2)}, u32[]{:S(2)}) %collective-permute-start) | collective-permute-done | bytes 139296 | tf_op jit(solution)/shard_map/ppermute | solution.py:341
  7.8 1.1 %collective-permute-done.1.right = bf16[272,256]{1,0:T(8,128)(2,1)S(1)} collective-permute-done((bf16[272,256]{1,0:T(8,128)(2,1)}, bf16[272,256]{1,0:T(8,128)(2,1)S(1)}, u32[]{:S(2)}, u32[]{:S(2)}) %collective-permute-start.1) | collective-permute-done | bytes 139296 | tf_op jit(solution)/shard_map/ppermute | solution.py:341
  8.9 0.0 copy-done.4
  8.9 1.5 %place.1 = (f32[120,512]{1,0:T(8,128)S(1)}, f32[120,512]{1,0:T(8,128)S(1)}, f32[64,512]{1,0:T(8,128)S(1)}, bf16[112,512]{1,0:T(8,128)(2,1)S(1)}) custom-call(s32[8,256]{1,0:T(8,128)S(1)} %copy-done.4, bf16[272,256]{1,0:T(8,128)(2,1)S(1)} %collective-permute-done.left, bf16[272,256]{1,0:T(8,128)(2,1)S(1)} %collective-permute-done.1.right, ...), custom_call_target="tpu_custom_call" | custom-call | flops 1500000000 | bytes 4500000 | tf_op jit(solution)/shard_map/place/pallas_call | solution.py:398
  10.4 1.9 %collective-permute-start.2 = (bf16[112,512]{1,0:T(8,128)(2,1)S(1)}, bf16[112,512]{1,0:T(8,128)(2,1)S(1)}, u32[]{:S(2)}, u32[]{:S(2)}) collective-permute-start(bf16[112,512]{1,0:T(8,128)(2,1)S(1)} %get-tuple-element.32), channel_id=1, source_target_pairs={{0,4},{1,5},{2,6},{3,7},{4,0},{5,1},{6,2},{7,3},{8,12},{9,13},{10,... | collective-permute-start | bytes 344072 | tf_op jit(solution)/shard_map/ppermute | solution.py:352
  12.3 0.0 copy-done.3
  12.3 1.5 %encode.1 = (f32[2,64,1280]{2,1,0:T(8,128)S(1)}, bf16[320,256]{1,0:T(8,128)(2,1)S(1)}, bf16[320,256]{1,0:T(8,128)(2,1)S(1)}, bf16[4,32,64]{2,1,0:T(8,128)(2,1)S(1)}) custom-call(bf16[4,512,256]{2,1,0:T(8,128)(2,1)S(1)} %flat.1, bf16[272,256]{1,0:T(8,128)(2,1)S(1)} %collective-permute-done.left, bf16[272,256]{1,0:T(8,128)(2,1)S(1)} %collective-permute-done.1.right, ...), custom_call_target="tpu_custom_call" | custom-call | flops 1500000000 | bytes 4500000 | tf_op jit(solution)/shard_map/encode/pallas_call | solution.py:412
  13.9 0.0 collective-permute-done.2.got
  13.9 0.1 outward.1
  13.9 1.6 %collective-permute-start.3 = (bf16[576,256]{1,0:T(8,128)(2,1)S(1)}, bf16[576,256]{1,0:T(8,128)(2,1)S(1)}, u32[]{:S(2)}, u32[]{:S(2)}) collective-permute-start(bf16[576,256]{1,0:T(8,128)(2,1)S(1)} %get-tuple-element.34), channel_id=1, source_target_pairs={{0,1},{1,0},{2,3},{3,2},{4,8},{5,9},{6,10},{7,11},{8,4},{9,5},{10,... | collective-permute-start | bytes 884744 | tf_op jit(solution)/shard_map/ppermute | solution.py:352
  15.6 1.6 %collective-permute-start.4 = (bf16[64,512]{1,0:T(8,128)(2,1)S(1)}, bf16[64,512]{1,0:T(8,128)(2,1)S(1)}, u32[]{:S(2)}, u32[]{:S(2)}) collective-permute-start(bf16[64,512]{1,0:T(8,128)(2,1)S(1)} %get-tuple-element.35), channel_id=1, source_target_pairs={{0,8},{1,9},{2,10},{3,11},{4,16},{5,17},{6,18},{7,19},{8,0},{9,1},... | collective-permute-start | bytes 196616 | tf_op jit(solution)/shard_map/ppermute | solution.py:352
  17.1 5.4 %collective-permute-done.4.far = bf16[64,512]{1,0:T(8,128)(2,1)S(1)} collective-permute-done((bf16[64,512]{1,0:T(8,128)(2,1)S(1)}, bf16[64,512]{1,0:T(8,128)(2,1)S(1)}, u32[]{:S(2)}, u32[]{:S(2)}) %collective-permute-start.4) | collective-permute-done | bytes 65568 | tf_op jit(solution)/shard_map/ppermute | solution.py:352
  22.5 0.0 collective-permute-done.3.near
  22.6 4.9 %collective-permute-start.5 = (bf16[480,256]{1,0:T(8,128)(2,1)S(1)}, bf16[480,256]{1,0:T(8,128)(2,1)S(1)}, u32[]{:S(2)}, u32[]{:S(2)}) collective-permute-start(bf16[480,256]{1,0:T(8,128)(2,1)S(1)} %inward.1), channel_id=1, source_target_pairs={{0,4},{1,5},{2,6},{3,7},{4,0},{5,1},{6,2},{7,3},{8,12},{9,13},{10,... | collective-permute-start | bytes 737288 | tf_op jit(solution)/shard_map/ppermute | solution.py:352
  27.5 1.1 %collective-permute-done.5.mate = bf16[480,256]{1,0:T(8,128)(2,1)S(1)} collective-permute-done((bf16[480,256]{1,0:T(8,128)(2,1)S(1)}, bf16[480,256]{1,0:T(8,128)(2,1)S(1)}, u32[]{:S(2)}, u32[]{:S(2)}) %collective-permute-start.5) | collective-permute-done | bytes 245792 | tf_op jit(solution)/shard_map/ppermute | solution.py:352
  28.6 4.9 %decode.1 = bf16[32,4,16,256]{3,2,1,0:T(8,128)(2,1)} custom-call(f32[120,512]{1,0:T(8,128)S(1)} %get-tuple-element.29.win, bf16[576,256]{1,0:T(8,128)(2,1)S(1)} %collective-permute-done.3.near, bf16[64,512]{1,0:T(8,128)(2,1)S(1)} %collective-permute-done.4.far, bf16[480,256]{1,0:T(8,128)(2,1)S(1)} %collective-permute-done.5.mate, ...), custom_call_target="tpu_custom_call" | custom-call | flops 5000000000 | bytes 15000000 | tf_op jit(solution)/shard_map/decode/pallas_call | solution.py:439
  (2 shorter events, 0.1 us)
Async XLA Ops:
  0.0 4.5 %copy-start = (bf16[32,4,16,256]{3,2,1,0:T(8,128)(2,1)S(1)}, bf16[32,4,16,256]{3,2,1,0:T(8,128)(2,1)}, u32[]{:S(2)}) copy-start(bf16[32,4,16,256]{3,2,1,0:T(8,128)(2,1)} %state.3) | copy-start | bytes 3145732
  0.0 4.9 %copy-start.5 = (bf16[64,4,768]{2,1,0:T(4,128)(2,1)S(1)}, bf16[64,4,768]{2,1,0:T(4,128)(2,1)}, u32[]{:S(2)}) copy-start(bf16[64,4,768]{2,1,0:T(4,128)(2,1)} %param.10) | copy-start | bytes 1179652
  0.0 5.0 %copy-start.2 = (bf16[4,4,4,32,64]{4,3,2,1,0:T(8,128)(2,1)S(1)}, bf16[4,4,4,32,64]{4,3,2,1,0:T(8,128)(2,1)}, u32[]{:S(2)}) copy-start(bf16[4,4,4,32,64]{4,3,2,1,0:T(8,128)(2,1)} %dec.1) | copy-start | bytes 786436
  2.9 2.4 %copy-start.1 = (bf16[4,768,512]{2,1,0:T(8,128)(2,1)S(1)}, bf16[4,768,512]{2,1,0:T(8,128)(2,1)}, u32[]{:S(2)}) copy-start(bf16[4,768,512]{2,1,0:T(8,128)(2,1)} %proj.1) | copy-start | bytes 9437188
  2.9 4.8 %collective-permute-start = (bf16[272,256]{1,0:T(8,128)(2,1)}, bf16[272,256]{1,0:T(8,128)(2,1)S(1)}, u32[]{:S(2)}, u32[]{:S(2)}) collective-permute-start(bf16[272,256]{1,0:T(8,128)(2,1)} %get-tuple-element.24), channel_id=1, source_target_pairs={{0,1},{1,2},{2,3},{3,0},{4,5},{5,6},{6,7},{7,4},{8,9},{9,10},{10,1... | collective-permute-start | bytes 417800 | tf_op jit(solution)/shard_map/ppermute | solution.py:341
  3.2 5.6 %collective-permute-start.1 = (bf16[272,256]{1,0:T(8,128)(2,1)}, bf16[272,256]{1,0:T(8,128)(2,1)S(1)}, u32[]{:S(2)}, u32[]{:S(2)}) collective-permute-start(bf16[272,256]{1,0:T(8,128)(2,1)} %get-tuple-element.25), channel_id=1, source_target_pairs={{0,3},{1,0},{2,1},{3,2},{4,7},{5,4},{6,5},{7,6},{8,11},{9,8},{10,9... | collective-permute-start | bytes 417800 | tf_op jit(solution)/shard_map/ppermute | solution.py:341
  5.3 3.6 %copy-start.4 = (s32[8,256]{1,0:T(8,128)S(1)}, s32[8,256]{1,0:T(8,128)}, u32[]{:S(2)}) copy-start(s32[8,256]{1,0:T(8,128)} %get-tuple-element.23.own) | copy-start | bytes 24580
  7.0 5.3 %copy-start.3 = (bf16[2,2,2,64,33]{3,2,4,1,0:T(2,128)(2,1)S(1)}, bf16[2,2,2,64,33]{3,2,4,1,0:T(2,128)(2,1)}, u32[]{:S(2)}) copy-start(bf16[2,2,2,64,33]{3,2,4,1,0:T(2,128)(2,1)} %param.16) | copy-start | bytes 101380
  10.4 3.5 %collective-permute-start.2 = (bf16[112,512]{1,0:T(8,128)(2,1)S(1)}, bf16[112,512]{1,0:T(8,128)(2,1)S(1)}, u32[]{:S(2)}, u32[]{:S(2)}) collective-permute-start(bf16[112,512]{1,0:T(8,128)(2,1)S(1)} %get-tuple-element.32), channel_id=1, source_target_pairs={{0,4},{1,5},{2,6},{3,7},{4,0},{5,1},{6,2},{7,3},{8,12},{9,13},{10,... | collective-permute-start | bytes 344072 | tf_op jit(solution)/shard_map/ppermute | solution.py:352
  13.9 8.6 %collective-permute-start.3 = (bf16[576,256]{1,0:T(8,128)(2,1)S(1)}, bf16[576,256]{1,0:T(8,128)(2,1)S(1)}, u32[]{:S(2)}, u32[]{:S(2)}) collective-permute-start(bf16[576,256]{1,0:T(8,128)(2,1)S(1)} %get-tuple-element.34), channel_id=1, source_target_pairs={{0,1},{1,0},{2,3},{3,2},{4,8},{5,9},{6,10},{7,11},{8,4},{9,5},{10,... | collective-permute-start | bytes 884744 | tf_op jit(solution)/shard_map/ppermute | solution.py:352
  15.6 7.0 %collective-permute-start.4 = (bf16[64,512]{1,0:T(8,128)(2,1)S(1)}, bf16[64,512]{1,0:T(8,128)(2,1)S(1)}, u32[]{:S(2)}, u32[]{:S(2)}) collective-permute-start(bf16[64,512]{1,0:T(8,128)(2,1)S(1)} %get-tuple-element.35), channel_id=1, source_target_pairs={{0,8},{1,9},{2,10},{3,11},{4,16},{5,17},{6,18},{7,19},{8,0},{9,1},... | collective-permute-start | bytes 196616 | tf_op jit(solution)/shard_map/ppermute | solution.py:352
  22.6 6.1 %collective-permute-start.5 = (bf16[480,256]{1,0:T(8,128)(2,1)S(1)}, bf16[480,256]{1,0:T(8,128)(2,1)S(1)}, u32[]{:S(2)}, u32[]{:S(2)}) collective-permute-start(bf16[480,256]{1,0:T(8,128)(2,1)S(1)} %inward.1), channel_id=1, source_target_pairs={{0,4},{1,5},{2,6},{3,7},{4,0},{5,1},{6,2},{7,3},{8,12},{9,13},{10,... | collective-permute-start | bytes 737288 | tf_op jit(solution)/shard_map/ppermute | solution.py:352

commit v5 on v4

--- a/solution.py
+++ b/solution.py
@@ -106,7 +106,7 @@
         flat[z] = dot(state[:, z].reshape(C1 * YD, XD), split).astype(BF)
 
 
-def place_kernel(own, left, right, high, low, small, win, near, far, mate, keys):
+def place_kernel(own, left, right, high, low, fs, win, near, far, mate, out, keys):
     slab, part = lax.axis_index("gz"), lax.axis_index("gy")
     core = slab % 2
     keys[0:1, 0:KL] = own[0:1, :].astype(F32)
@@ -145,9 +145,11 @@
     near[...] = acc[120:240]
     mate[...] = acc[240:352].astype(BF)
     far[...] = acc[352:]
-
-
-def encode_kernel(flat, left, right, enc, fs, out, keep, wb, we, x, wide):
+    for t in range(4):
+        out[t * C2 : (t + 1) * C2, :] = fs[core, :, t * XD : (t + 1) * XD].astype(BF)
+
+
+def encode_kernel(flat, enc, fs, wb, we, x, wide):
     rows = iota((32, C2), 0)
     bias = [jnp.zeros((32, C2), F32) for _ in range(4)]
     for p in range(2):
@@ -170,26 +172,34 @@
             for q in range(2):
                 for s in range(2):
                     k = (p * 4 + q * 2 + s) * C1
-                    lanes = slice(s * XC, (s + 1) * XC)
-                    h = z * 64 + q * C1
-                    x[k : k + C1, 0:XC] = left[h : h + C1, lanes]
-                    x[k : k + C1, 9 * XC : 10 * XC] = right[h : h + C1, lanes]
                     for b in range(8):
                         y = wide[z * 2 + s, pl.ds(2 * b + q, C1, stride=YD), :]
-                        x[k : k + C1, (b + 1) * XC : (b + 2) * XC] = y.astype(BF)
+                        x[k : k + C1, b * XC : (b + 1) * XC] = y.astype(BF)
         f = lax.dot_general(we[...], x[...], (((0,), (0,)), ((), ())), preferred_element_type=F32)
         fs[a] = f
 
-        def put(ref, f=f):
-            for t in range(5):
-                ref[t * C2 : (t + 1) * C2, :] = f[:, t * XD : (t + 1) * XD].astype(BF)
-
-        mine = lax.axis_index("gz") % 2 == a
-        pl.when(mine)(functools.partial(put, out))
-        pl.when(jnp.logical_not(mine))(functools.partial(put, keep))
-
-
-def prepare_kernel(dec, wdec, mats, small):
+
+def halo_kernel(left, right, we, fs, fh, edge, keep, x):
+    for a in range(2):
+        for p in range(2):
+            for q in range(2):
+                for s in range(2):
+                    k = (p * 4 + q * 2 + s) * C1
+                    lanes = slice(s * XC, (s + 1) * XC)
+                    h = (2 * a + p) * 64 + q * C1
+                    x[k : k + C1, 2 * a * XC : (2 * a + 1) * XC] = left[h : h + C1, lanes]
+                    x[k : k + C1, (2 * a + 1) * XC : (2 * a + 2) * XC] = right[h : h + C1, lanes]
+    f = lax.dot_general(we[...], x[...], (((0,), (0,)), ((), ())), preferred_element_type=F32)
+    for a in range(2):
+        fh[a] = f[:, a * XD : (a + 1) * XD]
+    core = lax.axis_index("gz") % 2
+    edge[...] = fh[core].astype(BF)
+    for t in range(4):
+        keep[t * C2 : (t + 1) * C2, :] = fs[1 - core, :, t * XD : (t + 1) * XD].astype(BF)
+    keep[4 * C2 :, :] = fh[1 - core].astype(BF)
+
+
+def prepare_kernel(dec, beyond, wdec, mats, small):
     mats[0:XD, 0:XD] = split_columns()
     mats[0:XD, XD : 2 * XD] = merge_columns()
     core = lax.axis_index("gz") % 2
@@ -212,14 +222,14 @@
                             wdec[pz, r0 : r0 + C1, c0 : c0 + C2] = dec[kz, ky, kx]
 
 
-def out_kernel(near, far, got, pre, pay, pay_far, tmp):
+def out_kernel(near, far, got, edge, pay, pay_far, tmp):
     tmp[0:CHIP] = near[...]
     tmp[CHIP:128] = jnp.zeros((8, TILE), F32)
     tmp[0:MATE] += got[...].astype(F32)[:MATE]
     total = tmp[...].astype(BF)
     pay[0:128, :] = total[:, :XD]
     pay[128:256, :] = total[:, XD:]
-    pay[256:, :] = pre[...]
+    pay[256:, :] = edge[...]
     tmp[0:64] = far[...]
     tmp[0 : 2 * ROWS] += got[...].astype(F32)[8 * ROWS : MATE]
     pay_far[...] = tmp[0:64].astype(BF)
@@ -230,7 +240,7 @@
     tmp[:, XD:] = win[:, XD:] + near[128:256, :].astype(F32)[:CHIP]
 
 
-def mate_kernel(win, near, far, pre, pay, tmp):
+def mate_kernel(win, near, far, pre, small, pay, tmp):
     add_near(tmp, win, near)
     tmp[0:64] += far[...].astype(F32)
     total = tmp[CHIP - OWN :, :].astype(BF)
@@ -239,7 +249,7 @@
     pay[2 * OWN :, :] = pre[...]
 
 
-def decode_kernel(win, near, far, mate, fs, flat, wdec, wb, mats, small, out, bp, x, ns, tmp, stage, sems):
+def decode_kernel(win, near, far, mate, beyond, fs, fh, flat, wdec, wb, mats, small, out, bp, x, ns, tmp, stage, sems):
     slab, part = lax.axis_index("gz"), lax.axis_index("gy")
     core = slab % 2
     split = mats[0:XD, 0:XD]
@@ -265,16 +275,16 @@
         if a == 3:
             inside = slab < 63
         for n in range(ROWS):
-            lanes = slice(n * XC, (n + 1) * XC)
+            outer = n in (0, 9)
+            half = slice((n != 0) * XC, ((n != 0) + 1) * XC) if outer else slice((n - 1) % 2 * XC, ((n - 1) % 2 + 1) * XC)
             if a in (1, 2):
-                v = fs[a - 1, :, lanes]
+                v = fh[a - 1, :, half] if outer else fs[a - 1, :, (n - 1) * XC : n * XC]
             else:
-                half = slice((n % 2) * XC, (n % 2 + 1) * XC)
-                r0 = (n // 2) * C2
-                v1 = near[256 + r0 : 256 + r0 + C2, half].astype(F32)
+                r0 = 4 * C2 if outer else (n - 1) // 2 * C2
+                v1 = (near[256:, half] if outer else beyond[r0 : r0 + C2, half]).astype(F32)
                 v2 = mate[2 * OWN + r0 : 2 * OWN + r0 + C2, half].astype(F32)
                 v = jnp.where(core == (0 if a == 0 else 1), v1, v2)
-            v = v + pb[:, lanes]
+            v = v + pb[:, n * XC : (n + 1) * XC]
             v = 0.5 * v * (1.0 + jnp.tanh(0.79788456 * (v + 0.044715 * (v * v * v))))
             ok = inside
             if n == 0:
@@ -388,57 +398,67 @@
         specs=[pl.BlockSpec((4, NB, TILE), lambda v: (0, v, 0))] * 2,
         name="project",
     )(rays, projector, flat)
-    wdec, mats, small = call(
-        prepare_kernel,
-        [VM],
-        [shape((2, 128, 1152)), shape((XD, 2 * XD)), shape((2, OWN, OWN))],
-        cost=cost(0.3),
-        name="prepare",
-    )(dec_weight)
-    win, near, far, mate = call(
+    fs, wb, we = call(
+        encode_kernel,
+        [VM] * 2,
+        [shape((2, C2, 8 * XC), F32), shape((4, 32, C2)), shape((8 * C1, C2))],
+        [V((8 * C1, 8 * XC), BF), V((2 * ZD, C1 * YD, XC), F32)],
+        cost=cost(1.3),
+        name="encode",
+    )(flat, jnp.transpose(enc_weight, (0, 1, 4, 2, 3)))
+    win, near, far, mate, pre_out = call(
         place_kernel,
-        [VM] * 5 + [ANY],
+        [VM] * 6,
         [
             shape((CHIP, TILE), F32),
             shape((CHIP, TILE), F32),
             shape((64, TILE), F32),
             shape((112, TILE)),
+            shape((4 * C2, XD)),
         ],
         [V((8, 3 * KL), F32)],
         cost=cost(1.5),
         name="place",
-    )(own, left, right, high, low, small)
+    )(own, left, right, high, low, fs)
     got = swapped(mate, 1)
-    fs, pre_out, pre_mate, wb = call(
-        encode_kernel,
+    beyond = swapped(pre_out, -1)
+    fh, edge, pre_mate = call(
+        halo_kernel,
         [VM] * 4,
-        [shape((2, C2, NL), F32), shape((5 * C2, XD)), shape((5 * C2, XD)), shape((4, 32, C2))],
-        [V((8 * C1, C2), BF), V((8 * C1, NL), BF), V((2 * ZD, C1 * YD, XC), F32)],
-        cost=cost(1.5),
-        name="encode",
-    )(flat, left, right, jnp.transpose(enc_weight, (0, 1, 4, 2, 3)))
+        [shape((2, C2, XD), F32), shape((C2, XD)), shape((5 * C2, XD))],
+        [V((8 * C1, 4 * XC), BF)],
+        cost=cost(0.5),
+        name="halo",
+    )(left, right, we, fs)
     pay, pay_far = call(
         out_kernel,
         [VM] * 4,
-        [shape((576, XD)), shape((64, TILE))],
+        [shape((320, XD)), shape((64, TILE))],
         [V((128, TILE), F32)],
         cost=cost(0.1),
         name="outward",
-    )(near, far, got, pre_out)
+    )(near, far, got, edge)
     got_near = swapped(pay, -1)
     got_far = swapped(pay_far, -3)
+    wdec, mats, small = call(
+        prepare_kernel,
+        [VM, ANY],
+        [shape((2, 128, 1152)), shape((XD, 2 * XD)), shape((2, OWN, OWN))],
+        cost=cost(4.0),
+        name="prepare",
+    )(dec_weight, beyond)
     pay_mate = call(
         mate_kernel,
-        [VM] * 4,
+        [VM] * 4 + [ANY],
         [shape((2 * OWN + 5 * C2, XD))],
         [V((CHIP, TILE), F32)],
         cost=cost(0.1),
         name="inward",
-    )(win, got_near, got_far, pre_mate)[0]
+    )(win, got_near, got_far, pre_mate, small)[0]
     got_mate = swapped(pay_mate, 1)
     return call(
         decode_kernel,
-        [VM] * 10,
+        [VM] * 12,
         [shape((C1, ZD, YD, XD))],
         [
             V((32, NL), F32),
@@ -452,7 +472,7 @@
         cost=cost(5.0),
         vlim=24 * MIB,
         name="decode",
-    )(win, got_near, got_far, got_mate, fs, flat, wdec, wb, mats, small)[0]
+    )(win, got_near, got_far, got_mate, beyond, fs, fh, flat, wdec, wb, mats, small)[0]
 
 
 def solution(mesh):

time: 33.6 us -> 32.9 us (0.979)
  waiting for transfers between devices: 8.38 us -> 7.46 us
    ppermute x2, waiting for transfers between devices: 1.83 us -> 0.89 us  [shifted(): lax.ppermute(block, axis, [(i, (i + distance) % n) for i in range(n)])]
    ppermute x4 -> x5, starting transfers between devices: 10.1 us -> 10.2 us  [swapped(): lax.ppermute(block, ('gz', 'gy'), sorted(pairs | {(j, i) for i, j in pair...]
    pallas_call x6 -> x7, Pallas kernels: 8.32 us -> 8.37 us  [the longest x1 5.01 us: per_device(): call(decode_kernel, [VM] * 12, [shape((C1, ZD, YD, XD))], [V((32, NL), F3...]
    ppermute x4 -> x5, waiting for transfers between devices: 6.54 us -> 6.58 us  [swapped(): lax.ppermute(block, ('gz', 'gy'), sorted(pairs | {(j, i) for i, j in pair...]
  transfers between devices with their start and end apart: 6 -> 7, of which waited for: 4 -> 5; matrix products, arithmetic and copies ran while one was open for 0% -> 0% of each run, Pallas kernels for 12% -> 12%
where the time goes in v5:
time: 32.9 us; the launch traced here: 32.8 us
  Pallas kernels  13.4 us (41%)
  starting transfers between devices  11.7 us (36%)
  waiting for transfers between devices  7.46 us (23%)
    ppermute x5, starting transfers between devices, swapped(): lax.ppermute(block, ('gz', 'gy'), sorted(pairs | {(j, i) for i, j in pair...  10.2 us
    ppermute x5, waiting for transfers between devices, swapped(): lax.ppermute(block, ('gz', 'gy'), sorted(pairs | {(j, i) for i, j in pair...  6.58 us
    pallas_call x1, Pallas kernels, per_device(): call(decode_kernel, [VM] * 12, [shape((C1, ZD, YD, XD))], [V((32, NL), F3...  5.01 us
    pallas_call x1, Pallas kernels, per_device(): call(edge_kernel, [ANY] * 5, [shape((272, XD)), shape((272, XD)), shape((...  2.92 us
    pallas_call x1, Pallas kernels, per_device(): call(project_kernel, [pl.BlockSpec((4, NB, DC), lambda v: (0, 0, 0)), pl....  1.69 us
    ppermute x2, starting transfers between devices, shifted(): lax.ppermute(block, axis, [(i, (i + distance) % n) for i in range(n)])  1.54 us
    pallas_call x1, Pallas kernels, per_device(): call(place_kernel, [VM] * 6, [shape((CHIP, TILE), F32), shape((CHIP, TILE...  1.53 us
    pallas_call x1, Pallas kernels, per_device(): call(encode_kernel, [VM] * 2, [shape((2, C2, 8 * XC), F32), shape((4, 32,...  1.23 us
  transfers between devices with their start and end apart: 7, of which 5 were waited for; matrix products, arithmetic and copies ran while one was open for 0% of the time, Pallas kernels for 12%

profile of v5, /device:TPU:31, one launch (start us, length us, event | category | flops | bytes accessed | tf_op | source)
XLA Modules:
  0.0 32.8 jit_solution(15649693581282189938)
XLA Ops:
  0.0 0.0 copy-start
  0.0 0.0 copy-start.5
  0.0 0.0 copy-start.1
  0.0 2.9 %edge.1 = (bf16[272,256]{1,0:T(8,128)(2,1)}, bf16[272,256]{1,0:T(8,128)(2,1)}, s32[8,256]{1,0:T(8,128)}) custom-call(s32[7,1,64]{2,1,0:T(1,128)} %bitcast.7, s32[1,64,224]{2,1,0:T(8,128)} %block.1, s32[1,64,224]{2,1,0:T(8,128)} %tile.1, s32[1,64,224]{2,1,0:T(8,128)} %view.1, bf16[32,4,16,256]{3,2,1,0:T(8,128)(2,1)} %state.3), custom_call_target="tpu_custom_call" | custom-call | flops 2900000000 | bytes 8700000 | tf_op jit(solution)/shard_map/edge/pallas_call | solution.py:368
  2.9 0.3 collective-permute-start
  3.2 1.3 %collective-permute-start.1 = (bf16[272,256]{1,0:T(8,128)(2,1)}, bf16[272,256]{1,0:T(8,128)(2,1)S(1)}, u32[]{:S(2)}, u32[]{:S(2)}) collective-permute-start(bf16[272,256]{1,0:T(8,128)(2,1)} %get-tuple-element.28), channel_id=1, source_target_pairs={{0,3},{1,0},{2,1},{3,2},{4,7},{5,4},{6,5},{7,6},{8,11},{9,8},{10,9... | collective-permute-start | bytes 417800 | tf_op jit(solution)/shard_map/ppermute | solution.py:351
  4.5 0.0 copy-done
  4.5 0.4 %flat.1 = bf16[4,512,256]{2,1,0:T(8,128)(2,1)S(1)} custom-call(bf16[32,4,16,256]{3,2,1,0:T(8,128)(2,1)S(1)} %copy-done), custom_call_target="tpu_custom_call" | custom-call | flops 400000000 | bytes 1200000 | tf_op jit(solution)/shard_map/flat/pallas_call | solution.py:386
  4.9 0.0 copy-done.5
  5.0 0.0 copy-done.1
  5.0 0.0 copy-start.3
  5.0 1.7 %project.1 = (bf16[4,256,512]{2,1,0:T(8,128)(2,1)S(1)}, bf16[4,256,512]{2,1,0:T(8,128)(2,1)S(1)}) custom-call(bf16[4,64,768]{2,1,0:T(8,128)(2,1)S(1)} %bitcast.5, bf16[4,768,512]{2,1,0:T(8,128)(2,1)S(1)} %copy-done.1, bf16[4,512,256]{2,1,0:T(8,128)(2,1)S(1)} %flat.1), custom_call_target="tpu_custom_call" | custom-call | flops 1700000000 | bytes 5100000 | tf_op jit(solution)/shard_map/project/pallas_call | solution.py:388
  6.7 0.0 copy-start.4
  6.7 0.0 copy-done.3
  6.7 1.2 %encode.1 = (f32[2,64,1024]{2,1,0:T(8,128)S(1)}, bf16[4,32,64]{2,1,0:T(8,128)(2,1)S(1)}, bf16[256,64]{1,0:T(8,128)(2,1)S(1)}) custom-call(bf16[4,512,256]{2,1,0:T(8,128)(2,1)S(1)} %flat.1, bf16[2,2,33,2,64]{4,3,2,1,0:T(2,128)(2,1)S(1)} %bitcast.6), custom_call_target="tpu_custom_call" | custom-call | flops 1300000000 | bytes 3900000 | tf_op jit(solution)/shard_map/encode/pallas_call | solution.py:401
  8.0 0.0 collective-permute-done.left
  8.0 0.9 %collective-permute-done.1.right = bf16[272,256]{1,0:T(8,128)(2,1)S(1)} collective-permute-done((bf16[272,256]{1,0:T(8,128)(2,1)}, bf16[272,256]{1,0:T(8,128)(2,1)S(1)}, u32[]{:S(2)}, u32[]{:S(2)}) %collective-permute-start.1) | collective-permute-done | bytes 139296 | tf_op jit(solution)/shard_map/ppermute | solution.py:351
  8.9 0.0 copy-done.4
  8.9 0.0 copy-start.2
  8.9 1.5 %place.1 = (f32[120,512]{1,0:T(8,128)S(1)}, f32[120,512]{1,0:T(8,128)S(1)}, f32[64,512]{1,0:T(8,128)S(1)}, bf16[112,512]{1,0:T(8,128)(2,1)S(1)}, bf16[256,256]{1,0:T(8,128)(2,1)S(1)}) custom-call(s32[8,256]{1,0:T(8,128)S(1)} %copy-done.4, bf16[272,256]{1,0:T(8,128)(2,1)S(1)} %collective-permute-done.left, bf16[272,256]{1,0:T(8,128)(2,1)S(1)} %collective-permute-done.1.right, ...), custom_call_target="tpu_custom_call" | custom-call | flops 1500000000 | bytes 4500000 | tf_op jit(solution)/shard_map/place/pallas_call | solution.py:409
  10.4 3.5 %collective-permute-start.5 = (bf16[256,256]{1,0:T(8,128)(2,1)S(1)}, bf16[256,256]{1,0:T(8,128)(2,1)S(1)}, u32[]{:S(2)}, u32[]{:S(2)}) collective-permute-start(bf16[256,256]{1,0:T(8,128)(2,1)S(1)} %get-tuple-element.41), channel_id=1, source_target_pairs={{0,1},{1,0},{2,3},{3,2},{4,8},{5,9},{6,10},{7,11},{8,4},{9,5},{10,... | collective-permute-start | bytes 393224 | tf_op jit(solution)/shard_map/ppermute | solution.py:362
  13.9 2.8 %collective-permute-start.2 = (bf16[112,512]{1,0:T(8,128)(2,1)S(1)}, bf16[112,512]{1,0:T(8,128)(2,1)S(1)}, u32[]{:S(2)}, u32[]{:S(2)}) collective-permute-start(bf16[112,512]{1,0:T(8,128)(2,1)S(1)} %get-tuple-element.35), channel_id=1, source_target_pairs={{0,4},{1,5},{2,6},{3,7},{4,0},{5,1},{6,2},{7,3},{8,12},{9,13},{10,... | collective-permute-start | bytes 344072 | tf_op jit(solution)/shard_map/ppermute | solution.py:362
  16.6 0.2 halo.1
  16.9 0.7 %collective-permute-done.2.got = bf16[112,512]{1,0:T(8,128)(2,1)S(1)} collective-permute-done((bf16[112,512]{1,0:T(8,128)(2,1)S(1)}, bf16[112,512]{1,0:T(8,128)(2,1)S(1)}, u32[]{:S(2)}, u32[]{:S(2)}) %collective-permute-start.2) | collective-permute-done | bytes 114720 | tf_op jit(solution)/shard_map/ppermute | solution.py:362
  17.7 0.1 collective-permute-start.3
  17.8 0.7 %collective-permute-start.4 = (bf16[64,512]{1,0:T(8,128)(2,1)S(1)}, bf16[64,512]{1,0:T(8,128)(2,1)S(1)}, u32[]{:S(2)}, u32[]{:S(2)}) collective-permute-start(bf16[64,512]{1,0:T(8,128)(2,1)S(1)} %get-tuple-element.39), channel_id=1, source_target_pairs={{0,8},{1,9},{2,10},{3,11},{4,16},{5,17},{6,18},{7,19},{8,0},{9,1},... | collective-permute-start | bytes 196616 | tf_op jit(solution)/shard_map/ppermute | solution.py:362
  18.5 0.0 collective-permute-done.5.beyond
  18.5 0.0 copy-done.2
  18.5 0.3 prepare.1
  18.8 3.8 %collective-permute-done.4.far = bf16[64,512]{1,0:T(8,128)(2,1)S(1)} collective-permute-done((bf16[64,512]{1,0:T(8,128)(2,1)S(1)}, bf16[64,512]{1,0:T(8,128)(2,1)S(1)}, u32[]{:S(2)}, u32[]{:S(2)}) %collective-permute-start.4) | collective-permute-done | bytes 65568 | tf_op jit(solution)/shard_map/ppermute | solution.py:362
  22.5 0.9 %collective-permute-done.3.near = bf16[320,256]{1,0:T(8,128)(2,1)S(1)} collective-permute-done((bf16[320,256]{1,0:T(8,128)(2,1)S(1)}, bf16[320,256]{1,0:T(8,128)(2,1)S(1)}, u32[]{:S(2)}, u32[]{:S(2)}) %collective-permute-start.3) | collective-permute-done | bytes 163872 | tf_op jit(solution)/shard_map/ppermute | solution.py:362
  23.5 3.1 %collective-permute-start.6 = (bf16[480,256]{1,0:T(8,128)(2,1)S(1)}, bf16[480,256]{1,0:T(8,128)(2,1)S(1)}, u32[]{:S(2)}, u32[]{:S(2)}) collective-permute-start(bf16[480,256]{1,0:T(8,128)(2,1)S(1)} %inward.1), channel_id=1, source_target_pairs={{0,4},{1,5},{2,6},{3,7},{4,0},{5,1},{6,2},{7,3},{8,12},{9,13},{10,... | collective-permute-start | bytes 737288 | tf_op jit(solution)/shard_map/ppermute | solution.py:362
  26.6 1.1 %collective-permute-done.6.mate = bf16[480,256]{1,0:T(8,128)(2,1)S(1)} collective-permute-done((bf16[480,256]{1,0:T(8,128)(2,1)S(1)}, bf16[480,256]{1,0:T(8,128)(2,1)S(1)}, u32[]{:S(2)}, u32[]{:S(2)}) %collective-permute-start.6) | collective-permute-done | bytes 245792 | tf_op jit(solution)/shard_map/ppermute | solution.py:362
  27.8 5.0 %decode.1 = bf16[32,4,16,256]{3,2,1,0:T(8,128)(2,1)} custom-call(f32[120,512]{1,0:T(8,128)S(1)} %get-tuple-element.32.win, bf16[320,256]{1,0:T(8,128)(2,1)S(1)} %collective-permute-done.3.near, bf16[64,512]{1,0:T(8,128)(2,1)S(1)} %collective-permute-done.4.far, bf16[480,256]{1,0:T(8,128)(2,1)S(1)} %collective-permute-done.6.mate, ...), custom_call_target="tpu_custom_call" | custom-call | flops 5000000000 | bytes 15000000 | tf_op jit(solution)/shard_map/decode/pallas_call | solution.py:459
  (3 shorter events, 0.1 us)
Async XLA Ops:
  0.0 4.5 %copy-start = (bf16[32,4,16,256]{3,2,1,0:T(8,128)(2,1)S(1)}, bf16[32,4,16,256]{3,2,1,0:T(8,128)(2,1)}, u32[]{:S(2)}) copy-start(bf16[32,4,16,256]{3,2,1,0:T(8,128)(2,1)} %state.3) | copy-start | bytes 3145732
  0.0 4.9 %copy-start.5 = (bf16[64,4,768]{2,1,0:T(4,128)(2,1)S(1)}, bf16[64,4,768]{2,1,0:T(4,128)(2,1)}, u32[]{:S(2)}) copy-start(bf16[64,4,768]{2,1,0:T(4,128)(2,1)} %param.10) | copy-start | bytes 1179652
  0.0 5.0 %copy-start.1 = (bf16[4,768,512]{2,1,0:T(8,128)(2,1)S(1)}, bf16[4,768,512]{2,1,0:T(8,128)(2,1)}, u32[]{:S(2)}) copy-start(bf16[4,768,512]{2,1,0:T(8,128)(2,1)} %proj.1) | copy-start | bytes 9437188
  2.9 5.0 %collective-permute-start = (bf16[272,256]{1,0:T(8,128)(2,1)}, bf16[272,256]{1,0:T(8,128)(2,1)S(1)}, u32[]{:S(2)}, u32[]{:S(2)}) collective-permute-start(bf16[272,256]{1,0:T(8,128)(2,1)} %get-tuple-element.27), channel_id=1, source_target_pairs={{0,1},{1,2},{2,3},{3,0},{4,5},{5,6},{6,7},{7,4},{8,9},{9,10},{10,1... | collective-permute-start | bytes 417800 | tf_op jit(solution)/shard_map/ppermute | solution.py:351
  3.2 5.6 %collective-permute-start.1 = (bf16[272,256]{1,0:T(8,128)(2,1)}, bf16[272,256]{1,0:T(8,128)(2,1)S(1)}, u32[]{:S(2)}, u32[]{:S(2)}) collective-permute-start(bf16[272,256]{1,0:T(8,128)(2,1)} %get-tuple-element.28), channel_id=1, source_target_pairs={{0,3},{1,0},{2,1},{3,2},{4,7},{5,4},{6,5},{7,6},{8,11},{9,8},{10,9... | collective-permute-start | bytes 417800 | tf_op jit(solution)/shard_map/ppermute | solution.py:351
  5.0 1.7 %copy-start.3 = (bf16[2,2,2,64,33]{3,2,4,1,0:T(2,128)(2,1)S(1)}, bf16[2,2,2,64,33]{3,2,4,1,0:T(2,128)(2,1)}, u32[]{:S(2)}) copy-start(bf16[2,2,2,64,33]{3,2,4,1,0:T(2,128)(2,1)} %param.16) | copy-start | bytes 101380
  6.7 2.2 %copy-start.4 = (s32[8,256]{1,0:T(8,128)S(1)}, s32[8,256]{1,0:T(8,128)}, u32[]{:S(2)}) copy-start(s32[8,256]{1,0:T(8,128)} %get-tuple-element.26.own) | copy-start | bytes 24580
  8.9 9.6 %copy-start.2 = (bf16[4,4,4,32,64]{4,3,2,1,0:T(8,128)(2,1)S(1)}, bf16[4,4,4,32,64]{4,3,2,1,0:T(8,128)(2,1)}, u32[]{:S(2)}) copy-start(bf16[4,4,4,32,64]{4,3,2,1,0:T(8,128)(2,1)} %dec.1) | copy-start | bytes 786436
  10.4 8.1 %collective-permute-start.5 = (bf16[256,256]{1,0:T(8,128)(2,1)S(1)}, bf16[256,256]{1,0:T(8,128)(2,1)S(1)}, u32[]{:S(2)}, u32[]{:S(2)}) collective-permute-start(bf16[256,256]{1,0:T(8,128)(2,1)S(1)} %get-tuple-element.41), channel_id=1, source_target_pairs={{0,1},{1,0},{2,3},{3,2},{4,8},{5,9},{6,10},{7,11},{8,4},{9,5},{10,... | collective-permute-start | bytes 393224 | tf_op jit(solution)/shard_map/ppermute | solution.py:362
  13.9 3.7 %collective-permute-start.2 = (bf16[112,512]{1,0:T(8,128)(2,1)S(1)}, bf16[112,512]{1,0:T(8,128)(2,1)S(1)}, u32[]{:S(2)}, u32[]{:S(2)}) collective-permute-start(bf16[112,512]{1,0:T(8,128)(2,1)S(1)} %get-tuple-element.35), channel_id=1, source_target_pairs={{0,4},{1,5},{2,6},{3,7},{4,0},{5,1},{6,2},{7,3},{8,12},{9,13},{10,... | collective-permute-start | bytes 344072 | tf_op jit(solution)/shard_map/ppermute | solution.py:362
  17.7 5.8 %collective-permute-start.3 = (bf16[320,256]{1,0:T(8,128)(2,1)S(1)}, bf16[320,256]{1,0:T(8,128)(2,1)S(1)}, u32[]{:S(2)}, u32[]{:S(2)}) collective-permute-start(bf16[320,256]{1,0:T(8,128)(2,1)S(1)} %get-tuple-element.38), channel_id=1, source_target_pairs={{0,1},{1,0},{2,3},{3,2},{4,8},{5,9},{6,10},{7,11},{8,4},{9,5},{10,... | collective-permute-start | bytes 491528 | tf_op jit(solution)/shard_map/ppermute | solution.py:362
  17.8 4.8 %collective-permute-start.4 = (bf16[64,512]{1,0:T(8,128)(2,1)S(1)}, bf16[64,512]{1,0:T(8,128)(2,1)S(1)}, u32[]{:S(2)}, u32[]{:S(2)}) collective-permute-start(bf16[64,512]{1,0:T(8,128)(2,1)S(1)} %get-tuple-element.39), channel_id=1, source_target_pairs={{0,8},{1,9},{2,10},{3,11},{4,16},{5,17},{6,18},{7,19},{8,0},{9,1},... | collective-permute-start | bytes 196616 | tf_op jit(solution)/shard_map/ppermute | solution.py:362
  23.5 4.3 %collective-permute-start.6 = (bf16[480,256]{1,0:T(8,128)(2,1)S(1)}, bf16[480,256]{1,0:T(8,128)(2,1)S(1)}, u32[]{:S(2)}, u32[]{:S(2)}) collective-permute-start(bf16[480,256]{1,0:T(8,128)(2,1)S(1)} %inward.1), channel_id=1, source_target_pairs={{0,4},{1,5},{2,6},{3,7},{4,0},{5,1},{6,2},{7,3},{8,12},{9,13},{10,... | collective-permute-start | bytes 737288 | tf_op jit(solution)/shard_map/ppermute | solution.py:362

commit v6 on v5

--- a/solution.py
+++ b/solution.py
@@ -46,7 +46,7 @@
     return (col == 2 * (row % XC) + row // XC).astype(BF)
 
 
-def edge_kernel(counts, block, tile, view, state, up, down, own, lists, cs, pairs, planes, some, sems):
+def edge_kernel(counts, block, tile, view, state, up, down, own, lists, cs, pairs, planes, sems):
     slab = lax.axis_index("gz")
     at = pl.multiple_of((slab // 8) * 8, 8)
     copies = [pltpu.make_async_copy(counts, cs, sems.at[0])]
@@ -56,7 +56,6 @@
         copies.append(pltpu.make_async_copy(state.at[:, z], planes.at[z], sems.at[4 + z]))
     for copy in copies:
         copy.start()
-    split = split_columns()
     row, col = iota((4 * C1, C1 * YD), 0), iota((4 * C1, C1 * YD), 1)
     y = row // C1
     y = jnp.where(y < 2, y, y + YD - 4)
@@ -84,11 +83,9 @@
     down[LIST:, :] = lists[...].astype(BF)
     for z in range(ZD):
         copies[4 + z].wait()
-        some[z * 128 : (z + 1) * 128, :] = dot(pick, planes[z].reshape(C1 * YD, XD)).astype(BF)
-    rows = dot(some[...], split).astype(BF)
-    for z in range(ZD):
-        down[z * 64 : z * 64 + 64, :] = rows[z * 128 : z * 128 + 64]
-        up[z * 64 : z * 64 + 64, :] = rows[z * 128 + 64 : z * 128 + 128]
+        rows = dot(pick, planes[z].reshape(C1 * YD, XD)).astype(BF)
+        down[z * 64 : z * 64 + 64, :] = rows[:64]
+        up[z * 64 : z * 64 + 64, :] = rows[64:]
 
 
 def project_kernel(res, proj, flat, high, low):
@@ -180,6 +177,9 @@
 
 
 def halo_kernel(left, right, we, fs, fh, edge, keep, x):
+    split = split_columns()
+    before = dot(left[:LIST, :], split).astype(BF)
+    after = dot(right[:LIST, :], split).astype(BF)
     for a in range(2):
         for p in range(2):
             for q in range(2):
@@ -187,8 +187,8 @@
                     k = (p * 4 + q * 2 + s) * C1
                     lanes = slice(s * XC, (s + 1) * XC)
                     h = (2 * a + p) * 64 + q * C1
-                    x[k : k + C1, 2 * a * XC : (2 * a + 1) * XC] = left[h : h + C1, lanes]
-                    x[k : k + C1, (2 * a + 1) * XC : (2 * a + 2) * XC] = right[h : h + C1, lanes]
+                    x[k : k + C1, 2 * a * XC : (2 * a + 1) * XC] = before[h : h + C1, lanes]
+                    x[k : k + C1, (2 * a + 1) * XC : (2 * a + 2) * XC] = after[h : h + C1, lanes]
     f = lax.dot_general(we[...], x[...], (((0,), (0,)), ((), ())), preferred_element_type=F32)
     for a in range(2):
         fh[a] = f[:, a * XD : (a + 1) * XD]
@@ -304,9 +304,12 @@
                     for dx in range(3):
                         r0 = a * 576 + dy * 192 + dx * C2
                         x[r0 : r0 + C2, m * XC : (m + 1) * XC] = shifts[dx]
+    middle = dot(wdec[...].reshape(256, 1152), x[576:1728, :])
     for f in range(ZD):
-        start = (f + 1) // 2 * 576
-        d = dot(wdec[f % 2], x[start : start + 1152, :])
+        if f in (1, 2):
+            d = middle[128:] if f == 1 else middle[:128]
+        else:
+            d = dot(wdec[f % 2], x[f // 2 * 1152 : f // 2 * 1152 + 1152, :])
         for py in range(2):
             for px in range(2):
                 r0 = (py * 2 + px) * C1
@@ -374,7 +377,6 @@
             pltpu.SMEM((SPAN, 1, 64), I32),
             V((3, 8, NPD), I32),
             V((ZD, C1, YD, XD), BF),
-            V((ZD * 128, XD), BF),
             pltpu.SemaphoreType.DMA((8,)),
         ],
         cost=cost(2.9),

time: 32.9 us -> 32.6 us (level)
  transfers between devices with their start and end apart: 7 -> 7, of which waited for: 5 -> 5; matrix products, arithmetic and copies ran while one was open for 0% -> 0% of each run, Pallas kernels for 12% -> 13%
where the time goes in v6:
time: 32.6 us; the launch traced here: 32.5 us
  Pallas kernels  13.3 us (41%)
  starting transfers between devices  11.7 us (36%)
  waiting for transfers between devices  7.29 us (22%)
    ppermute x5, starting transfers between devices, swapped(): lax.ppermute(block, ('gz', 'gy'), sorted(pairs | {(j, i) for i, j in pair...  10.2 us
    ppermute x5, waiting for transfers between devices, swapped(): lax.ppermute(block, ('gz', 'gy'), sorted(pairs | {(j, i) for i, j in pair...  6.41 us
    pallas_call x1, Pallas kernels, per_device(): call(decode_kernel, [VM] * 12, [shape((C1, ZD, YD, XD))], [V((32, NL), F3...  4.87 us
    pallas_call x1, Pallas kernels, per_device(): call(edge_kernel, [ANY] * 5, [shape((272, XD)), shape((272, XD)), shape((...  2.81 us
    pallas_call x1, Pallas kernels, per_device(): call(project_kernel, [pl.BlockSpec((4, NB, DC), lambda v: (0, 0, 0)), pl....  1.69 us
    ppermute x2, starting transfers between devices, shifted(): lax.ppermute(block, axis, [(i, (i + distance) % n) for i in range(n)])  1.54 us
    pallas_call x1, Pallas kernels, per_device(): call(place_kernel, [VM] * 6, [shape((CHIP, TILE), F32), shape((CHIP, TILE...  1.53 us
    pallas_call x1, Pallas kernels, per_device(): call(encode_kernel, [VM] * 2, [shape((2, C2, 8 * XC), F32), shape((4, 32,...  1.23 us
  transfers between devices with their start and end apart: 7, of which 5 were waited for; matrix products, arithmetic and copies ran while one was open for 0% of the time, Pallas kernels for 13%

profile of v6, /device:TPU:31, one launch (start us, length us, event | category | flops | bytes accessed | tf_op | source)
XLA Modules:
  0.0 32.5 jit_solution(3547800216953834744)
XLA Ops:
  0.0 0.0 copy-start
  0.0 0.0 copy-start.5
  0.0 0.0 copy-start.1
  0.0 2.8 %edge.1 = (bf16[272,256]{1,0:T(8,128)(2,1)}, bf16[272,256]{1,0:T(8,128)(2,1)}, s32[8,256]{1,0:T(8,128)}) custom-call(s32[7,1,64]{2,1,0:T(1,128)} %bitcast.7, s32[1,64,224]{2,1,0:T(8,128)} %block.1, s32[1,64,224]{2,1,0:T(8,128)} %tile.1, s32[1,64,224]{2,1,0:T(8,128)} %view.1, bf16[32,4,16,256]{3,2,1,0:T(8,128)(2,1)} %state.3), custom_call_target="tpu_custom_call" | custom-call | flops 2900000000 | bytes 8700000 | tf_op jit(solution)/shard_map/edge/pallas_call | solution.py:371
  2.8 0.3 collective-permute-start
  3.1 1.3 %collective-permute-start.1 = (bf16[272,256]{1,0:T(8,128)(2,1)}, bf16[272,256]{1,0:T(8,128)(2,1)S(1)}, u32[]{:S(2)}, u32[]{:S(2)}) collective-permute-start(bf16[272,256]{1,0:T(8,128)(2,1)} %get-tuple-element.28), channel_id=1, source_target_pairs={{0,3},{1,0},{2,1},{3,2},{4,7},{5,4},{6,5},{7,6},{8,11},{9,8},{10,9... | collective-permute-start | bytes 417800 | tf_op jit(solution)/shard_map/ppermute | solution.py:354
  4.4 0.0 copy-done
  4.4 0.4 %flat.1 = bf16[4,512,256]{2,1,0:T(8,128)(2,1)S(1)} custom-call(bf16[32,4,16,256]{3,2,1,0:T(8,128)(2,1)S(1)} %copy-done), custom_call_target="tpu_custom_call" | custom-call | flops 400000000 | bytes 1200000 | tf_op jit(solution)/shard_map/flat/pallas_call | solution.py:388
  4.8 0.0 copy-done.5
  4.9 0.0 copy-done.1
  4.9 0.0 copy-start.3
  4.9 1.7 %project.1 = (bf16[4,256,512]{2,1,0:T(8,128)(2,1)S(1)}, bf16[4,256,512]{2,1,0:T(8,128)(2,1)S(1)}) custom-call(bf16[4,64,768]{2,1,0:T(8,128)(2,1)S(1)} %bitcast.5, bf16[4,768,512]{2,1,0:T(8,128)(2,1)S(1)} %copy-done.1, bf16[4,512,256]{2,1,0:T(8,128)(2,1)S(1)} %flat.1), custom_call_target="tpu_custom_call" | custom-call | flops 1700000000 | bytes 5100000 | tf_op jit(solution)/shard_map/project/pallas_call | solution.py:390
  6.6 0.0 copy-start.4
  6.6 0.0 copy-done.3
  6.6 1.2 %encode.1 = (f32[2,64,1024]{2,1,0:T(8,128)S(1)}, bf16[4,32,64]{2,1,0:T(8,128)(2,1)S(1)}, bf16[256,64]{1,0:T(8,128)(2,1)S(1)}) custom-call(bf16[4,512,256]{2,1,0:T(8,128)(2,1)S(1)} %flat.1, bf16[2,2,33,2,64]{4,3,2,1,0:T(2,128)(2,1)S(1)} %bitcast.6), custom_call_target="tpu_custom_call" | custom-call | flops 1300000000 | bytes 3900000 | tf_op jit(solution)/shard_map/encode/pallas_call | solution.py:403
  7.8 0.0 collective-permute-done.left
  7.9 0.9 %collective-permute-done.1.right = bf16[272,256]{1,0:T(8,128)(2,1)S(1)} collective-permute-done((bf16[272,256]{1,0:T(8,128)(2,1)}, bf16[272,256]{1,0:T(8,128)(2,1)S(1)}, u32[]{:S(2)}, u32[]{:S(2)}) %collective-permute-start.1) | collective-permute-done | bytes 139296 | tf_op jit(solution)/shard_map/ppermute | solution.py:354
  8.7 0.0 copy-done.4
  8.7 0.0 copy-start.2
  8.7 1.5 %place.1 = (f32[120,512]{1,0:T(8,128)S(1)}, f32[120,512]{1,0:T(8,128)S(1)}, f32[64,512]{1,0:T(8,128)S(1)}, bf16[112,512]{1,0:T(8,128)(2,1)S(1)}, bf16[256,256]{1,0:T(8,128)(2,1)S(1)}) custom-call(s32[8,256]{1,0:T(8,128)S(1)} %copy-done.4, bf16[272,256]{1,0:T(8,128)(2,1)S(1)} %collective-permute-done.left, bf16[272,256]{1,0:T(8,128)(2,1)S(1)} %collective-permute-done.1.right, ...), custom_call_target="tpu_custom_call" | custom-call | flops 1500000000 | bytes 4500000 | tf_op jit(solution)/shard_map/place/pallas_call | solution.py:411
  10.3 3.5 %collective-permute-start.5 = (bf16[256,256]{1,0:T(8,128)(2,1)S(1)}, bf16[256,256]{1,0:T(8,128)(2,1)S(1)}, u32[]{:S(2)}, u32[]{:S(2)}) collective-permute-start(bf16[256,256]{1,0:T(8,128)(2,1)S(1)} %get-tuple-element.41), channel_id=1, source_target_pairs={{0,1},{1,0},{2,3},{3,2},{4,8},{5,9},{6,10},{7,11},{8,4},{9,5},{10,... | collective-permute-start | bytes 393224 | tf_op jit(solution)/shard_map/ppermute | solution.py:365
  13.8 2.8 %collective-permute-start.2 = (bf16[112,512]{1,0:T(8,128)(2,1)S(1)}, bf16[112,512]{1,0:T(8,128)(2,1)S(1)}, u32[]{:S(2)}, u32[]{:S(2)}) collective-permute-start(bf16[112,512]{1,0:T(8,128)(2,1)S(1)} %get-tuple-element.35), channel_id=1, source_target_pairs={{0,4},{1,5},{2,6},{3,7},{4,0},{5,1},{6,2},{7,3},{8,12},{9,13},{10,... | collective-permute-start | bytes 344072 | tf_op jit(solution)/shard_map/ppermute | solution.py:365
  16.5 0.4 %halo.1 = (f32[2,64,256]{2,1,0:T(8,128)S(1)}, bf16[64,256]{1,0:T(8,128)(2,1)S(1)}, bf16[320,256]{1,0:T(8,128)(2,1)S(1)}) custom-call(bf16[272,256]{1,0:T(8,128)(2,1)S(1)} %collective-permute-done.left, bf16[272,256]{1,0:T(8,128)(2,1)S(1)} %collective-permute-done.1.right, bf16[256,64]{1,0:T(8,128)(2,1)S(1)} %get-tuple-element.36.we, ...), custom_call_target="tpu_custom_call" | custom-call | flops 500000000 | bytes 1500000 | tf_op jit(solution)/shard_map/halo/pallas_call | solution.py:427
  16.9 0.6 %collective-permute-done.2.got = bf16[112,512]{1,0:T(8,128)(2,1)S(1)} collective-permute-done((bf16[112,512]{1,0:T(8,128)(2,1)S(1)}, bf16[112,512]{1,0:T(8,128)(2,1)S(1)}, u32[]{:S(2)}, u32[]{:S(2)}) %collective-permute-start.2) | collective-permute-done | bytes 114720 | tf_op jit(solution)/shard_map/ppermute | solution.py:365
  17.5 0.1 collective-permute-start.3
  17.6 0.7 %collective-permute-start.4 = (bf16[64,512]{1,0:T(8,128)(2,1)S(1)}, bf16[64,512]{1,0:T(8,128)(2,1)S(1)}, u32[]{:S(2)}, u32[]{:S(2)}) collective-permute-start(bf16[64,512]{1,0:T(8,128)(2,1)S(1)} %get-tuple-element.39), channel_id=1, source_target_pairs={{0,8},{1,9},{2,10},{3,11},{4,16},{5,17},{6,18},{7,19},{8,0},{9,1},... | collective-permute-start | bytes 196616 | tf_op jit(solution)/shard_map/ppermute | solution.py:365
  18.3 0.0 collective-permute-done.5.beyond
  18.3 0.0 copy-done.2
  18.4 0.3 prepare.1
  18.6 3.8 %collective-permute-done.4.far = bf16[64,512]{1,0:T(8,128)(2,1)S(1)} collective-permute-done((bf16[64,512]{1,0:T(8,128)(2,1)S(1)}, bf16[64,512]{1,0:T(8,128)(2,1)S(1)}, u32[]{:S(2)}, u32[]{:S(2)}) %collective-permute-start.4) | collective-permute-done | bytes 65568 | tf_op jit(solution)/shard_map/ppermute | solution.py:365
  22.4 0.9 %collective-permute-done.3.near = bf16[320,256]{1,0:T(8,128)(2,1)S(1)} collective-permute-done((bf16[320,256]{1,0:T(8,128)(2,1)S(1)}, bf16[320,256]{1,0:T(8,128)(2,1)S(1)}, u32[]{:S(2)}, u32[]{:S(2)}) %collective-permute-start.3) | collective-permute-done | bytes 163872 | tf_op jit(solution)/shard_map/ppermute | solution.py:365
  23.4 3.1 %collective-permute-start.6 = (bf16[480,256]{1,0:T(8,128)(2,1)S(1)}, bf16[480,256]{1,0:T(8,128)(2,1)S(1)}, u32[]{:S(2)}, u32[]{:S(2)}) collective-permute-start(bf16[480,256]{1,0:T(8,128)(2,1)S(1)} %inward.1), channel_id=1, source_target_pairs={{0,4},{1,5},{2,6},{3,7},{4,0},{5,1},{6,2},{7,3},{8,12},{9,13},{10,... | collective-permute-start | bytes 737288 | tf_op jit(solution)/shard_map/ppermute | solution.py:365
  26.5 1.1 %collective-permute-done.6.mate = bf16[480,256]{1,0:T(8,128)(2,1)S(1)} collective-permute-done((bf16[480,256]{1,0:T(8,128)(2,1)S(1)}, bf16[480,256]{1,0:T(8,128)(2,1)S(1)}, u32[]{:S(2)}, u32[]{:S(2)}) %collective-permute-start.6) | collective-permute-done | bytes 245792 | tf_op jit(solution)/shard_map/ppermute | solution.py:365
  27.6 4.9 %decode.1 = bf16[32,4,16,256]{3,2,1,0:T(8,128)(2,1)} custom-call(f32[120,512]{1,0:T(8,128)S(1)} %get-tuple-element.32.win, bf16[320,256]{1,0:T(8,128)(2,1)S(1)} %collective-permute-done.3.near, bf16[64,512]{1,0:T(8,128)(2,1)S(1)} %collective-permute-done.4.far, bf16[480,256]{1,0:T(8,128)(2,1)S(1)} %collective-permute-done.6.mate, ...), custom_call_target="tpu_custom_call" | custom-call | flops 5000000000 | bytes 15000000 | tf_op jit(solution)/shard_map/decode/pallas_call | solution.py:461
  (3 shorter events, 0.1 us)
Async XLA Ops:
  0.0 4.4 %copy-start = (bf16[32,4,16,256]{3,2,1,0:T(8,128)(2,1)S(1)}, bf16[32,4,16,256]{3,2,1,0:T(8,128)(2,1)}, u32[]{:S(2)}) copy-start(bf16[32,4,16,256]{3,2,1,0:T(8,128)(2,1)} %state.3) | copy-start | bytes 3145732
  0.0 4.8 %copy-start.5 = (bf16[64,4,768]{2,1,0:T(4,128)(2,1)S(1)}, bf16[64,4,768]{2,1,0:T(4,128)(2,1)}, u32[]{:S(2)}) copy-start(bf16[64,4,768]{2,1,0:T(4,128)(2,1)} %param.10) | copy-start | bytes 1179652
  0.0 4.9 %copy-start.1 = (bf16[4,768,512]{2,1,0:T(8,128)(2,1)S(1)}, bf16[4,768,512]{2,1,0:T(8,128)(2,1)}, u32[]{:S(2)}) copy-start(bf16[4,768,512]{2,1,0:T(8,128)(2,1)} %proj.1) | copy-start | bytes 9437188
  2.8 5.0 %collective-permute-start = (bf16[272,256]{1,0:T(8,128)(2,1)}, bf16[272,256]{1,0:T(8,128)(2,1)S(1)}, u32[]{:S(2)}, u32[]{:S(2)}) collective-permute-start(bf16[272,256]{1,0:T(8,128)(2,1)} %get-tuple-element.27), channel_id=1, source_target_pairs={{0,1},{1,2},{2,3},{3,0},{4,5},{5,6},{6,7},{7,4},{8,9},{9,10},{10,1... | collective-permute-start | bytes 417800 | tf_op jit(solution)/shard_map/ppermute | solution.py:354
  3.1 5.6 %collective-permute-start.1 = (bf16[272,256]{1,0:T(8,128)(2,1)}, bf16[272,256]{1,0:T(8,128)(2,1)S(1)}, u32[]{:S(2)}, u32[]{:S(2)}) collective-permute-start(bf16[272,256]{1,0:T(8,128)(2,1)} %get-tuple-element.28), channel_id=1, source_target_pairs={{0,3},{1,0},{2,1},{3,2},{4,7},{5,4},{6,5},{7,6},{8,11},{9,8},{10,9... | collective-permute-start | bytes 417800 | tf_op jit(solution)/shard_map/ppermute | solution.py:354
  4.9 1.7 %copy-start.3 = (bf16[2,2,2,64,33]{3,2,4,1,0:T(2,128)(2,1)S(1)}, bf16[2,2,2,64,33]{3,2,4,1,0:T(2,128)(2,1)}, u32[]{:S(2)}) copy-start(bf16[2,2,2,64,33]{3,2,4,1,0:T(2,128)(2,1)} %param.16) | copy-start | bytes 101380
  6.6 2.2 %copy-start.4 = (s32[8,256]{1,0:T(8,128)S(1)}, s32[8,256]{1,0:T(8,128)}, u32[]{:S(2)}) copy-start(s32[8,256]{1,0:T(8,128)} %get-tuple-element.26.own) | copy-start | bytes 24580
  8.7 9.6 %copy-start.2 = (bf16[4,4,4,32,64]{4,3,2,1,0:T(8,128)(2,1)S(1)}, bf16[4,4,4,32,64]{4,3,2,1,0:T(8,128)(2,1)}, u32[]{:S(2)}) copy-start(bf16[4,4,4,32,64]{4,3,2,1,0:T(8,128)(2,1)} %dec.1) | copy-start | bytes 786436
  10.3 8.1 %collective-permute-start.5 = (bf16[256,256]{1,0:T(8,128)(2,1)S(1)}, bf16[256,256]{1,0:T(8,128)(2,1)S(1)}, u32[]{:S(2)}, u32[]{:S(2)}) collective-permute-start(bf16[256,256]{1,0:T(8,128)(2,1)S(1)} %get-tuple-element.41), channel_id=1, source_target_pairs={{0,1},{1,0},{2,3},{3,2},{4,8},{5,9},{6,10},{7,11},{8,4},{9,5},{10,... | collective-permute-start | bytes 393224 | tf_op jit(solution)/shard_map/ppermute | solution.py:365
  13.8 3.7 %collective-permute-start.2 = (bf16[112,512]{1,0:T(8,128)(2,1)S(1)}, bf16[112,512]{1,0:T(8,128)(2,1)S(1)}, u32[]{:S(2)}, u32[]{:S(2)}) collective-permute-start(bf16[112,512]{1,0:T(8,128)(2,1)S(1)} %get-tuple-element.35), channel_id=1, source_target_pairs={{0,4},{1,5},{2,6},{3,7},{4,0},{5,1},{6,2},{7,3},{8,12},{9,13},{10,... | collective-permute-start | bytes 344072 | tf_op jit(solution)/shard_map/ppermute | solution.py:365
  17.5 5.8 %collective-permute-start.3 = (bf16[320,256]{1,0:T(8,128)(2,1)S(1)}, bf16[320,256]{1,0:T(8,128)(2,1)S(1)}, u32[]{:S(2)}, u32[]{:S(2)}) collective-permute-start(bf16[320,256]{1,0:T(8,128)(2,1)S(1)} %get-tuple-element.38), channel_id=1, source_target_pairs={{0,1},{1,0},{2,3},{3,2},{4,8},{5,9},{6,10},{7,11},{8,4},{9,5},{10,... | collective-permute-start | bytes 491528 | tf_op jit(solution)/shard_map/ppermute | solution.py:365
  17.6 4.8 %collective-permute-start.4 = (bf16[64,512]{1,0:T(8,128)(2,1)S(1)}, bf16[64,512]{1,0:T(8,128)(2,1)S(1)}, u32[]{:S(2)}, u32[]{:S(2)}) collective-permute-start(bf16[64,512]{1,0:T(8,128)(2,1)S(1)} %get-tuple-element.39), channel_id=1, source_target_pairs={{0,8},{1,9},{2,10},{3,11},{4,16},{5,17},{6,18},{7,19},{8,0},{9,1},... | collective-permute-start | bytes 196616 | tf_op jit(solution)/shard_map/ppermute | solution.py:365
  23.4 4.3 %collective-permute-start.6 = (bf16[480,256]{1,0:T(8,128)(2,1)S(1)}, bf16[480,256]{1,0:T(8,128)(2,1)S(1)}, u32[]{:S(2)}, u32[]{:S(2)}) collective-permute-start(bf16[480,256]{1,0:T(8,128)(2,1)S(1)} %inward.1), channel_id=1, source_target_pairs={{0,4},{1,5},{2,6},{3,7},{4,0},{5,1},{6,2},{7,3},{8,12},{9,13},{10,... | collective-permute-start | bytes 737288 | tf_op jit(solution)/shard_map/ppermute | solution.py:365
